TPU v7x, 32 devices: a whole 2x2x4 slice. The times are simulated.
32 devices in a mesh: dp: 8 (over z, x), fsdp: 4 (over y, core).
Axes of the slice: x: 2, y: 2, z: 4, core: 2. Of those that a mesh axis runs over, the one named last changes fastest.
Arguments:
- hidden_in: bfloat16 [2, 8, 256, 2048], P(None, 'dp', 'fsdp'), may hold values from -6 to 6
- seq_lengths: int32 [2, 8], P(None, 'dp'), may hold values from 64 to 256, as said below
- out_grad: bfloat16 [2, 8, 256, 2048], P(None, 'dp', 'fsdp'), may hold values from -6 to 6
- attn_gain: bfloat16 [2048], P(('dp', 'fsdp')), may hold values from 0.5 to 1.5
- w_query: bfloat16 [2048, 2048], P(('dp', 'fsdp')), may hold values from -0.125 to 0.125
- key_matrix: bfloat16 [2048, 1024], P(('dp', 'fsdp')), may hold values from -0.125 to 0.125
- value_matrix: bfloat16 [2048, 1024], P(('dp', 'fsdp')), may hold values from -0.125 to 0.125
- w_out: bfloat16 [2048, 2048], P(('dp', 'fsdp')), may hold values from -0.5 to 0.5
- mlp_gain: bfloat16 [2048], P(('dp', 'fsdp')), may hold values from 0.5 to 1.5
- w_gate: bfloat16 [2048, 8192], P(('dp', 'fsdp')), may hold values from -0.125 to 0.125
- w_up: bfloat16 [2048, 8192], P(('dp', 'fsdp')), may hold values from -0.125 to 0.125
- w_down: bfloat16 [2048, 8192], P(('dp', 'fsdp')), may hold values from -0.09375 to 0.09375
Outputs:
- hidden_out: bfloat16 [2, 8, 256, 2048], P(None, 'dp', 'fsdp')
- in_grad: bfloat16 [2, 8, 256, 2048], P(None, 'dp', 'fsdp')
- grad_attn_gain: float32 [2048], P(('dp', 'fsdp'))
- grad_query: float32 [2048, 2048], P(('dp', 'fsdp'))
- grad_key: float32 [2048, 1024], P(('dp', 'fsdp'))
- grad_value: float32 [2048, 1024], P(('dp', 'fsdp'))
- grad_out: float32 [2048, 2048], P(('dp', 'fsdp'))
- grad_mlp_gain: float32 [2048], P(('dp', 'fsdp'))
- grad_gate: float32 [2048, 8192], P(('dp', 'fsdp'))
- grad_up: float32 [2048, 8192], P(('dp', 'fsdp'))
- grad_down: float32 [2048, 8192], P(('dp', 'fsdp'))
Inputs may be any that keep to these rules, and one draw needn't show every extreme that they name: Slots at or past seq_lengths are padding; in every draw some sequence has all 256 slots live and some has 64.
All inputs are finite; a program needn't handle non-finite values.
Results may differ from a plain program's by a relative error of at most 0.015.
Values may be sent and summed in bfloat16 or wider, within the bound.
No kernel may reach another device: no remote copies, remote signals or barrier semaphores. Data moves between devices by JAX's collectives and lax.ppermute only.
A program may use at most 896 MiB of HBM per device.

v0:
```python
import jax
import jax.numpy as jnp
from jax import lax
from jax.sharding import PartitionSpec as P

QUERY_HEADS = 8
KEY_VALUE_HEADS = 4
HEAD_DIMENSION = 256
FF = 8192


EPS_NORM = 1e-06
ROPE_BASE = 1000042.0
NEG_FILL = -1e30


def rope_tables(positions, head_size):
    half_size = head_size // 2
    inverse = ROPE_BASE ** (-(jnp.arange(half_size, dtype=jnp.float32) * 2.0 / head_size))
    angles = positions.astype(jnp.float32)[:, None] * inverse[None, :]
    angles = jnp.concatenate([angles, angles], axis=-1)
    return (jnp.cos(angles), jnp.sin(angles))


def rotate_half(value_rows):
    half_size = value_rows.shape[-1] // 2
    return jnp.concatenate([-value_rows[..., half_size:], value_rows[..., :half_size]], axis=-1)


def unrotate_half(value_rows):
    half_size = value_rows.shape[-1] // 2
    return jnp.concatenate([value_rows[..., half_size:], -value_rows[..., :half_size]], axis=-1)


def rotary_embed(value_rows, cosine_table, sine_table):
    return value_rows * cosine_table + rotate_half(value_rows) * sine_table


def rotary_backward(grads, cosine_table, sine_table):
    return grads * cosine_table + unrotate_half(grads * sine_table)


def norm_backward(normalized_input, reciprocal_scale, normalized_gradient):
    return reciprocal_scale * (
        normalized_gradient
        - normalized_input
        * jnp.mean(normalized_gradient * normalized_input, axis=-1, keepdims=True)
    )


def right_product(left, piece):
    return lax.dot_general(
        left, piece, (((1,), (1,)), ((), ())), preferred_element_type=jnp.float32
    )


def rows_product(left, right):
    return lax.dot_general(
        left, right, (((0,), (0,)), ((), ())), preferred_element_type=jnp.float32
    )


def per_device(
    hidden_in,
    seq_lengths,
    out_grad,
    attn_gain,
    w_query,
    key_matrix,
    value_matrix,
    w_out,
    mlp_gain,
    w_gate,
    w_up,
    w_down,
):
    token_count = hidden_in.shape[0]
    row_block = hidden_in.shape[2]
    width = hidden_in.shape[3]
    row_total_count = token_count * row_block
    lengths = seq_lengths.reshape(token_count)
    sequence_length = row_block * lax.axis_size("fsdp")
    positions = lax.axis_index("fsdp") * row_block + jnp.arange(row_block, dtype=jnp.int32)
    key_slots = jnp.arange(sequence_length, dtype=jnp.int32)
    cosine_table, sine_table = rope_tables(positions, HEAD_DIMENSION)
    cosine_table = cosine_table[:, None, :]
    sine_table = sine_table[:, None, :]
    local_portion = QUERY_HEADS // KEY_VALUE_HEADS
    scale = HEAD_DIMENSION ** (-0.5)
    input_rows = hidden_in.astype(jnp.float32).reshape(row_total_count, width)
    valid = positions[None, :] < lengths[:, None]
    mask_rows = valid.astype(jnp.float32).reshape(row_total_count, 1)
    allowed = (key_slots[None, None, :] <= positions[None, :, None]) & (
        key_slots[None, None, :] < lengths[:, None, None]
    )
    allowed = allowed[:, None, None, :, :]
    first_scale = lax.rsqrt(jnp.mean(input_rows * input_rows, axis=-1, keepdims=True) + EPS_NORM)
    first_unscaled = input_rows * first_scale
    attn_set = (
        lax.all_gather(attn_gain, ("dp", "fsdp"), axis=0, tiled=True),
        lax.all_gather(w_query, ("dp", "fsdp"), axis=0, tiled=True),
        lax.all_gather(key_matrix, ("dp", "fsdp"), axis=0, tiled=True),
        lax.all_gather(value_matrix, ("dp", "fsdp"), axis=0, tiled=True),
        lax.all_gather(w_out, ("dp", "fsdp"), axis=0, tiled=True),
    )
    first_norm_weight = attn_set[0].astype(jnp.float32)
    first_normalized = (first_unscaled * first_norm_weight).astype(jnp.bfloat16)
    query_acc = jnp.dot(first_normalized, attn_set[1], preferred_element_type=jnp.float32)
    key_accumulator = jnp.dot(first_normalized, attn_set[2], preferred_element_type=jnp.float32)
    value_accumulator = jnp.dot(first_normalized, attn_set[3], preferred_element_type=jnp.float32)
    query_rows = rotary_embed(
        query_acc.reshape(token_count, row_block, QUERY_HEADS, HEAD_DIMENSION),
        cosine_table,
        sine_table,
    ).astype(jnp.bfloat16)
    query_rows = query_rows.reshape(
        token_count, row_block, KEY_VALUE_HEADS, local_portion, HEAD_DIMENSION
    )
    local_keys = rotary_embed(
        key_accumulator.reshape(token_count, row_block, KEY_VALUE_HEADS, HEAD_DIMENSION),
        cosine_table,
        sine_table,
    ).astype(jnp.bfloat16)
    local_values = value_accumulator.reshape(
        token_count, row_block, KEY_VALUE_HEADS, HEAD_DIMENSION
    ).astype(jnp.bfloat16)
    keys_all, values_all = (
        lax.all_gather(local_keys, "fsdp", axis=1, tiled=True),
        lax.all_gather(local_values, "fsdp", axis=1, tiled=True),
    )

    def scores_of():
        raw_scores = (
            jnp.einsum(
                "mqkgd,mskd->mkgqs", query_rows, keys_all, preferred_element_type=jnp.float32
            )
            * scale
        )
        return jnp.where(allowed, raw_scores, NEG_FILL)

    scores = scores_of()
    top_score = jnp.max(scores, axis=-1, keepdims=True)
    log_total = top_score + jnp.log(jnp.sum(jnp.exp(scores - top_score), axis=-1, keepdims=True))
    probs = jnp.where(allowed, jnp.exp(scores - log_total), 0.0)
    mixed = jnp.einsum(
        "mkgqs,mskd->mqkgd",
        probs.astype(jnp.bfloat16),
        values_all,
        preferred_element_type=jnp.float32,
    )
    mixed = mixed.reshape(row_total_count, QUERY_HEADS * HEAD_DIMENSION).astype(jnp.bfloat16)
    branch = right_product(mixed, attn_set[4])
    residual_middle = input_rows + branch
    second_scale = lax.rsqrt(
        jnp.mean(residual_middle * residual_middle, axis=-1, keepdims=True) + EPS_NORM
    )
    second_unscaled = residual_middle * second_scale
    feedforward_params = (
        lax.all_gather(mlp_gain, ("dp", "fsdp"), axis=0, tiled=True),
        lax.all_gather(w_gate, ("dp", "fsdp"), axis=0, tiled=True),
        lax.all_gather(w_up, ("dp", "fsdp"), axis=0, tiled=True),
        lax.all_gather(w_down, ("dp", "fsdp"), axis=0, tiled=True),
    )
    second_normalized = (second_unscaled * feedforward_params[0].astype(jnp.float32)).astype(
        jnp.bfloat16
    )
    gate = jnp.dot(second_normalized, feedforward_params[1], preferred_element_type=jnp.float32)
    up_proj = jnp.dot(second_normalized, feedforward_params[2], preferred_element_type=jnp.float32)
    sigmoid_gate = jax.nn.sigmoid(gate)
    activated = gate * sigmoid_gate
    hidden = (activated * up_proj).astype(jnp.bfloat16)
    feed = right_product(hidden, feedforward_params[3])
    outputs = (
        (mask_rows * (residual_middle + feed))
        .astype(jnp.bfloat16)
        .reshape(token_count, 1, row_block, width)
    )
    output_gradient = out_grad.astype(jnp.float32).reshape(row_total_count, width) * mask_rows
    feed_grad = output_gradient.astype(jnp.bfloat16)
    back_set = (
        lax.all_gather(mlp_gain, ("dp", "fsdp"), axis=0, tiled=True),
        lax.all_gather(w_gate, ("dp", "fsdp"), axis=0, tiled=True),
        lax.all_gather(w_up, ("dp", "fsdp"), axis=0, tiled=True),
        lax.all_gather(w_down, ("dp", "fsdp"), axis=0, tiled=True),
    )
    second_norm_weight = back_set[0].astype(jnp.float32)
    hidden_grad = jnp.dot(feed_grad, back_set[3], preferred_element_type=jnp.float32)
    gate_grad = (hidden_grad * up_proj * sigmoid_gate * (1.0 + gate * (1.0 - sigmoid_gate))).astype(
        jnp.bfloat16
    )
    up_grad = (hidden_grad * activated).astype(jnp.bfloat16)
    second_normalized_gradient = right_product(gate_grad, back_set[1]) + right_product(
        up_grad, back_set[2]
    )
    second_norm_weight_gradient = jnp.sum(second_unscaled * second_normalized_gradient, axis=0)
    second_unscaled_gradient = second_normalized_gradient * second_norm_weight
    mlp_pair = jnp.concatenate([gate_grad, up_grad], axis=1)
    normed_cols = second_normalized
    grad_cols = feed_grad
    mlp_total = lax.psum_scatter(
        jnp.concatenate(
            [rows_product(normed_cols, mlp_pair), rows_product(grad_cols, hidden)], axis=1
        ),
        ("dp", "fsdp"),
        scatter_dimension=0,
        tiled=True,
    )
    residual_middle_gradient = output_gradient + norm_backward(
        second_unscaled, second_scale, second_unscaled_gradient
    )
    branch_grad = residual_middle_gradient.astype(jnp.bfloat16)
    attention_recomputed = (
        lax.all_gather(attn_gain, ("dp", "fsdp"), axis=0, tiled=True),
        lax.all_gather(w_query, ("dp", "fsdp"), axis=0, tiled=True),
        lax.all_gather(key_matrix, ("dp", "fsdp"), axis=0, tiled=True),
        lax.all_gather(value_matrix, ("dp", "fsdp"), axis=0, tiled=True),
        lax.all_gather(w_out, ("dp", "fsdp"), axis=0, tiled=True),
    )
    combined_gradient = jnp.dot(
        branch_grad, attention_recomputed[4], preferred_element_type=jnp.float32
    )
    combined_gradient = combined_gradient.astype(jnp.bfloat16).reshape(
        token_count, row_block, KEY_VALUE_HEADS, local_portion, HEAD_DIMENSION
    )
    scores = scores_of()
    probs = jnp.where(allowed, jnp.exp(scores - log_total), 0.0)
    prob_grad = jnp.einsum(
        "mqkgd,mskd->mkgqs", combined_gradient, values_all, preferred_element_type=jnp.float32
    )
    score_grad = (probs * (prob_grad - jnp.sum(probs * prob_grad, axis=-1, keepdims=True))).astype(
        jnp.bfloat16
    )
    query_grad = (
        jnp.einsum("mkgqs,mskd->mqkgd", score_grad, keys_all, preferred_element_type=jnp.float32)
        * scale
    )
    key_part = (
        jnp.einsum("mkgqs,mqkgd->mskd", score_grad, query_rows, preferred_element_type=jnp.float32)
        * scale
    )
    value_part = jnp.einsum(
        "mkgqs,mqkgd->mskd",
        probs.astype(jnp.bfloat16),
        combined_gradient,
        preferred_element_type=jnp.float32,
    )
    key_total, value_total = (
        lax.psum_scatter(key_part, "fsdp", scatter_dimension=1, tiled=True),
        lax.psum_scatter(value_part, "fsdp", scatter_dimension=1, tiled=True),
    )
    query_low = (
        rotary_backward(
            query_grad.reshape(token_count, row_block, QUERY_HEADS, HEAD_DIMENSION),
            cosine_table,
            sine_table,
        )
        .astype(jnp.bfloat16)
        .reshape(row_total_count, QUERY_HEADS * HEAD_DIMENSION)
    )
    key_begin = (
        rotary_backward(key_total, cosine_table, sine_table)
        .astype(jnp.bfloat16)
        .reshape(row_total_count, KEY_VALUE_HEADS * HEAD_DIMENSION)
    )
    value_begin = value_total.astype(jnp.bfloat16).reshape(
        row_total_count, KEY_VALUE_HEADS * HEAD_DIMENSION
    )
    qkv_grad = jnp.concatenate([query_low, key_begin, value_begin], axis=1)
    normed_cols = first_normalized
    grad_cols = branch_grad
    attn_total = lax.psum_scatter(
        jnp.concatenate(
            [rows_product(normed_cols, qkv_grad), rows_product(grad_cols, mixed)], axis=1
        ),
        ("dp", "fsdp"),
        scatter_dimension=0,
        tiled=True,
    )
    first_normalized_gradient = (
        right_product(query_low, attention_recomputed[1])
        + right_product(key_begin, attention_recomputed[2])
        + right_product(value_begin, attention_recomputed[3])
    )
    first_norm_weight_gradient = jnp.sum(first_unscaled * first_normalized_gradient, axis=0)
    first_unscaled_gradient = first_normalized_gradient * attention_recomputed[0].astype(
        jnp.float32
    )
    input_grads = (
        (
            residual_middle_gradient
            + norm_backward(first_unscaled, first_scale, first_unscaled_gradient)
        )
        .astype(jnp.bfloat16)
        .reshape(token_count, 1, row_block, width)
    )
    gain_one_share, gain_two_share = (
        lax.psum_scatter(
            first_norm_weight_gradient, ("dp", "fsdp"), scatter_dimension=0, tiled=True
        ),
        lax.psum_scatter(
            second_norm_weight_gradient, ("dp", "fsdp"), scatter_dimension=0, tiled=True
        ),
    )
    query_stop = QUERY_HEADS * HEAD_DIMENSION
    key_stop = query_stop + KEY_VALUE_HEADS * HEAD_DIMENSION
    value_stop = key_stop + KEY_VALUE_HEADS * HEAD_DIMENSION
    return (
        outputs,
        input_grads,
        gain_one_share,
        attn_total[:, :query_stop],
        attn_total[:, query_stop:key_stop],
        attn_total[:, key_stop:value_stop],
        attn_total[:, value_stop:],
        gain_two_share,
        mlp_total[:, :FF],
        mlp_total[:, FF : 2 * FF],
        mlp_total[:, 2 * FF :],
    )


def solution(mesh):
    placed = (
        P(None, "dp", "fsdp", None),
        P(None, "dp"),
        P(None, "dp", "fsdp", None),
        P(("dp", "fsdp")),
        P(("dp", "fsdp"), None),
        P(("dp", "fsdp"), None),
        P(("dp", "fsdp"), None),
        P(("dp", "fsdp"), None),
        P(("dp", "fsdp")),
        P(("dp", "fsdp"), None),
        P(("dp", "fsdp"), None),
        P(("dp", "fsdp"), None),
    )
    return jax.shard_map(
        per_device,
        mesh=mesh,
        in_specs=placed,
        out_specs=(
            P(None, "dp", "fsdp", None),
            P(None, "dp", "fsdp", None),
            P(("dp", "fsdp")),
            P(("dp", "fsdp"), None),
            P(("dp", "fsdp"), None),
            P(("dp", "fsdp"), None),
            P(("dp", "fsdp"), None),
            P(("dp", "fsdp")),
            P(("dp", "fsdp"), None),
            P(("dp", "fsdp"), None),
            P(("dp", "fsdp"), None),
        ),
        check_vma=False,
    )
```

profile of v0, /device:TPU:0, one launch (start us, length us, event | category | flops | bytes accessed | tf_op | source)
XLA Modules:
  0.0 3161.0 jit_solution(14321150900577090442)
XLA Ops:
  11.2 42.2 %all-reduce.6 = (bf16[2048]{0:T(1024)(128)(2,1)S(1)}, bf16[2048]{0:T(1024)(128)(2,1)S(1)}) all-reduce(bf16[2048]{0:T(1024)(128)(2,1)S(1)} %dynamic-update-slice, bf16[2048]{0:T(1024)(128)(2,1)S(1)} %dynamic-update-slice.1), channel_id=1, replica_groups=mesh['dp'=8,'fsdp'=4] {'dp','fsdp'}, use_global_device_ids=true, to_apply=%add | all-reduce | flops 4096 | bytes 16384
  54.9 20.8 all-gather.14.cloned.1.call-done
  86.9 52.3 %all-gather.10.cloned.1.call-done = bf16[2048,1024]{1,0:T(8,128)(2,1)} async-done(((bf16[64,1024]{1,0:T(8,128)(2,1)}), bf16[2048,1024]{1,0:T(8,128)(2,1)}) %all-gather.10.cloned.1.call-update) | async-done | bytes 4194320 | tf_op jit(solution)/shard_map/all_gather | solution.py:103
  157.1 61.2 %all-gather.18.cloned.1.call-done = bf16[2048,2048]{1,0:T(8,128)(2,1)} async-done(((bf16[64,2048]{1,0:T(8,128)(2,1)}), bf16[2048,2048]{1,0:T(8,128)(2,1)}) %all-gather.18.cloned.1.call-update) | async-done | bytes 8388624 | tf_op jit(solution)/shard_map/all_gather | solution.py:101
  239.9 14.4 all-gather.12.cloned.1.call-done
  256.9 77.7 %all-gather.20.cloned.1.call-done = bf16[2048,2048]{1,0:T(8,128)(2,1)} async-done(((bf16[64,2048]{1,0:T(8,128)(2,1)}), bf16[2048,2048]{1,0:T(8,128)(2,1)}) %all-gather.20.cloned.1.call-update) | async-done | bytes 8388624 | tf_op jit(solution)/shard_map/all_gather | solution.py:104
  341.2 189.7 %all-gather.24.cloned.1.call-done = bf16[2048,8192]{1,0:T(8,128)(2,1)} async-done(((bf16[64,8192]{1,0:T(8,128)(2,1)}), bf16[2048,8192]{1,0:T(8,128)(2,1)}) %all-gather.24.cloned.1.call-update) | async-done | bytes 33554448 | tf_op jit(solution)/shard_map/all_gather | solution.py:161
  530.9 17.8 fusion.56
  548.7 178.1 %all-gather.22.cloned.1.call-done = bf16[2048,8192]{1,0:T(8,128)(2,1)} async-done(((bf16[64,8192]{1,0:T(8,128)(2,1)}), bf16[2048,8192]{1,0:T(8,128)(2,1)}) %all-gather.22.cloned.1.call-update) | async-done | bytes 33554448 | tf_op jit(solution)/shard_map/all_gather | solution.py:160
  726.7 18.2 fusion.55
  745.0 177.7 %all-gather.26.cloned.1.call-done = bf16[2048,8192]{1,0:T(8,128)(2,1)} async-done(((bf16[64,8192]{1,0:T(8,128)(2,1)}), bf16[2048,8192]{1,0:T(8,128)(2,1)}) %all-gather.26.cloned.1.call-update) | async-done | bytes 33554448 | tf_op jit(solution)/shard_map/all_gather | solution.py:162
  922.6 19.4 multiply_convert_fusion
  942.0 17.3 fusion.57
  959.3 17.6 multiply_reduce_fusion
  992.4 51.7 %all-reduce.8 = bf16[2,256,4,256]{3,2,0,1:T(4,128)(2,1)S(1)} all-reduce(f32[2,256,4,256]{3,2,0,1:T(4,128)} %copy.58), channel_id=3, replica_groups=mesh['dp'=8,'fsdp'=4] {'fsdp'}, use_global_device_ids=true, to_apply=%region_7.8.clone | all-reduce | flops 524288 | bytes 3145728
  1072.7 13.4 fusion.13
  1086.1 33.7 %pad_maximum_fusion.1 = f32[2048,6144]{1,0:T(8,128)} fusion(f32[2048,2048]{1,0:T(8,128)} %fusion.37, f32[2048,4096]{1,0:T(8,128)} %fusion.13), kind=kLoop, calls=%fused_computation.1 | loop fusion | flops 12582912 | bytes 100663296 | tf_op jit(solution)/shard_map/concatenate | solution.py:272
  1120.8 40.7 %fusion.59 = f32[2048,8192]{1,0:T(8,128)} fusion(bf16[128,2048]{1,0:T(8,128)(2,1)S(1)} %copy-done.16, bf16[128,8192]{1,0:T(8,128)(2,1)} %get-tuple-element.54), kind=kOutput, calls=%fused_computation.114 | convolution fusion | flops 4294967296 | bytes 69730304 | tf_op jit(solution)/shard_map/dot_general | solution.py:58
  1161.5 56.9 %fusion = f32[2048,16384]{1,0:T(8,128)} fusion(bf16[128,2048]{1,0:T(8,128)(2,1)S(1)} %multiply_convert_fusion.5, bf16[128,8192]{1,0:T(8,128)(2,1)S(1)} %copy-done.9, bf16[128,8192]{1,0:T(8,128)(2,1)} %get-tuple-element.53), kind=kOutput, calls=%fused_computation.2 | convolution fusion | flops 8598323200 | bytes 138936320 | tf_op jit(solution)/shard_map/dot_general | solution.py:58
  1218.3 134.5 %pad_maximum_fusion = f32[2048,24576]{1,0:T(8,128)} fusion(f32[2048,8192]{1,0:T(8,128)} %fusion.59, f32[2048,16384]{1,0:T(8,128)} %fusion), kind=kLoop, calls=%fused_computation | loop fusion | flops 50331648 | bytes 402653184 | tf_op jit(solution)/shard_map/concatenate | solution.py:201
  1354.1 17.9 fusion.6
  1372.0 38.9 %all-reduce.5 = (f32[2048]{0:T(1024)S(1)}, f32[2048]{0:T(1024)S(1)}) all-reduce(f32[2048]{0:T(1024)S(1)} %copy-done.22, f32[2048]{0:T(1024)S(1)} %copy-done.21), channel_id=4, replica_groups=mesh['dp'=8,'fsdp'=4] {'dp','fsdp'}, use_global_device_ids=true, to_apply=%region_10.11.clone | all-reduce | flops 4096 | bytes 32768
  1414.4 135.3 %reduce-scatter.6.cloned.1.call-done = f32[64,6144]{1,0:T(8,128)} async-done(((f32[2048,6144]{1,0:T(8,128)}), f32[64,6144]{1,0:T(8,128)}) %reduce-scatter.6.cloned.1.call-update) | async-done | bytes 1572880 | tf_op jit(solution)/shard_map/reduce_scatter | solution.py:271
  1553.9 1594.3 %reduce-scatter.8.cloned.1.call-done = f32[64,24576]{1,0:T(8,128)} async-done(((f32[2048,24576]{1,0:T(8,128)}), f32[64,24576]{1,0:T(8,128)}) %reduce-scatter.8.cloned.1.call-update) | async-done | bytes 6291472 | tf_op jit(solution)/shard_map/reduce_scatter | solution.py:200
  (164 shorter events, 123.8 us)
Async XLA Ops:
  7.2 68.5 %all-gather.14.cloned.1.call-start = ((), (), s32[]{:S(2)}) async-start(), calls=%async_computation.5 | async-start | bytes 4325376 | tf_op jit(solution)/shard_map/all_gather | solution.py:102
  7.9 131.3 %all-gather.10.cloned.1.call-start = ((), (), s32[]{:S(2)}) async-start(), calls=%async_computation.3 | async-start | bytes 4325376 | tf_op jit(solution)/shard_map/all_gather | solution.py:103
  8.7 209.6 %all-gather.18.cloned.1.call-start = ((), (), s32[]{:S(2)}) async-start(), calls=%async_computation.7 | async-start | bytes 8650752 | tf_op jit(solution)/shard_map/all_gather | solution.py:101
  9.4 228.1 %all-gather.16.cloned.1.call-start = ((), (), s32[]{:S(2)}) async-start(), calls=%async_computation.6 | async-start | bytes 1310720 | tf_op jit(solution)/shard_map/all_gather | solution.py:128
  53.3 1016.1 %copy-start.19 = (f32[2048]{0:T(1024)}, f32[2048]{0:T(1024)S(1)}, u32[]{:S(2)}) copy-start(f32[2048]{0:T(1024)S(1)} %convert_element_type.107) | copy-start | bytes 24580
  86.9 167.4 %all-gather.12.cloned.1.call-start = ((), (), s32[]{:S(2)}) async-start(), calls=%async_computation.4 | async-start | bytes 1310720 | tf_op jit(solution)/shard_map/all_gather | solution.py:129
  150.2 184.4 %all-gather.20.cloned.1.call-start = ((), (), s32[]{:S(2)}) async-start(), calls=%async_computation.8 | async-start | bytes 8650752 | tf_op jit(solution)/shard_map/all_gather | solution.py:104
  150.8 380.1 %all-gather.24.cloned.1.call-start = ((), (), s32[]{:S(2)}) async-start(), calls=%async_computation.10 | async-start | bytes 34603008 | tf_op jit(solution)/shard_map/all_gather | solution.py:161
  151.5 575.2 %all-gather.22.cloned.1.call-start = ((), (), s32[]{:S(2)}) async-start(), calls=%async_computation.9 | async-start | bytes 34603008 | tf_op jit(solution)/shard_map/all_gather | solution.py:160
  152.3 770.4 %all-gather.26.cloned.1.call-start = ((), (), s32[]{:S(2)}) async-start(), calls=%async_computation.11 | async-start | bytes 34603008 | tf_op jit(solution)/shard_map/all_gather | solution.py:162
  153.0 912.1 %reduce-scatter.4.cloned.1.call-start = ((), (), s32[]{:S(2)}) async-start(), calls=%async_computation.12 | async-start | bytes 2621440 | tf_op jit(solution)/shard_map/reduce_scatter | solution.py:248
  153.1 916.3 %copy-start.25 = (f32[128]{0:T(128)}, f32[128]{0:T(128)S(1)}, u32[]{:S(2)}) copy-start(f32[128]{0:T(128)S(1)} %rsqrt.22) | copy-start | bytes 1540
  153.3 823.6 %copy-start.23 = (f32[128]{0:T(128)}, f32[128]{0:T(128)S(1)}, u32[]{:S(2)}) copy-start(f32[128]{0:T(128)S(1)} %reshape.303) | copy-start | bytes 1540
  237.4 19.4 copy-start.10
  256.9 84.1 %copy-start.12 = (bf16[128,2048]{1,0:T(8,128)(2,1)}, bf16[128,2048]{1,0:T(8,128)(2,1)S(1)}, u32[]{:S(2)}) copy-start(bf16[128,2048]{1,0:T(8,128)(2,1)S(1)} %convert_element_type.117) | copy-start | bytes 1572868
  341.0 635.9 %copy-start = (f32[128,2048]{1,0:T(8,128)}, f32[128,2048]{1,0:T(8,128)S(1)}, u32[]{:S(2)}) copy-start(f32[128,2048]{1,0:T(8,128)S(1)} %get-tuple-element.76) | copy-start | bytes 3145732
  992.4 557.4 %reduce-scatter.6.cloned.1.call-start = ((), (), s32[]{:S(2)}) async-start(), calls=%async_computation.13 | async-start | bytes 51904512 | tf_op jit(solution)/shard_map/reduce_scatter | solution.py:271
  1119.8 2028.4 %reduce-scatter.8.cloned.1.call-start = ((), (), s32[]{:S(2)}) async-start(), calls=%async_computation.14 | async-start | bytes 207618048 | tf_op jit(solution)/shard_map/reduce_scatter | solution.py:200
  1120.8 40.7 %copy-start.9 = (bf16[128,8192]{1,0:T(8,128)(2,1)S(1)}, bf16[128,8192]{1,0:T(8,128)(2,1)}, u32[]{:S(2)}) copy-start(bf16[128,8192]{1,0:T(8,128)(2,1)} %get-tuple-element.52) | copy-start | bytes 6291460
  1354.0 58.0 %copy-start.27 = (f32[128]{0:T(128)S(1)}, f32[128]{0:T(128)}, u32[]{:S(2)}) copy-start(f32[128]{0:T(128)} %get-tuple-element.47) | copy-start | bytes 1540
  1354.0 58.0 %copy-start.3 = (bf16[2,1,64,2048]{3,2,1,0:T(8,128)(2,1)S(1)}, bf16[2,1,64,2048]{3,2,1,0:T(8,128)(2,1)}, u32[]{:S(2)}) copy-start(bf16[2,1,64,2048]{3,2,1,0:T(8,128)(2,1)} %param.12) | copy-start | bytes 1572868
  1354.1 58.0 %copy-start.6 = (f32[128,2048]{1,0:T(8,128)S(1)}, f32[128,2048]{1,0:T(8,128)}, u32[]{:S(2)}) copy-start(f32[128,2048]{1,0:T(8,128)} %copy-done.4) | copy-start | bytes 3145732
  1354.1 58.0 %copy-start.20 = (f32[2048]{0:T(1024)S(1)}, f32[2048]{0:T(1024)}, u32[]{:S(2)}) copy-start(f32[2048]{0:T(1024)} %copy-done.19) | copy-start | bytes 24580
  1354.1 58.0 %copy-start.26 = (f32[128]{0:T(128)S(1)}, f32[128]{0:T(128)}, u32[]{:S(2)}) copy-start(f32[128]{0:T(128)} %copy-done.25) | copy-start | bytes 1540
  (18 other events, 106.2 us)
Sparse Core Ops, SparseCore 0:
  10.9 64.7 all-gather.13
  78.6 60.5 all-gather.9
  142.1 76.0 all-gather.17
  220.2 15.3 all-gather.15
  237.5 16.7 all-gather.11
  257.0 77.5 all-gather.19
  337.5 193.3 all-gather.23
  533.8 192.9 all-gather.21
  729.6 192.9 all-gather.25
  992.5 37.2 reduce-scatter.3
  1119.9 429.8 reduce-scatter.5
  1557.2 1590.9 reduce-scatter.7
where the time goes:
time: 3170 us; the launch traced here: 3160 us
  waiting for transfers between devices  2510 us (79%)
  matrix products  275 us (9%)
  other arithmetic  179 us (6%)
  blocking collectives  133 us (4%)
  local copies, waits for them, and re-layouts  52.5 us (2%)
    reduce_scatter x1, waiting for transfers between devices, per_device(): lax.psum_scatter(jnp.concatenate([rows_product(normed_cols, mlp_pair), ro...  1590 us
    all_gather x1, waiting for transfers between devices, per_device(): lax.all_gather(w_up, ('dp', 'fsdp'), axis=0, tiled=True)  190 us
    all_gather x1, waiting for transfers between devices, per_device(): lax.all_gather(w_gate, ('dp', 'fsdp'), axis=0, tiled=True)  178 us
    all_gather x1, waiting for transfers between devices, per_device(): lax.all_gather(w_down, ('dp', 'fsdp'), axis=0, tiled=True)  178 us
    reduce_scatter x1, waiting for transfers between devices, per_device(): lax.psum_scatter(jnp.concatenate([rows_product(normed_cols, qkv_grad), ro...  135 us
    concatenate x1, other arithmetic, per_device(): jnp.concatenate([rows_product(normed_cols, mlp_pair), rows_product(grad_c...  134 us
    unnamed x3, blocking collectives  133 us
    dot_general x4, matrix products, rows_product(): lax.dot_general(left, right, (((0,), (0,)), ((), ())), preferred_element_...  119 us
  transfers between devices with their start and end apart: 12, of which 10 were waited for; matrix products, arithmetic and copies ran while one was open for 12% of the time, Pallas kernels for 0%

commit v1 on v0

v1 whole, which is shorter than its diff:
```python
import jax
import jax.numpy as jnp
from jax import lax
from jax.sharding import Mesh, PartitionSpec as P

QUERY_HEADS = 8
KEY_VALUE_HEADS = 4
HEAD_DIMENSION = 256

EPS_NORM = 1e-06
ROPE_BASE = 1000042.0
NEG_FILL = -1e30

BF = jnp.bfloat16
F32 = jnp.float32


def rope_tables(positions, head_size):
    half_size = head_size // 2
    inverse = ROPE_BASE ** (-(jnp.arange(half_size, dtype=F32) * 2.0 / head_size))
    angles = positions.astype(F32)[:, None] * inverse[None, :]
    return jnp.cos(angles), jnp.sin(angles)


def rotary_embed(rows, cosine, sine):
    half = rows.shape[-1] // 2
    first, second = rows[..., :half], rows[..., half:]
    return jnp.concatenate(
        [first * cosine - second * sine, second * cosine + first * sine], axis=-1
    )


def rotary_backward(grads, cosine, sine):
    half = grads.shape[-1] // 2
    first, second = grads[..., :half], grads[..., half:]
    return jnp.concatenate(
        [first * cosine + second * sine, second * cosine - first * sine], axis=-1
    )


def norm_backward(normalized, reciprocal, gradient):
    return reciprocal * (
        gradient - normalized * jnp.mean(gradient * normalized, axis=-1, keepdims=True)
    )


def dot(left, right):
    return jnp.dot(left, right, preferred_element_type=F32)


def dot_right(left, right):
    return lax.dot_general(left, right, (((1,), (1,)), ((), ())), preferred_element_type=F32)


def dot_rows(left, right):
    return lax.dot_general(left, right, (((0,), (0,)), ((), ())), preferred_element_type=F32)


def swap(value, axis):
    return lax.ppermute(value, axis, [(0, 1), (1, 0)])


def ring(value, size):
    return lax.ppermute(value, "z", [(i, (i + 1) % size) for i in range(size)])


def pick(value, index, axis=0):
    return lax.dynamic_index_in_dim(value, index, axis, keepdims=False)


def put(buffer, piece, *index):
    piece = piece.reshape((1,) * len(index) + piece.shape)
    starts = tuple(index) + (0,) * (buffer.ndim - len(index))
    return lax.dynamic_update_slice(buffer, piece, starts)


def gather_yc(block):
    across = swap(block, "y")
    return [block, swap(block, "c"), across, swap(across, "c")]


def scatter_yc(parts):
    near = [parts[0].astype(F32) + swap(parts[1], "c"), parts[2].astype(F32) + swap(parts[3], "c")]
    return near[0] + swap(near[1].astype(BF), "y")


def gather_z(block, size):
    blocks = [block]
    for _ in range(size - 1):
        blocks.append(ring(blocks[-1], size))
    return blocks


def gather_zy(block, size):
    return [[b, swap(b, "y")] for b in gather_z(block, size)]


def scatter_z(parts, partners, axis, size):
    dtype = partners[0].dtype
    total = None
    for step in range(size):
        s = (step + 1) % size
        own = parts[s].astype(F32) + swap(partners[s], axis)
        total = own if total is None else own + ring(total.astype(dtype), size)
    return total


def per_device(
    hidden_in,
    seq_lengths,
    out_grad,
    attn_gain,
    w_query,
    key_matrix,
    value_matrix,
    w_out,
    mlp_gain,
    w_gate,
    w_up,
    w_down,
):
    micro, _, slots, width = hidden_in.shape
    size = lax.axis_size("z")
    z, x, y, c = (lax.axis_index(a) for a in ("z", "x", "y", "c"))
    j = y * 2 + c
    own_rows = w_query.shape[0]
    block_rows = 4 * own_rows
    q_cols = w_query.shape[1] // 4
    kv_cols = key_matrix.shape[1] // 4
    qkv_cols = q_cols + 2 * kv_cols
    ff = w_gate.shape[1]
    chunk = ff // (2 * size)
    rows = micro * slots
    group_rows = 4 * rows
    q_heads = q_cols // HEAD_DIMENSION
    scale = HEAD_DIMENSION ** (-0.5)
    lengths = seq_lengths.reshape(micro)

    def by_head(weight):
        return jnp.swapaxes(weight.reshape(own_rows, 4, -1), 0, 1)

    qkv_local = jnp.concatenate(
        [by_head(w_query), by_head(key_matrix), by_head(value_matrix)], axis=2
    )
    out_local = by_head(w_out)

    def to_heads(local):
        block = jnp.zeros(local.shape, local.dtype)
        for k in range(4):
            piece = pick(local, j ^ k)
            if k:
                piece = lax.ppermute(piece, ("y", "c"), [(i, i ^ k) for i in range(4)])
            block = put(block, piece, j ^ k)
        return block.reshape(block_rows, local.shape[2])

    def whole_zx(block):
        whole = jnp.zeros((size, 2) + block.shape, block.dtype)
        for s, b in enumerate(gather_z(block, size)):
            source = lax.rem(z - s + size, size)
            whole = put(whole, b, source, x)
            whole = put(whole, swap(b, "x"), source, 1 - x)
        return whole.reshape((size * 2 * block.shape[0],) + block.shape[1:])

    tokens = hidden_in.reshape(micro, slots, width)
    token_blocks = gather_yc(tokens)

    gains = jnp.stack([attn_gain, mlp_gain], axis=1).astype(F32)
    gain_blocks = jnp.zeros((4, own_rows, 2), F32)
    for k, g in enumerate(gather_yc(gains)):
        gain_blocks = put(gain_blocks, g, j ^ k)
    gains_all = whole_zx(gain_blocks.reshape(block_rows, 2))
    gain_one, gain_two = gains_all[:, 0][None, :], gains_all[:, 1][None, :]

    wqkv = whole_zx(to_heads(qkv_local))
    wo = whole_zx(to_heads(out_local))

    def to_chunks(local):
        whole = jnp.zeros((size, 2, 2, 2, own_rows, local.shape[2]), local.dtype)
        for s in range(size):
            for k in range(2):
                piece = pick(local, lax.rem(z + s, size) * 2 + (y ^ k), 1)
                if s or k:
                    perm = [
                        (a * 2 + b, ((a + s) % size) * 2 + (b ^ k))
                        for a in range(size)
                        for b in range(2)
                    ]
                    piece = lax.ppermute(piece, ("z", "y"), perm)
                source = lax.rem(z - s + size, size)
                over = swap(piece, "x")
                whole = put(whole, piece, source, x, y ^ k, c)
                whole = put(whole, swap(piece, "c"), source, x, y ^ k, 1 - c)
                whole = put(whole, over, source, 1 - x, y ^ k, c)
                whole = put(whole, swap(over, "c"), source, 1 - x, y ^ k, 1 - c)
        return whole.reshape(width, local.shape[2])

    gate_up_local = jnp.concatenate(
        [w_gate.reshape(own_rows, 2 * size, chunk), w_up.reshape(own_rows, 2 * size, chunk)], axis=2
    )
    wgu = to_chunks(gate_up_local)
    wd = to_chunks(w_down.reshape(own_rows, 2 * size, chunk))

    offsets = jnp.arange(slots, dtype=jnp.int32)
    positions = jnp.concatenate([(j ^ k) * slots + offsets for k in range(4)])
    cosine, sine = rope_tables(positions, HEAD_DIMENSION)
    cosine, sine = cosine[None, :, None, :], sine[None, :, None, :]
    span = 4 * slots
    all_rows = jnp.concatenate(token_blocks, axis=1).astype(F32).reshape(group_rows, width)
    all_scale = lax.rsqrt(jnp.mean(all_rows * all_rows, axis=-1, keepdims=True) + EPS_NORM)
    all_hat = all_rows * all_scale
    xn1 = (all_hat * gain_one).astype(BF)
    qkv = dot(xn1, wqkv)
    q = rotary_embed(
        qkv[:, :q_cols].reshape(micro, span, q_heads, HEAD_DIMENSION), cosine, sine
    ).astype(BF)
    k = rotary_embed(
        qkv[:, q_cols : q_cols + kv_cols].reshape(micro, span, 1, HEAD_DIMENSION), cosine, sine
    ).astype(BF)[:, :, 0]
    v = qkv[:, q_cols + kv_cols :].reshape(micro, span, HEAD_DIMENSION).astype(BF)
    allowed = (positions[None, None, :] <= positions[None, :, None]) & (
        positions[None, None, :] < lengths[:, None, None]
    )
    allowed = allowed[:, None, :, :]
    scores = jnp.einsum("mqgd,msd->mgqs", q, k, preferred_element_type=F32) * scale
    scores = jnp.where(allowed, scores, NEG_FILL)
    top = jnp.max(scores, axis=-1, keepdims=True)
    log_total = top + jnp.log(jnp.sum(jnp.exp(scores - top), axis=-1, keepdims=True))
    probs = jnp.where(allowed, jnp.exp(scores - log_total), 0.0)
    probs_low = probs.astype(BF)
    mixed = (
        jnp.einsum("mgqs,msd->mqgd", probs_low, v, preferred_element_type=F32)
        .astype(BF)
        .reshape(group_rows, q_cols)
    )
    branch_part = dot_right(mixed, wo).astype(BF).reshape(micro, 4, slots, width)
    branch = scatter_yc([branch_part[:, k] for k in range(4)]).reshape(rows, width)

    own_slots = j * slots + offsets
    live = (own_slots[None, :] < lengths[:, None]).astype(F32).reshape(rows, 1)
    own_x = tokens.astype(F32).reshape(rows, width)
    first_scale = lax.rsqrt(jnp.mean(own_x * own_x, axis=-1, keepdims=True) + EPS_NORM)
    first_hat = own_x * first_scale
    middle = own_x + branch
    second_scale = lax.rsqrt(jnp.mean(middle * middle, axis=-1, keepdims=True) + EPS_NORM)
    second_hat = middle * second_scale
    second_normalized = (second_hat * gain_two).astype(BF)
    dy = out_grad.astype(F32).reshape(rows, width) * live

    def joined(block):
        return jnp.concatenate([b for pair in gather_zy(block, size) for b in pair], axis=0)

    dfb = joined(dy.astype(BF))
    xn2 = joined(second_normalized)
    gate_up = dot(xn2, wgu)
    gate, up = gate_up[:, :chunk], gate_up[:, chunk:]
    sigmoid = jax.nn.sigmoid(gate)
    activated = gate * sigmoid
    hidden = (activated * up).astype(BF)
    dhid = dot(dfb, wd)
    dgu = jnp.concatenate(
        [
            (dhid * up * sigmoid * (1.0 + gate * (1.0 - sigmoid))).astype(BF),
            (dhid * activated).astype(BF),
        ],
        axis=1,
    )

    def home(part):
        part = part.astype(BF).reshape(size, 2, rows, width)
        return scatter_z(
            [part[s, 0] for s in range(size)], [part[s, 1] for s in range(size)], "y", size
        )

    dxn2 = home(dot_right(dgu, wgu))
    feed = home(dot_right(hidden, wd))

    def to_owners(grad):
        columns = grad.shape[1]
        grad = grad.astype(BF).reshape(size, 2, 2, 2, own_rows, columns)
        near = pick(grad, c, 3).astype(F32) + swap(pick(grad, 1 - c, 3), "c")
        near = near.astype(BF)
        total = (pick(near, x, 1).astype(F32) + swap(pick(near, 1 - x, 1), "x")).astype(BF)
        result = jnp.zeros((2 * size, own_rows, columns), BF)
        for s in range(size):
            for k in range(2):
                piece = pick(pick(total, lax.rem(z + s, size)), y ^ k)
                if s or k:
                    perm = [
                        (a * 2 + b, ((a + s) % size) * 2 + (b ^ k))
                        for a in range(size)
                        for b in range(2)
                    ]
                    piece = lax.ppermute(piece, ("z", "y"), perm)
                result = put(result, piece, lax.rem(z - s + size, size) * 2 + (y ^ k))
        return jnp.swapaxes(result, 0, 1).astype(F32)

    gate_up_grad = to_owners(dot_rows(xn2, dgu))
    grad_gate = gate_up_grad[:, :, :chunk].reshape(own_rows, ff)
    grad_up = gate_up_grad[:, :, chunk:].reshape(own_rows, ff)
    grad_down = to_owners(dot_rows(dfb, hidden)).reshape(own_rows, ff)

    outputs = (live * (middle + feed)).astype(BF).reshape(hidden_in.shape)

    gain_two_part = jnp.sum(second_hat * dxn2, axis=0)
    dh1 = dy + norm_backward(second_hat, second_scale, dxn2 * gain_two)
    dab = jnp.concatenate(gather_yc(dh1.astype(BF).reshape(micro, slots, width)), axis=1).reshape(
        group_rows, width
    )
    dob = dot(dab, wo).astype(BF).reshape(micro, span, q_heads, HEAD_DIMENSION)
    dprob = jnp.einsum("mqgd,msd->mgqs", dob, v, preferred_element_type=F32)
    dscore = (probs * (dprob - jnp.sum(probs * dprob, axis=-1, keepdims=True))).astype(BF)
    dq = jnp.einsum("mgqs,msd->mqgd", dscore, k, preferred_element_type=F32) * scale
    dk = jnp.einsum("mgqs,mqgd->msd", dscore, q, preferred_element_type=F32) * scale
    dv = jnp.einsum("mgqs,mqgd->msd", probs_low, dob, preferred_element_type=F32)
    dq = rotary_backward(dq, cosine, sine).astype(BF).reshape(group_rows, q_cols)
    dk = rotary_backward(dk[:, :, None, :], cosine, sine).astype(BF).reshape(group_rows, kv_cols)
    dqkv = jnp.concatenate([dq, dk, dv.astype(BF).reshape(group_rows, kv_cols)], axis=1)
    dxn1_part = dot_right(dqkv, wqkv)
    gain_one_part = jnp.sum(all_hat * dxn1_part, axis=0)

    def to_blocks(grad):
        grad = grad.reshape((size, 2, block_rows) + grad.shape[1:])
        parts, partners = [], []
        for s in range(size):
            at = pick(grad, lax.rem(z - s + size, size))
            parts.append(pick(at, x))
            partners.append(pick(at, 1 - x))
        return scatter_z(parts, partners, "x", size)

    def to_rows(block):
        block = block.astype(BF).reshape(4, own_rows, -1)
        result = jnp.zeros(block.shape, BF)
        for k in range(4):
            piece = pick(block, j ^ k)
            if k:
                piece = lax.ppermute(piece, ("y", "c"), [(i, i ^ k) for i in range(4)])
            result = put(result, piece, j ^ k)
        return jnp.swapaxes(result, 0, 1).astype(F32)

    out_grads = to_rows(to_blocks(dot_rows(dab, mixed).astype(BF)))
    qkv_grads = to_rows(to_blocks(dot_rows(xn1, dqkv).astype(BF)))
    grad_query = qkv_grads[:, :, :q_cols].reshape(own_rows, 4 * q_cols)
    grad_key = qkv_grads[:, :, q_cols : q_cols + kv_cols].reshape(own_rows, 4 * kv_cols)
    grad_value = qkv_grads[:, :, q_cols + kv_cols :].reshape(own_rows, 4 * kv_cols)
    grad_out = out_grads.reshape(own_rows, 4 * q_cols)

    gain_block = to_blocks(jnp.stack([gain_one_part, gain_two_part], axis=1))
    gain_block = gain_block.reshape(4, own_rows, 2)
    gain_grads = pick(gain_block, j)
    for k in range(1, 4):
        gain_grads = gain_grads + lax.ppermute(
            pick(gain_block, j ^ k), ("y", "c"), [(i, i ^ k) for i in range(4)]
        )

    dxn1_part = dxn1_part.astype(BF).reshape(micro, 4, slots, width)
    dxn1 = scatter_yc([dxn1_part[:, k] for k in range(4)]).reshape(rows, width)
    input_grads = (
        (dh1 + norm_backward(first_hat, first_scale, dxn1 * gain_one))
        .astype(BF)
        .reshape(hidden_in.shape)
    )
    return (
        outputs,
        input_grads,
        gain_grads[:, 0],
        grad_query,
        grad_key,
        grad_value,
        grad_out,
        gain_grads[:, 1],
        grad_gate,
        grad_up,
        grad_down,
    )


def solution(mesh):
    dp, fsdp = mesh.shape["dp"], mesh.shape["fsdp"]
    fine = Mesh(mesh.devices.reshape(dp // 2, 2, fsdp // 2, 2), ("z", "x", "y", "c"))
    batch, slot, both = ("z", "x"), ("y", "c"), ("z", "x", "y", "c")
    vector, matrix = P(both), P(both, None)
    rows = P(None, batch, slot, None)
    return jax.shard_map(
        per_device,
        mesh=fine,
        in_specs=(rows, P(None, batch), rows) + (vector,) + (matrix,) * 4 + (vector,) + (matrix,) * 3,
        out_specs=(rows, rows, vector) + (matrix,) * 4 + (vector,) + (matrix,) * 3,
        check_vma=False,
    )
```

time: 3170 us -> 951 us (0.30)
  waiting for transfers between devices: 2510 us -> 392 us
  local copies, waits for them, and re-layouts: 52.5 us -> 252 us
  matrix products: 275 us -> 81.5 us
  starting transfers between devices: 0.47 us -> 147 us
  blocking collectives: 133 us -> 0 us
  other arithmetic: 179 us -> 55.4 us
    reduce_scatter x3 -> x0, waiting for transfers between devices: 1730 us -> none  [the longest x1 1590 us: per_device(): lax.psum_scatter(jnp.concatenate([rows_product(normed_cols, mlp_pair), ro...]
    all_gather x9 -> x0, waiting for transfers between devices: 772 us -> none  [the longest x1 190 us: per_device(): lax.all_gather(w_up, ('dp', 'fsdp'), axis=0, tiled=True)]
    ppermute x0 -> x180, waiting for transfers between devices: none -> 392 us  [the longest x107 168 us: swap(): return lax.ppermute(value, axis, [(0, 1), (1, 0)])]
    dot_general x24 -> x18, matrix products: 275 us -> 81.5 us  [the longest x4 28.1 us: dot_right(): lax.dot_general(left, right, (((1,), (1,)), ((), ())), preferred_element_...]
    concatenate x3 -> x4, other arithmetic: 168 us -> 3.15 us  [the longest x1 1.76 us: per_device(): jnp.concatenate(gather_yc(dh1.astype(BF).reshape(micro, slots, width)), a...]
    ppermute x0 -> x180, starting transfers between devices: none -> 147 us  [the longest x107 78 us: swap(): return lax.ppermute(value, axis, [(0, 1), (1, 0)])]
    unnamed x3 -> x0, blocking collectives: 133 us -> none
    dynamic_update_slice x0 -> x122, local copies, waits for them, and re-layouts: none -> 116 us  [put(): return lax.dynamic_update_slice(buffer, piece, starts)]
  transfers between devices with their start and end apart: 12 -> 180, of which waited for: 10 -> 80; matrix products, arithmetic and copies ran while one was open for 12% -> 31% of each run, Pallas kernels for 0% -> 0%
where the time goes in v1:
time: 951 us; the launch traced here: 932 us
  waiting for transfers between devices  392 us (41%)
  local copies, waits for them, and re-layouts  252 us (26%)
  starting transfers between devices  147 us (15%)
  matrix products  81.5 us (9%)
  other arithmetic  55.4 us (6%)
    ppermute x107, waiting for transfers between devices, swap(): return lax.ppermute(value, axis, [(0, 1), (1, 0)])  168 us
    dynamic_update_slice x122, local copies, waits for them, and re-layouts, put(): return lax.dynamic_update_slice(buffer, piece, starts)  116 us
    ppermute x30, waiting for transfers between devices, ring(): return lax.ppermute(value, 'z', [(i, (i + 1) % size) for i in range(size)])  115 us
    ppermute x107, starting transfers between devices, swap(): return lax.ppermute(value, axis, [(0, 1), (1, 0)])  78 us
    unnamed x229, local copies, waits for them, and re-layouts  55.2 us
    ppermute x14, waiting for transfers between devices, to_chunks(): piece = lax.ppermute(piece, ('z', 'y'), perm)  48.9 us
    ppermute x14, waiting for transfers between devices, to_owners(): piece = lax.ppermute(piece, ('z', 'y'), perm)  35 us
    dot_general x4, matrix products, dot_right(): lax.dot_general(left, right, (((1,), (1,)), ((), ())), preferred_element_...  28.1 us
  transfers between devices with their start and end apart: 180, of which 80 were waited for; matrix products, arithmetic and copies ran while one was open for 31% of the time, Pallas kernels for 0%

profile of v1, /device:TPU:0, one launch (start us, length us, event | category | flops | bytes accessed | tf_op | source)
XLA Modules:
  0.0 931.9 jit_solution(15288154136227680828)
XLA Ops:
  210.1 11.5 %collective-permute-done.28 = bf16[256,512]{1,0:T(8,128)(2,1)S(1)} collective-permute-done((bf16[256,512]{1,0:T(8,128)(2,1)S(1)}, bf16[256,512]{1,0:T(8,128)(2,1)S(1)}, u32[]{:S(2)}, u32[]{:S(2)}) %collective-permute-start.28) | collective-permute-done | bytes 262176 | tf_op jit(solution)/shard_map/ppermute | solution.py:60
  224.0 18.0 %collective-permute-done.50 = bf16[64,2048]{1,0:T(8,128)(2,1)S(1)} collective-permute-done((bf16[64,2048]{1,0:T(8,128)(2,1)S(1)}, bf16[64,2048]{1,0:T(8,128)(2,1)S(1)}, u32[]{:S(2)}, u32[]{:S(2)}) %collective-permute-start.50) | collective-permute-done | bytes 262176 | tf_op jit(solution)/shard_map/ppermute | solution.py:188
  266.9 9.8 %collective-permute-done.62 = bf16[64,2048]{1,0:T(8,128)(2,1)S(1)} collective-permute-done((bf16[64,2048]{1,0:T(8,128)(2,1)S(1)}, bf16[64,2048]{1,0:T(8,128)(2,1)S(1)}, u32[]{:S(2)}, u32[]{:S(2)}) %collective-permute-start.62) | collective-permute-done | bytes 262176 | tf_op jit(solution)/shard_map/ppermute | solution.py:188
  314.7 8.6 collective-permute-done.19
  336.1 9.9 %collective-permute-done.20 = bf16[256,1024]{1,0:T(8,128)(2,1)S(1)} collective-permute-done((bf16[256,1024]{1,0:T(8,128)(2,1)S(1)}, bf16[256,1024]{1,0:T(8,128)(2,1)S(1)}, u32[]{:S(2)}, u32[]{:S(2)}) %collective-permute-start.20) | collective-permute-done | bytes 524320 | tf_op jit(solution)/shard_map/ppermute | solution.py:60
  375.4 9.3 %collective-permute-done.35 = bf16[2,64,2048]{2,1,0:T(8,128)(2,1)S(1)} collective-permute-done((bf16[2,64,2048]{2,1,0:T(8,128)(2,1)S(1)}, bf16[2,64,2048]{2,1,0:T(8,128)(2,1)S(1)}, u32[]{:S(2)}, u32[]{:S(2)}) %collective-permute-start.35) | collective-permute-done | bytes 524320 | tf_op jit(solution)/shard_map/ppermute | solution.py:60
  409.9 8.7 collective-permute-done.39
  420.1 10.2 %collective-permute-done.38 = bf16[128,2048]{1,0:T(8,128)(2,1)S(1)} collective-permute-done((bf16[128,2048]{1,0:T(8,128)(2,1)S(1)}, bf16[128,2048]{1,0:T(8,128)(2,1)S(1)}, u32[]{:S(2)}, u32[]{:S(2)}) %collective-permute-start.38) | collective-permute-done | bytes 524320 | tf_op jit(solution)/shard_map/ppermute | solution.py:60
  441.5 10.2 %collective-permute-done.42 = bf16[128,2048]{1,0:T(8,128)(2,1)S(1)} collective-permute-done((bf16[128,2048]{1,0:T(8,128)(2,1)S(1)}, bf16[128,2048]{1,0:T(8,128)(2,1)S(1)}, u32[]{:S(2)}, u32[]{:S(2)}) %collective-permute-start.42) | collective-permute-done | bytes 524320 | tf_op jit(solution)/shard_map/ppermute | solution.py:60
  451.8 12.8 %fusion.88 = f32[1024,2048]{1,0:T(8,128)S(1)} fusion(bf16[1024,2048]{1,0:T(8,128)(2,1)S(1)} %constant_dynamic-update-slice_fusion.2, bf16[2048,2048]{1,0:T(8,128)(2,1)} %bitcast.99), kind=kOutput, calls=%fused_computation.436 | convolution fusion | flops 8589934592 | bytes 20971520 | tf_op jit(solution)/shard_map/dot_general | solution.py:48
  464.6 9.2 multiply_convert_fusion.2
  473.9 12.8 %convolution_convert_fusion.2 = bf16[1024,2048]{1,0:T(8,128)(2,1)S(1)} fusion(bf16[2048,2048]{1,0:T(8,128)(2,1)} %bitcast.99, bf16[1024,1024]{1,0:T(8,128)(2,1)S(1)} %get-tuple-element.22, bf16[1024,1024]{1,0:T(8,128)(2,1)S(1)} %get-tuple-element.21), kind=kOutput, calls=%fused_computation.22 | convolution fusion | flops 8600420352 | bytes 16777216 | tf_op jit(solution)/shard_map/dot_general | solution.py:52
  501.7 11.2 %collective-permute-done.108 = bf16[128,2048]{1,0:T(8,128)(2,1)S(1)} collective-permute-done((bf16[128,2048]{1,0:T(8,128)(2,1)S(1)}, bf16[128,2048]{1,0:T(8,128)(2,1)S(1)}, u32[]{:S(2)}, u32[]{:S(2)}) %collective-permute-start.108) | collective-permute-done | bytes 524320 | tf_op jit(solution)/shard_map/ppermute | solution.py:60
  526.4 9.0 collective-permute-done.107
  554.4 14.6 %collective-permute-done.106 = bf16[128,2048]{1,0:T(8,128)(2,1)S(1)} collective-permute-done((bf16[128,2048]{1,0:T(8,128)(2,1)S(1)}, bf16[128,2048]{1,0:T(8,128)(2,1)S(1)}, u32[]{:S(2)}, u32[]{:S(2)}) %collective-permute-start.106) | collective-permute-done | bytes 524320 | tf_op jit(solution)/shard_map/ppermute | solution.py:60
  576.9 10.6 %collective-permute-done.125 = bf16[128,2048]{1,0:T(8,128)(2,1)} collective-permute-done((bf16[128,2048]{1,0:T(8,128)(2,1)}, bf16[128,2048]{1,0:T(8,128)(2,1)}, u32[]{:S(2)}, u32[]{:S(2)}) %collective-permute-start.125) | collective-permute-done | bytes 524320 | tf_op jit(solution)/shard_map/ppermute | solution.py:64
  607.2 12.0 %convolution_convert_fusion = bf16[2048,2048]{1,0:T(8,128)(2,1)} fusion(bf16[1024,2048]{1,0:T(8,128)(2,1)S(1)} %copy-done.73, bf16[1024,1024]{1,0:T(8,128)(2,1)S(1)} %copy-done.88, bf16[1024,1024]{1,0:T(8,128)(2,1)S(1)} %copy-done.86), kind=kOutput, calls=%fused_computation.2 | convolution fusion | flops 8602517504 | bytes 16777216 | tf_op jit(solution)/shard_map/dot_general | solution.py:56
  738.1 8.7 collective-permute-done.145
  771.7 13.2 %collective-permute-done.146 = bf16[256,1024]{1,0:T(8,128)(2,1)} collective-permute-done((bf16[256,1024]{1,0:T(8,128)(2,1)}, bf16[256,1024]{1,0:T(8,128)(2,1)}, u32[]{:S(2)}, u32[]{:S(2)}) %collective-permute-start.146) | collective-permute-done | bytes 524320 | tf_op jit(solution)/shard_map/ppermute | solution.py:64
  796.7 10.1 %collective-permute-done.147 = bf16[256,1024]{1,0:T(8,128)(2,1)S(1)} collective-permute-done((bf16[256,1024]{1,0:T(8,128)(2,1)S(1)}, bf16[256,1024]{1,0:T(8,128)(2,1)S(1)}, u32[]{:S(2)}, u32[]{:S(2)}) %collective-permute-start.147) | collective-permute-done | bytes 524320 | tf_op jit(solution)/shard_map/ppermute | solution.py:64
  810.8 14.3 %collective-permute-done.148 = bf16[256,1024]{1,0:T(8,128)(2,1)S(1)} collective-permute-done((bf16[256,1024]{1,0:T(8,128)(2,1)S(1)}, bf16[256,1024]{1,0:T(8,128)(2,1)S(1)}, u32[]{:S(2)}, u32[]{:S(2)}) %collective-permute-start.148) | collective-permute-done | bytes 524320 | tf_op jit(solution)/shard_map/ppermute | solution.py:64
  862.7 9.1 collective-permute-done.167
  892.4 8.3 dynamic_update_slice.483
  900.7 8.3 dynamic_update_slice.484
  (861 shorter events, 668.1 us)
Async XLA Ops:
  2.0 39.6 %collective-permute-start.3 = (f32[64,2]{0,1:T(2,128)}, f32[64,2]{0,1:T(2,128)S(1)}, u32[]{:S(2)}, u32[]{:S(2)}) collective-permute-start(f32[64,2]{0,1:T(2,128)} %maximum_convert_fusion.1), channel_id=1, source_target_pairs={{0,1},{1,0},{2,3},{3,2},{4,5},{5,4},{6,7},{7,6},{8,9},{9,8},{10,11... | collective-permute-start | bytes 1544 | tf_op jit(solution)/shard_map/ppermute | solution.py:60
  2.5 38.6 %collective-permute-start.4 = (f32[64,2]{0,1:T(2,128)}, f32[64,2]{0,1:T(2,128)}, u32[]{:S(2)}, u32[]{:S(2)}) collective-permute-start(f32[64,2]{0,1:T(2,128)} %maximum_convert_fusion.1), channel_id=1, source_target_pairs={{0,2},{2,0},{1,3},{3,1},{4,6},{6,4},{5,7},{7,5},{8,10},{10,8},{9,1... | collective-permute-start | bytes 1544 | tf_op jit(solution)/shard_map/ppermute | solution.py:60
  5.0 290.4 %collective-permute-start.1 = (bf16[2,64,2048]{2,1,0:T(8,128)(2,1)}, bf16[2,64,2048]{2,1,0:T(8,128)(2,1)}, u32[]{:S(2)}, u32[]{:S(2)}) collective-permute-start(bf16[2,64,2048]{2,1,0:T(8,128)(2,1)} %bitcast.742), channel_id=1, source_target_pairs={{0,2},{2,0},{1,3},{3,1},{4,6},{6,4},{5,7},{7,5},{8,10},{10,8},{9,1... | collective-permute-start | bytes 1572872 | tf_op jit(solution)/shard_map/ppermute | solution.py:60
  81.4 228.8 %collective-permute-start = (bf16[2,64,2048]{2,1,0:T(8,128)(2,1)S(1)}, bf16[2,64,2048]{2,1,0:T(8,128)(2,1)S(1)}, u32[]{:S(2)}, u32[]{:S(2)}) collective-permute-start(bf16[2,64,2048]{2,1,0:T(8,128)(2,1)S(1)} %bitcast.743), channel_id=1, source_target_pairs={{0,1},{1,0},{2,3},{3,2},{4,5},{5,4},{6,7},{7,6},{8,9},{9,8},{10,11... | collective-permute-start | bytes 1572872 | tf_op jit(solution)/shard_map/ppermute | solution.py:60
  82.2 36.9 %collective-permute-start.43 = (bf16[64,2048]{1,0:T(8,128)(2,1)}, bf16[64,2048]{1,0:T(8,128)(2,1)S(1)}, u32[]{:S(2)}, u32[]{:S(2)}) collective-permute-start(bf16[64,2048]{1,0:T(8,128)(2,1)} %bitcast.733), channel_id=1, source_target_pairs={{0,1},{1,0},{2,3},{3,2},{4,5},{5,4},{6,7},{7,6},{8,9},{9,8},{10,11... | collective-permute-start | bytes 786440 | tf_op jit(solution)/shard_map/ppermute | solution.py:60
  83.6 36.4 %collective-permute-start.44 = (bf16[64,2048]{1,0:T(8,128)(2,1)}, bf16[64,2048]{1,0:T(8,128)(2,1)}, u32[]{:S(2)}, u32[]{:S(2)}) collective-permute-start(bf16[64,2048]{1,0:T(8,128)(2,1)} %bitcast.733), channel_id=1, source_target_pairs={{0,4},{4,0},{1,5},{5,1},{2,6},{6,2},{3,7},{7,3},{8,12},{12,8},{9,1... | collective-permute-start | bytes 786440 | tf_op jit(solution)/shard_map/ppermute | solution.py:60
  295.4 74.5 %collective-permute-start.71 = (bf16[64,2048]{1,0:T(8,128)(2,1)}, bf16[64,2048]{1,0:T(8,128)(2,1)}, u32[]{:S(2)}, u32[]{:S(2)}) collective-permute-start(bf16[64,2048]{1,0:T(8,128)(2,1)} %collective-permute-done.70), channel_id=1, source_target_pairs={{0,1},{1,0},{2,3},{3,2},{4,5},{5,4},{6,7},{7,6},{8,9},{9,8},{10,11... | collective-permute-start | bytes 786440 | tf_op jit(solution)/shard_map/ppermute | solution.py:60
  306.2 40.9 %collective-permute-start.72 = (bf16[64,2048]{1,0:T(8,128)(2,1)}, bf16[64,2048]{1,0:T(8,128)(2,1)}, u32[]{:S(2)}, u32[]{:S(2)}) collective-permute-start(bf16[64,2048]{1,0:T(8,128)(2,1)} %collective-permute-done.70), channel_id=1, source_target_pairs={{0,4},{4,0},{1,5},{5,1},{2,6},{6,2},{3,7},{7,3},{8,12},{12,8},{9,1... | collective-permute-start | bytes 786440 | tf_op jit(solution)/shard_map/ppermute | solution.py:60
  331.9 33.9 %collective-permute-start.69 = (bf16[64,2048]{1,0:T(8,128)(2,1)}, bf16[64,2048]{1,0:T(8,128)(2,1)}, u32[]{:S(2)}, u32[]{:S(2)}) collective-permute-start(bf16[64,2048]{1,0:T(8,128)(2,1)} %collective-permute-done.68), channel_id=1, source_target_pairs={{0,1},{1,0},{2,3},{3,2},{4,5},{5,4},{6,7},{7,6},{8,9},{9,8},{10,11... | collective-permute-start | bytes 786440 | tf_op jit(solution)/shard_map/ppermute | solution.py:60
  346.0 43.7 %collective-permute-start.114 = (bf16[128,2048]{1,0:T(8,128)(2,1)}, bf16[128,2048]{1,0:T(8,128)(2,1)}, u32[]{:S(2)}, u32[]{:S(2)}) collective-permute-start(bf16[128,2048]{1,0:T(8,128)(2,1)} %collective-permute-done.113), channel_id=1, source_target_pairs={{0,2},{2,0},{1,3},{3,1},{4,6},{6,4},{5,7},{7,5},{8,10},{10,8},{9,1... | collective-permute-start | bytes 1572872 | tf_op jit(solution)/shard_map/ppermute | solution.py:60
  500.3 35.1 %collective-permute-start.107 = (bf16[128,2048]{1,0:T(8,128)(2,1)S(1)}, bf16[128,2048]{1,0:T(8,128)(2,1)S(1)}, u32[]{:S(2)}, u32[]{:S(2)}) collective-permute-start(bf16[128,2048]{1,0:T(8,128)(2,1)S(1)} %get-tuple-element.42), channel_id=1, source_target_pairs={{0,2},{2,0},{1,3},{3,1},{4,6},{6,4},{5,7},{7,5},{8,10},{10,8},{9,1... | collective-permute-start | bytes 1572872 | tf_op jit(solution)/shard_map/ppermute | solution.py:60
  524.1 52.7 %collective-permute-start.119 = (bf16[128,2048]{1,0:T(8,128)(2,1)}, bf16[128,2048]{1,0:T(8,128)(2,1)}, u32[]{:S(2)}, u32[]{:S(2)}) collective-permute-start(bf16[128,2048]{1,0:T(8,128)(2,1)} %get-tuple-element.36), channel_id=1, source_target_pairs={{0,2},{2,0},{1,3},{3,1},{4,6},{6,4},{5,7},{7,5},{8,10},{10,8},{9,1... | collective-permute-start | bytes 1572872 | tf_op jit(solution)/shard_map/ppermute | solution.py:60
  525.3 43.8 %collective-permute-start.106 = (bf16[128,2048]{1,0:T(8,128)(2,1)S(1)}, bf16[128,2048]{1,0:T(8,128)(2,1)S(1)}, u32[]{:S(2)}, u32[]{:S(2)}) collective-permute-start(bf16[128,2048]{1,0:T(8,128)(2,1)S(1)} %get-tuple-element.43), channel_id=1, source_target_pairs={{0,2},{2,0},{1,3},{3,1},{4,6},{6,4},{5,7},{7,5},{8,10},{10,8},{9,1... | collective-permute-start | bytes 1572872 | tf_op jit(solution)/shard_map/ppermute | solution.py:60
  535.6 33.5 %collective-permute-start.110 = (bf16[128,2048]{1,0:T(8,128)(2,1)S(1)}, bf16[128,2048]{1,0:T(8,128)(2,1)S(1)}, u32[]{:S(2)}, u32[]{:S(2)}) collective-permute-start(bf16[128,2048]{1,0:T(8,128)(2,1)S(1)} %fusion.35), channel_id=1, source_target_pairs={{0,8},{8,16},{16,24},{24,0},{1,9},{9,17},{17,25},{25,1},{2,10},{10... | collective-permute-start | bytes 1572872 | tf_op jit(solution)/shard_map/ppermute | solution.py:64
  546.6 43.4 %collective-permute-start.105 = (bf16[128,2048]{1,0:T(8,128)(2,1)}, bf16[128,2048]{1,0:T(8,128)(2,1)}, u32[]{:S(2)}, u32[]{:S(2)}) collective-permute-start(bf16[128,2048]{1,0:T(8,128)(2,1)} %get-tuple-element.40), channel_id=1, source_target_pairs={{0,2},{2,0},{1,3},{3,1},{4,6},{6,4},{5,7},{7,5},{8,10},{10,8},{9,1... | collective-permute-start | bytes 1572872 | tf_op jit(solution)/shard_map/ppermute | solution.py:60
  553.4 48.0 %collective-permute-start.171 = (bf16[4,2,2,64,1024]{4,3,2,0,1:T(8,128)(2,1)}, bf16[4,2,2,64,1024]{4,3,2,0,1:T(8,128)(2,1)}, u32[]{:S(2)}, u32[]{:S(2)}) collective-permute-start(bf16[4,2,2,64,1024]{4,3,2,0,1:T(8,128)(2,1)} %bitcast.715), channel_id=1, source_target_pairs={{0,1},{1,0},{2,3},{3,2},{4,5},{5,4},{6,7},{7,6},{8,9},{9,8},{10,11... | collective-permute-start | bytes 6291464 | tf_op jit(solution)/shard_map/ppermute | solution.py:60
  628.7 126.8 %collective-permute-start.162 = (bf16[4,2,2,64,2048]{4,3,2,0,1:T(8,128)(2,1)}, bf16[4,2,2,64,2048]{4,3,2,0,1:T(8,128)(2,1)}, u32[]{:S(2)}, u32[]{:S(2)}) collective-permute-start(bf16[4,2,2,64,2048]{4,3,2,0,1:T(8,128)(2,1)} %bitcast.714), channel_id=1, source_target_pairs={{0,1},{1,0},{2,3},{3,2},{4,5},{5,4},{6,7},{7,6},{8,9},{9,8},{10,11... | collective-permute-start | bytes 12582920 | tf_op jit(solution)/shard_map/ppermute | solution.py:60
  692.4 42.9 %collective-permute-start.130 = (bf16[2,64,2048]{2,1,0:T(8,128)(2,1)}, bf16[2,64,2048]{2,1,0:T(8,128)(2,1)}, u32[]{:S(2)}, u32[]{:S(2)}) collective-permute-start(bf16[2,64,2048]{2,1,0:T(8,128)(2,1)} %get-tuple-element.58), channel_id=1, source_target_pairs={{0,1},{1,0},{2,3},{3,2},{4,5},{5,4},{6,7},{7,6},{8,9},{9,8},{10,11... | collective-permute-start | bytes 1572872 | tf_op jit(solution)/shard_map/ppermute | solution.py:60
  715.3 48.8 %collective-permute-start.129 = (bf16[2,64,2048]{2,1,0:T(8,128)(2,1)}, bf16[2,64,2048]{2,1,0:T(8,128)(2,1)}, u32[]{:S(2)}, u32[]{:S(2)}) collective-permute-start(bf16[2,64,2048]{2,1,0:T(8,128)(2,1)} %get-tuple-element.57), channel_id=1, source_target_pairs={{0,1},{1,0},{2,3},{3,2},{4,5},{5,4},{6,7},{7,6},{8,9},{9,8},{10,11... | collective-permute-start | bytes 1572872 | tf_op jit(solution)/shard_map/ppermute | solution.py:60
  752.4 43.2 %collective-permute-start.143 = (bf16[256,1024]{1,0:T(8,128)(2,1)}, bf16[256,1024]{1,0:T(8,128)(2,1)}, u32[]{:S(2)}, u32[]{:S(2)}) collective-permute-start(bf16[256,1024]{1,0:T(8,128)(2,1)} %get-tuple-element.33), channel_id=1, source_target_pairs={{0,4},{4,0},{1,5},{5,1},{2,6},{6,2},{3,7},{7,3},{8,12},{12,8},{9,1... | collective-permute-start | bytes 1572872 | tf_op jit(solution)/shard_map/ppermute | solution.py:60
  753.8 57.0 %collective-permute-start.142 = (bf16[256,1024]{1,0:T(8,128)(2,1)}, bf16[256,1024]{1,0:T(8,128)(2,1)S(1)}, u32[]{:S(2)}, u32[]{:S(2)}) collective-permute-start(bf16[256,1024]{1,0:T(8,128)(2,1)} %get-tuple-element.30), channel_id=1, source_target_pairs={{0,4},{4,0},{1,5},{5,1},{2,6},{6,2},{3,7},{7,3},{8,12},{12,8},{9,1... | collective-permute-start | bytes 1572872 | tf_op jit(solution)/shard_map/ppermute | solution.py:60
  784.9 51.4 %collective-permute-start.163 = (bf16[4,2,64,2048]{3,2,1,0:T(8,128)(2,1)}, bf16[4,2,64,2048]{3,2,1,0:T(8,128)(2,1)S(1)}, u32[]{:S(2)}, u32[]{:S(2)}) collective-permute-start(bf16[4,2,64,2048]{3,2,1,0:T(8,128)(2,1)} %dynamic-slice_bitcast_fusion), channel_id=1, source_target_pairs={{0,4},{4,0},{1,5},{5,1},{2,6},{6,2},{3,7},{7,3},{8,12},{12,8},{9,1... | collective-permute-start | bytes 6291464 | tf_op jit(solution)/shard_map/ppermute | solution.py:60
  844.3 33.6 %collective-permute-start.168 = (bf16[64,2048]{1,0:T(8,128)(2,1)}, bf16[64,2048]{1,0:T(8,128)(2,1)}, u32[]{:S(2)}, u32[]{:S(2)}) collective-permute-start(bf16[64,2048]{1,0:T(8,128)(2,1)} %get-tuple-element.47), channel_id=1, source_target_pairs={{0,18},{2,16},{8,26},{10,24},{16,2},{18,0},{24,10},{26,8},{1,19},{... | collective-permute-start | bytes 786440 | tf_op jit(solution)/shard_map/ppermute | solution.py:293
  846.6 33.5 %collective-permute-start.169 = (bf16[64,2048]{1,0:T(8,128)(2,1)}, bf16[64,2048]{1,0:T(8,128)(2,1)}, u32[]{:S(2)}, u32[]{:S(2)}) collective-permute-start(bf16[64,2048]{1,0:T(8,128)(2,1)} %get-tuple-element.46), channel_id=1, source_target_pairs={{0,24},{2,26},{8,0},{10,2},{16,8},{18,10},{24,16},{26,18},{1,25},{... | collective-permute-start | bytes 786440 | tf_op jit(solution)/shard_map/ppermute | solution.py:293
  (245 other events, 3501.7 us)

commit v2 on v1

v2 whole, which is shorter than its diff:
```python
import jax
import jax.numpy as jnp
from jax import lax
from jax.sharding import Mesh, PartitionSpec as P

QUERY_HEADS = 8
KEY_VALUE_HEADS = 4
HEAD_DIMENSION = 256

EPS_NORM = 1e-06
ROPE_BASE = 1000042.0
NEG_FILL = -1e30

BF = jnp.bfloat16
F32 = jnp.float32


def rope_tables(positions, head_size):
    half_size = head_size // 2
    inverse = ROPE_BASE ** (-(jnp.arange(half_size, dtype=F32) * 2.0 / head_size))
    angles = positions.astype(F32)[:, None] * inverse[None, :]
    return jnp.cos(angles), jnp.sin(angles)


def rotary_embed(rows, cosine, sine):
    half = rows.shape[-1] // 2
    first, second = rows[..., :half], rows[..., half:]
    return jnp.concatenate(
        [first * cosine - second * sine, second * cosine + first * sine], axis=-1
    )


def rotary_backward(grads, cosine, sine):
    half = grads.shape[-1] // 2
    first, second = grads[..., :half], grads[..., half:]
    return jnp.concatenate(
        [first * cosine + second * sine, second * cosine - first * sine], axis=-1
    )


def norm_backward(normalized, reciprocal, gradient):
    return reciprocal * (
        gradient - normalized * jnp.mean(gradient * normalized, axis=-1, keepdims=True)
    )


def dot(left, right):
    return jnp.dot(left, right, preferred_element_type=F32)


def dot_right(left, right):
    return lax.dot_general(left, right, (((1,), (1,)), ((), ())), preferred_element_type=F32)


def dot_rows(left, right):
    return lax.dot_general(left, right, (((0,), (0,)), ((), ())), preferred_element_type=F32)


def swap(value, axis):
    return lax.ppermute(value, axis, [(0, 1), (1, 0)])


def ring(value, size):
    return lax.ppermute(value, "z", [(i, (i + 1) % size) for i in range(size)])


def pick(value, index, axis=0):
    return lax.dynamic_index_in_dim(value, index, axis, keepdims=False)


def put(buffer, piece, *index):
    piece = piece.reshape((1,) * len(index) + piece.shape)
    starts = tuple(index) + (0,) * (buffer.ndim - len(index))
    return lax.dynamic_update_slice(buffer, piece, starts)


def tie(*values):
    return lax.optimization_barrier(values)


def cut(value, start, count, axis):
    return lax.dynamic_slice_in_dim(value, start, count, axis)


def swap_cores(blocks):
    return [[swap(b[i], "c") for i in range(b.shape[0])] for b in blocks]


def gather_yc(block, across=None):
    if across is None:
        across = swap(block, "y")
    near, far = (jnp.stack(b) for b in swap_cores([block, across]))
    return [block, near, across, far]


def scatter_yc(parts):
    far, near = (jnp.stack(b) for b in swap_cores([parts[3], parts[1]]))
    away = (parts[2].astype(F32) + far).astype(BF)
    return parts[0].astype(F32) + near + swap(away, "y")


def to_peers_yc(piece_for):
    pieces = [piece_for(0)]
    for k in range(1, 4):
        pieces.append(lax.ppermute(piece_for(k), ("y", "c"), [(i, i ^ k) for i in range(4)]))
    return pieces


def swap_in_turn(pieces, axis):
    got = []
    for piece in pieces:
        if got:
            piece, got[-1] = tie(piece, got[-1])
        got.append(swap(piece, axis))
    return got


def scatter_z(parts, partners, axis, size, ties=None):
    total = None
    order = [(step + 1) % size for step in range(size)]
    got = swap_in_turn([partners[s] for s in order], axis)
    for step in range(size):
        own = parts[order[step]].astype(F32) + got[step]
        total = own if total is None else own + ring(total, size)
        if step < size - 1:
            total = total.astype(BF)
            if ties and step in ties:
                total, *ties[step] = tie(total, *ties[step])
    return total


def per_device(
    hidden_in,
    seq_lengths,
    out_grad,
    attn_gain,
    w_query,
    key_matrix,
    value_matrix,
    w_out,
    mlp_gain,
    w_gate,
    w_up,
    w_down,
):
    micro, _, slots, width = hidden_in.shape
    size = lax.axis_size("z")
    z, x, y, c = (lax.axis_index(a) for a in ("z", "x", "y", "c"))
    j = y * 2 + c
    own_rows = w_query.shape[0]
    block_rows = 4 * own_rows
    q_cols = w_query.shape[1] // 4
    kv_cols = key_matrix.shape[1] // 4
    qkv_cols = q_cols + 2 * kv_cols
    ff = w_gate.shape[1]
    chunk = ff // (2 * size)
    rows = micro * slots
    group_rows = 4 * rows
    span = 4 * slots
    q_heads = q_cols // HEAD_DIMENSION
    scale = HEAD_DIMENSION ** (-0.5)
    lengths = seq_lengths.reshape(micro)

    def behind(s):
        return lax.rem(z - s + size, size)

    def by_chunk(weight):
        return jnp.swapaxes(weight.reshape(own_rows, 2 * size, chunk), 0, 1)

    def exchange(parts):
        return lax.all_to_all(parts, ("z", "y"), 0, 0, tiled=True)

    offsets = jnp.arange(slots, dtype=jnp.int32)
    own_slots = j * slots + offsets
    live = (own_slots[None, :] < lengths[:, None]).astype(F32).reshape(rows, 1)
    dy = out_grad.astype(F32).reshape(rows, width) * live
    dfb_around = [dy.astype(BF)]
    dfb_around.append(ring(dfb_around[-1], size))

    def beside(values, columns):
        return jnp.pad(values, ((0, 8 - values.shape[0]), (0, columns - values.shape[1])))

    gains = jnp.stack([attn_gain, mlp_gain])

    def head_piece(k):
        to = j ^ k
        weights = jnp.concatenate(
            [
                cut(w_query, to * q_cols, q_cols, 1),
                cut(key_matrix, to * kv_cols, kv_cols, 1),
                cut(value_matrix, to * kv_cols, kv_cols, 1),
                cut(w_out, to * q_cols, q_cols, 1),
            ],
            axis=1,
        )
        return jnp.concatenate([weights, beside(gains, weights.shape[1])], axis=0)

    head_pieces = to_peers_yc(head_piece)

    head_cols = qkv_cols + q_cols
    block = jnp.zeros((4, own_rows, head_cols), BF)
    gain_block = jnp.zeros((4, 2, own_rows), BF)
    for k, piece in enumerate(head_pieces):
        block = put(block, piece[:own_rows], j ^ k)
        gain_block = put(gain_block, piece[own_rows : own_rows + 2, :own_rows], j ^ k)
    gain_block = jnp.swapaxes(gain_block, 0, 1).reshape(2, block_rows)
    block = jnp.concatenate(
        [block.reshape(block_rows, head_cols), beside(gain_block, head_cols)], axis=0
    )

    block, dfb_around[1], hidden_in, w_gate, w_up, w_down = tie(
        block, dfb_around[1], hidden_in, w_gate, w_up, w_down
    )
    tokens = hidden_in.reshape(micro, slots, width)
    around, over = [block], []
    across = [swap(tokens, "y")]
    token_blocks = gather_yc(tokens, across[0])
    for s in range(1, size):
        over.append(swap(around[-1], "x"))
        around.append(ring(around[-1], size))
        around[s], over[s - 1] = tie(around[s], over[s - 1])
        if s < size - 1:
            dfb_around.append(ring(dfb_around[-1], size))
            around[s], dfb_around[s + 1] = tie(around[s], dfb_around[s + 1])
        if s == size - 2:
            around[s], *token_blocks = tie(around[s], *token_blocks)
    dfb_over = swap_in_turn(dfb_around, "y")
    gate_up_local = jnp.concatenate([by_chunk(w_gate), by_chunk(w_up)], axis=2)
    gate_up_local, around[-1], *dfb_over = tie(gate_up_local, around[-1], *dfb_over)
    gate_up_mine = exchange(gate_up_local)
    over.append(swap(around[-1], "x"))
    down_local, gate_up_mine = tie(by_chunk(w_down), gate_up_mine)
    down_mine = exchange(down_local)
    gate_up_over = swap(gate_up_mine, "x")

    wqkv = jnp.zeros((size, 2, block_rows, qkv_cols), BF)
    gains_all = jnp.zeros((size, 2, 2, block_rows), BF)
    wo = jnp.zeros((size, 2, block_rows, q_cols), BF)
    for s in range(size):
        for at, piece in ((x, around[s]), (1 - x, over[s])):
            wqkv = put(wqkv, piece[:block_rows, :qkv_cols], behind(s), at)
            wo = put(wo, piece[:block_rows, qkv_cols:], behind(s), at)
            gains_all = put(gains_all, piece[block_rows : block_rows + 2, :block_rows], behind(s), at)
    wqkv = wqkv.reshape(width, qkv_cols)
    wo = wo.reshape(width, q_cols)
    gain_one = gains_all[:, :, 0].astype(F32).reshape(1, width)
    gain_two = gains_all[:, :, 1].astype(F32).reshape(1, width)

    def put_rows(whole, piece, at):
        piece = piece.reshape(size, 1, 2, 1, own_rows, piece.shape[2])
        whole = lax.dynamic_update_slice(whole, piece, (0, at, 0, c, 0, 0))
        for i in range(0, size, size // 4):
            part = swap(piece[i : i + size // 4], "c")
            whole = lax.dynamic_update_slice(whole, part, (i, at, 0, 1 - c, 0, 0))
        return whole

    def empty_rows(columns):
        return jnp.zeros((size, 2, 2, 2, own_rows, columns), BF)

    positions = jnp.concatenate([(j ^ k) * slots + offsets for k in range(4)])
    cosine, sine = rope_tables(positions, HEAD_DIMENSION)
    cosine, sine = cosine[None, :, None, :], sine[None, :, None, :]
    all_x = jnp.concatenate(token_blocks, axis=1).astype(F32).reshape(group_rows, width)
    all_scale = lax.rsqrt(jnp.mean(all_x * all_x, axis=-1, keepdims=True) + EPS_NORM)
    xn1 = (all_x * all_scale * gain_one).astype(BF)
    qkv = dot(xn1, wqkv)
    q = rotary_embed(
        qkv[:, :q_cols].reshape(micro, span, q_heads, HEAD_DIMENSION), cosine, sine
    ).astype(BF)
    k = rotary_embed(
        qkv[:, q_cols : q_cols + kv_cols].reshape(micro, span, 1, HEAD_DIMENSION), cosine, sine
    ).astype(BF)[:, :, 0]
    v = qkv[:, q_cols + kv_cols :].reshape(micro, span, HEAD_DIMENSION).astype(BF)
    allowed = (positions[None, None, :] <= positions[None, :, None]) & (
        positions[None, None, :] < lengths[:, None, None]
    )
    allowed = allowed[:, None, :, :]
    scores = jnp.einsum("mqgd,msd->mgqs", q, k, preferred_element_type=F32) * scale
    scores = jnp.where(allowed, scores, NEG_FILL)
    top = jnp.max(scores, axis=-1, keepdims=True)
    log_total = top + jnp.log(jnp.sum(jnp.exp(scores - top), axis=-1, keepdims=True))
    probs = jnp.where(allowed, jnp.exp(scores - log_total), 0.0)
    probs_low = probs.astype(BF)
    mixed = (
        jnp.einsum("mgqs,msd->mqgd", probs_low, v, preferred_element_type=F32)
        .astype(BF)
        .reshape(group_rows, q_cols)
    )
    branch_part = dot_right(mixed, wo).astype(BF).reshape(micro, 4, slots, width)
    branch = scatter_yc([branch_part[:, i] for i in range(4)]).reshape(rows, width)

    own_x = tokens.astype(F32).reshape(rows, width)
    first_scale = lax.rsqrt(jnp.mean(own_x * own_x, axis=-1, keepdims=True) + EPS_NORM)
    first_hat = own_x * first_scale
    middle = own_x + branch
    second_scale = lax.rsqrt(jnp.mean(middle * middle, axis=-1, keepdims=True) + EPS_NORM)
    second_hat = middle * second_scale
    second_normalized = (second_hat * gain_two).astype(BF)

    second_normalized, down_mine = tie(second_normalized, down_mine)
    xn2_around = [second_normalized, ring(second_normalized, size)]
    down_mine, gate_up_over = tie(down_mine, gate_up_over)
    down_over = swap(down_mine, "x")
    wgu = put_rows(put_rows(empty_rows(2 * chunk), gate_up_mine, x), gate_up_over, 1 - x)
    wd = put_rows(put_rows(empty_rows(chunk), down_mine, x), down_over, 1 - x)
    for s in range(2, size):
        come = ring(xn2_around[-1], size)
        xn2_around.append(come)
    wgu = wgu.reshape(width, 2 * chunk)
    wd = wd.reshape(width, chunk)
    xn2_blocks = [b for near in xn2_around for b in (near, swap(near, "y"))]
    dfb_blocks = [b for pair in zip(dfb_around, dfb_over) for b in pair]

    halves = []
    for part in (slice(0, -2), slice(-2, None)):
        xn2 = jnp.concatenate(xn2_blocks[part], axis=0)
        dfb = jnp.concatenate(dfb_blocks[part], axis=0)
        if halves:
            xn2, *halves[0] = tie(xn2, *halves[0])
        gate_up = dot(xn2, wgu)
        gate, up = gate_up[:, :chunk], gate_up[:, chunk:]
        sigmoid = jax.nn.sigmoid(gate)
        activated = gate * sigmoid
        hidden = (activated * up).astype(BF)
        dhid = dot(dfb, wd)
        dgu = jnp.concatenate(
            [
                (dhid * up * sigmoid * (1.0 + gate * (1.0 - sigmoid))).astype(BF),
                (dhid * activated).astype(BF),
            ],
            axis=1,
        )
        if halves:
            ahead = halves[0][4].reshape(size - 1, 2, rows, width)[1]
            first_total = (ahead[0].astype(F32) + swap(ahead[1], "y")).astype(BF)
            first_total, dgu = tie(first_total, dgu)
        dxn2_part = dot_right(dgu, wgu).astype(BF)
        halves.append([xn2, dfb, hidden, dgu, dxn2_part])

    def pieces(parts):
        parts = [p.reshape(-1, 2, rows, width) for p in parts]
        return [[p[s, i] for p in parts for s in range(p.shape[0])] for i in range(2)]

    def over_cores(grad, pieces):
        grad = grad.reshape(size, 2, 2, 2, own_rows, grad.shape[1])
        sums = []
        for i in range(0, size, size // pieces):
            part = grad[i : i + size // pieces]
            sums.append((pick(part, c, 3).astype(F32) + swap(pick(part, 1 - c, 3), "c")).astype(BF))
        return jnp.concatenate(sums, axis=0)

    def over_x(grad):
        total = (pick(grad, x, 1).astype(F32) + swap(pick(grad, 1 - x, 1), "x")).astype(BF)
        return total.reshape(2 * size, own_rows, grad.shape[-1])

    (xn2_a, dfb_a, hidden_a, dgu_a, dxn2_a), (xn2_b, dfb_b, hidden_b, dgu_b, dxn2_b) = halves
    own, away = pieces([dxn2_a, dxn2_b])
    order = [(step + 1) % size for step in range(1, size)]
    away[order[0]], first_total = tie(away[order[0]], first_total)
    got = swap_in_turn([away[s] for s in order], "y")
    dxn2_b, hidden_b, dfb_a, xn2_a = tie(dxn2_b, hidden_b, dfb_a, xn2_a)
    down_grad = (dot_rows(dfb_a, hidden_a) + dot_rows(dfb_b, hidden_b)).astype(BF)
    total = first_total
    for step in range(1, size):
        total = own[order[step - 1]].astype(F32) + got[step - 1] + ring(total, size)
        if step < size - 1:
            total = total.astype(BF)
        if step == 1:
            total, down_grad, xn2_a = tie(total, down_grad, xn2_a)
            down_near = over_cores(down_grad, 2)
            gate_up_grad = dot_rows(xn2_a, dgu_a)
        if step == size - 2:
            total, gate_up_grad = tie(total, gate_up_grad)
            gate_up_grad = (gate_up_grad + dot_rows(xn2_b, dgu_b)).astype(BF)
    feed_a, feed_b = dot_right(hidden_a, wd).astype(BF), dot_right(hidden_b, wd).astype(BF)
    down_sum = over_x(down_near)
    dxn2, gate_up_grad, feed_a, feed_b = tie(total, gate_up_grad, feed_a, feed_b)
    gate_up_sum = over_x(over_cores(gate_up_grad, 4))

    dh1 = dy + norm_backward(second_hat, second_scale, dxn2 * gain_two)
    dab_blocks = gather_yc(dh1.astype(BF).reshape(micro, slots, width))
    dab_blocks[2], down_sum = tie(dab_blocks[2], down_sum)
    down_parts = exchange(down_sum)
    dab_blocks[3], feed_a, feed_b = tie(dab_blocks[3], feed_a, feed_b)
    dab = jnp.concatenate(dab_blocks, axis=1).reshape(group_rows, width)

    def blocks_of(*grads):
        grads = [g.reshape(size, 2, block_rows, g.shape[1]) for g in grads]
        at = [[pick(g, behind(s)) for g in grads] for s in range(size)]
        return [
            [jnp.concatenate([pick(g, i) for g in gs], axis=1) for gs in at] for i in (x, 1 - x)
        ]

    out_grad_part = dot_rows(dab, mixed).astype(BF)

    dob = dot(dab, wo).astype(BF)
    dob = dob.reshape(micro, span, q_heads, HEAD_DIMENSION)
    dprob = jnp.einsum("mqgd,msd->mgqs", dob, v, preferred_element_type=F32)
    dscore = (probs * (dprob - jnp.sum(probs * dprob, axis=-1, keepdims=True))).astype(BF)
    dq = jnp.einsum("mgqs,msd->mqgd", dscore, k, preferred_element_type=F32) * scale
    dk = jnp.einsum("mgqs,mqgd->msd", dscore, q, preferred_element_type=F32) * scale
    dv = jnp.einsum("mgqs,mqgd->msd", probs_low, dob, preferred_element_type=F32)
    dq = rotary_backward(dq, cosine, sine).astype(BF).reshape(group_rows, q_cols)
    dk = rotary_backward(dk[:, :, None, :], cosine, sine).astype(BF).reshape(group_rows, kv_cols)
    dqkv = jnp.concatenate([dq, dk, dv.astype(BF).reshape(group_rows, kv_cols)], axis=1)

    dqkv, gate_up_sum = tie(dqkv, gate_up_sum)
    gate_up_parts = exchange(gate_up_sum)
    feed = scatter_z(*pieces([feed_a, feed_b]), "y", size)
    outputs = (live * (middle + feed)).astype(BF)
    head_ties = {size - 2: [outputs]}
    head_sum = scatter_z(
        *blocks_of(dot_rows(xn1, dqkv).astype(BF), out_grad_part), "x", size, head_ties
    )
    (outputs,) = head_ties[size - 2]
    outputs = outputs.reshape(hidden_in.shape)

    dxn1_part = dot_right(dqkv, wqkv).astype(BF).reshape(micro, 4, slots, width)
    dxn1 = scatter_yc([dxn1_part[:, i] for i in range(4)]).reshape(rows, width)
    input_grads = (
        (dh1 + norm_backward(first_hat, first_scale, dxn1 * gain_one))
        .astype(BF)
        .reshape(hidden_in.shape)
    )

    def owned(block):
        block = block.astype(BF)
        came = to_peers_yc(lambda k: cut(block, (j ^ k) * own_rows, own_rows, 0))
        heads = jnp.zeros((4, own_rows, block.shape[1]), BF)
        for k in range(4):
            heads = put(heads, came[k], j ^ k)
        return heads

    def side_by_side(parts, start, count):
        return jnp.concatenate(
            [parts[i, :, start : start + count] for i in range(parts.shape[0])], axis=1
        ).astype(F32)

    heads = owned(head_sum)
    grad_query = side_by_side(heads, 0, q_cols)
    grad_key = side_by_side(heads, q_cols, kv_cols)
    grad_value = side_by_side(heads, q_cols + kv_cols, kv_cols)
    grad_out = side_by_side(heads, qkv_cols, q_cols)
    grad_gate = side_by_side(gate_up_parts, 0, chunk)
    grad_up = side_by_side(gate_up_parts, chunk, chunk)
    grad_down = side_by_side(down_parts, 0, chunk)

    def gain_gradient(gain, *pairs):
        total = sum(jnp.sum(w.astype(F32) * g, axis=1) for w, g in pairs)
        return total / gain.astype(F32)

    grad_attn_gain = gain_gradient(
        attn_gain, (w_query, grad_query), (key_matrix, grad_key), (value_matrix, grad_value)
    )
    grad_mlp_gain = gain_gradient(mlp_gain, (w_gate, grad_gate), (w_up, grad_up))
    return (
        outputs,
        input_grads,
        grad_attn_gain,
        grad_query,
        grad_key,
        grad_value,
        grad_out,
        grad_mlp_gain,
        grad_gate,
        grad_up,
        grad_down,
    )


def solution(mesh):
    dp, fsdp = mesh.shape["dp"], mesh.shape["fsdp"]
    fine = Mesh(mesh.devices.reshape(dp // 2, 2, fsdp // 2, 2), ("z", "x", "y", "c"))
    batch, slot, both = ("z", "x"), ("y", "c"), ("z", "x", "y", "c")
    vector, matrix = P(both), P(both, None)
    rows = P(None, batch, slot, None)
    return jax.shard_map(
        per_device,
        mesh=fine,
        in_specs=(rows, P(None, batch), rows) + (vector,) + (matrix,) * 4 + (vector,) + (matrix,) * 3,
        out_specs=(rows, rows, vector) + (matrix,) * 4 + (vector,) + (matrix,) * 3,
        check_vma=False,
    )
```

time: 951 us -> 641 us (0.67); the launches traced: 932 us -> 632 us
  local copies, waits for them, and re-layouts: 252 us -> 113 us
  waiting for transfers between devices: 392 us -> 268 us
  starting transfers between devices: 147 us -> 84.1 us
  other arithmetic: 55.4 us -> 69.4 us
  matrix products: 81.5 us -> 94.8 us
    dynamic_update_slice x122 -> x35, local copies, waits for them, and re-layouts: 116 us -> 30.7 us  [put(): return lax.dynamic_update_slice(buffer, piece, starts)]
    ppermute x43 -> x6, waiting for transfers between devices: 109 us -> 35.1 us  [to_peers_yc(): lax.ppermute(piece_for(k), ('y', 'c'), [(i, i ^ k) for i in range(4)])]
    ppermute x107 -> x70, waiting for transfers between devices: 168 us -> 110 us  [swap(): return lax.ppermute(value, axis, [(0, 1), (1, 0)])]
    ppermute x43 -> x6, starting transfers between devices: 51.7 us -> 3.94 us  [to_peers_yc(): lax.ppermute(piece_for(k), ('y', 'c'), [(i, i ^ k) for i in range(4)])]
    ppermute x107 -> x70, starting transfers between devices: 78 us -> 45.1 us  [swap(): return lax.ppermute(value, axis, [(0, 1), (1, 0)])]
    unnamed x229 -> x226, local copies, waits for them, and re-layouts: 55.2 us -> 24.5 us
    all_to_all x0 -> x4, starting transfers between devices: none -> 24.5 us  [exchange(): return lax.all_to_all(parts, ('z', 'y'), 0, 0, tiled=True)]
    dynamic_slice x11 -> x3, local copies, waits for them, and re-layouts: 23.7 us -> 2.06 us  [cut(): return lax.dynamic_slice_in_dim(value, start, count, axis)]
  transfers between devices with their start and end apart: 180 -> 98, of which waited for: 80 -> 40; matrix products, arithmetic and copies ran while one was open for 31% -> 37% of each run, Pallas kernels for 0% -> 0%
where the time goes in v2:
time: 641 us; the launch traced here: 632 us
  waiting for transfers between devices  268 us (42%)
  local copies, waits for them, and re-layouts  113 us (18%)
  matrix products  94.8 us (15%)
  starting transfers between devices  84.1 us (13%)
  other arithmetic  69.4 us (11%)
    ppermute x70, waiting for transfers between devices, swap(): return lax.ppermute(value, axis, [(0, 1), (1, 0)])  110 us
    ppermute x18, waiting for transfers between devices, ring(): return lax.ppermute(value, 'z', [(i, (i + 1) % size) for i in range(size)])  101 us
    ppermute x70, starting transfers between devices, swap(): return lax.ppermute(value, axis, [(0, 1), (1, 0)])  45.1 us
    ppermute x6, waiting for transfers between devices, to_peers_yc(): lax.ppermute(piece_for(k), ('y', 'c'), [(i, i ^ k) for i in range(4)])  35.1 us
    dot_general x6, matrix products, dot_rows(): lax.dot_general(left, right, (((0,), (0,)), ((), ())), preferred_element_...  34.6 us
    dynamic_update_slice x35, local copies, waits for them, and re-layouts, put(): return lax.dynamic_update_slice(buffer, piece, starts)  30.7 us
    dot_general x6, matrix products, dot(): return jnp.dot(left, right, preferred_element_type=F32)  30.4 us
    dot_general x6, matrix products, dot_right(): lax.dot_general(left, right, (((1,), (1,)), ((), ())), preferred_element_...  27.6 us
  transfers between devices with their start and end apart: 98, of which 40 were waited for; matrix products, arithmetic and copies ran while one was open for 37% of the time, Pallas kernels for 0%

profile of v2, /device:TPU:0, one launch (start us, length us, event | category | flops | bytes accessed | tf_op | source)
XLA Modules:
  0.0 632.0 jit_solution(12519845679822057162)
XLA Ops:
  15.7 10.9 %collective-permute-done.1 = bf16[72,1536]{1,0:T(8,128)(2,1)} collective-permute-done((bf16[72,1536]{1,0:T(8,128)(2,1)S(1)}, bf16[72,1536]{1,0:T(8,128)(2,1)}, u32[]{:S(2)}, u32[]{:S(2)}) %collective-permute-start.1) | collective-permute-done | bytes 221216 | tf_op jit(solution)/shard_map/ppermute | solution.py:105
  62.9 8.3 %collective-permute-done.6 = bf16[128,2048]{1,0:T(8,128)(2,1)} collective-permute-done((bf16[128,2048]{1,0:T(8,128)(2,1)}, bf16[128,2048]{1,0:T(8,128)(2,1)}, u32[]{:S(2)}, u32[]{:S(2)}) %collective-permute-start.6) | collective-permute-done | bytes 524320 | tf_op jit(solution)/shard_map/ppermute | solution.py:64
  83.0 11.2 %collective-permute-done.7 = bf16[264,1536]{1,0:T(8,128)(2,1)S(1)} collective-permute-done((bf16[264,1536]{1,0:T(8,128)(2,1)}, bf16[264,1536]{1,0:T(8,128)(2,1)S(1)}, u32[]{:S(2)}, u32[]{:S(2)}) %collective-permute-start.7) | collective-permute-done | bytes 811040 | tf_op jit(solution)/shard_map/ppermute | solution.py:64
  94.2 10.0 %collective-permute-done.9 = bf16[128,2048]{1,0:T(8,128)(2,1)S(1)} collective-permute-done((bf16[128,2048]{1,0:T(8,128)(2,1)}, bf16[128,2048]{1,0:T(8,128)(2,1)S(1)}, u32[]{:S(2)}, u32[]{:S(2)}) %collective-permute-start.9) | collective-permute-done | bytes 524320 | tf_op jit(solution)/shard_map/ppermute | solution.py:64
  115.6 9.3 %collective-permute-done.15 = bf16[264,1536]{1,0:T(8,128)(2,1)} collective-permute-done((bf16[264,1536]{1,0:T(8,128)(2,1)S(1)}, bf16[264,1536]{1,0:T(8,128)(2,1)}, u32[]{:S(2)}, u32[]{:S(2)}) %collective-permute-start.15) | collective-permute-done | bytes 811040 | tf_op jit(solution)/shard_map/ppermute | solution.py:64
  170.5 13.2 %collective-permute-done.26 = bf16[2,64,2048]{2,1,0:T(8,128)(2,1)S(1)} collective-permute-done((bf16[2,64,2048]{2,1,0:T(8,128)(2,1)S(1)}, bf16[2,64,2048]{2,1,0:T(8,128)(2,1)S(1)}, u32[]{:S(2)}, u32[]{:S(2)}) %collective-permute-start.26) | collective-permute-done | bytes 524320 | tf_op jit(solution)/shard_map/ppermute | solution.py:60
  185.8 8.2 %all-to-all-start.1 = ((bf16[8,64,1024]{2,1,0:T(8,128)(2,1)}), bf16[8,64,1024]{2,1,0:T(8,128)(2,1)S(1)}, u32[]{:S(2)}, u32[]{:S(2)}) async-start(bf16[8,64,1024]{2,1,0:T(8,128)(2,1)} %copy.139), calls=%async_computation.1 | async-start | bytes 2097152 | tf_op jit(solution)/shard_map/all_to_all | solution.py:171
  209.4 10.4 %all-to-all-done.1 = bf16[8,64,1024]{2,1,0:T(8,128)(2,1)S(1)} async-done(((bf16[8,64,1024]{2,1,0:T(8,128)(2,1)}), bf16[8,64,1024]{2,1,0:T(8,128)(2,1)S(1)}, u32[]{:S(2)}, u32[]{:S(2)}) %all-to-all-start.1) | async-done | bytes 1048608 | tf_op jit(solution)/shard_map/all_to_all | solution.py:171
  221.2 20.2 %collective-permute-done.38 = bf16[8,64,2048]{2,1,0:T(8,128)(2,1)} collective-permute-done((bf16[8,64,2048]{2,1,0:T(8,128)(2,1)}, bf16[8,64,2048]{2,1,0:T(8,128)(2,1)}, u32[]{:S(2)}, u32[]{:S(2)}) %collective-permute-start.38) | collective-permute-done | bytes 2097184 | tf_op jit(solution)/shard_map/ppermute | solution.py:60
  258.5 11.6 %collective-permute-done.28 = bf16[128,2048]{1,0:T(8,128)(2,1)S(1)} collective-permute-done((bf16[128,2048]{1,0:T(8,128)(2,1)S(1)}, bf16[128,2048]{1,0:T(8,128)(2,1)S(1)}, u32[]{:S(2)}, u32[]{:S(2)}) %collective-permute-start.28) | collective-permute-done | bytes 524320 | tf_op jit(solution)/shard_map/ppermute | solution.py:64
  273.6 9.3 %collective-permute-done.33 = bf16[128,2048]{1,0:T(8,128)(2,1)S(1)} collective-permute-done((bf16[128,2048]{1,0:T(8,128)(2,1)S(1)}, bf16[128,2048]{1,0:T(8,128)(2,1)S(1)}, u32[]{:S(2)}, u32[]{:S(2)}) %collective-permute-start.33) | collective-permute-done | bytes 524320 | tf_op jit(solution)/shard_map/ppermute | solution.py:60
  283.0 10.9 %fusion.113 = f32[768,2048]{1,0:T(8,128)S(1)} fusion(bf16[768,2048]{1,0:T(8,128)(2,1)S(1)} %constant_dynamic-update-slice_fusion, bf16[2048,2048]{1,0:T(8,128)(2,1)} %bitcast.95), kind=kOutput, calls=%fused_computation.438 | convolution fusion | flops 6442450944 | bytes 17825792 | tf_op jit(solution)/shard_map/dot_general | solution.py:48
  299.0 9.3 %convolution_convert_fusion.1 = bf16[768,2048]{1,0:T(8,128)(2,1)S(1)} fusion(bf16[2048,2048]{1,0:T(8,128)(2,1)} %bitcast.95, bf16[768,1024]{1,0:T(8,128)(2,1)S(1)} %get-tuple-element.246, bf16[768,1024]{1,0:T(8,128)(2,1)S(1)} %get-tuple-element.245), kind=kOutput, calls=%fused_computation.11 | convolution fusion | flops 6450315264 | bytes 14680064 | tf_op jit(solution)/shard_map/dot_general | solution.py:52
  354.2 10.6 %fusion.116 = f32[2048,2048]{1,0:T(8,128)} fusion(bf16[768,2048]{1,0:T(8,128)(2,1)S(1)} %copy-done.81, bf16[768,2048]{1,0:T(8,128)(2,1)S(1)} %copy-done.29), kind=kOutput, calls=%fused_computation.441 | convolution fusion | flops 6442450944 | bytes 23068672 | tf_op jit(solution)/shard_map/dot_general | solution.py:56
  371.1 11.5 %add_convert_fusion = bf16[2048,2048]{1,0:T(8,128)(2,1)} fusion(f32[2048,2048]{1,0:T(8,128)} %fusion.116, bf16[256,2048]{1,0:T(8,128)(2,1)S(1)} %pad_maximum_fusion.4, bf16[256,2048]{1,0:T(8,128)(2,1)S(1)} %pad_maximum_fusion.5), kind=kOutput, calls=%fused_computation | convolution fusion | flops 2155872256 | bytes 27262976 | tf_op jit(solution)/shard_map/dot_general | solution.py:56
  446.9 8.6 %collective-permute-done.78 = bf16[128,2048]{1,0:T(8,128)(2,1)S(1)} collective-permute-done((bf16[128,2048]{1,0:T(8,128)(2,1)S(1)}, bf16[128,2048]{1,0:T(8,128)(2,1)S(1)}, u32[]{:S(2)}, u32[]{:S(2)}) %collective-permute-start.78) | collective-permute-done | bytes 524320 | tf_op jit(solution)/shard_map/ppermute | solution.py:60
  494.8 15.1 %collective-permute-done.72 = bf16[256,1536]{1,0:T(8,128)(2,1)S(1)} collective-permute-done((bf16[256,1536]{1,0:T(8,128)(2,1)S(1)}, bf16[256,1536]{1,0:T(8,128)(2,1)S(1)}, u32[]{:S(2)}, u32[]{:S(2)}) %collective-permute-start.72) | collective-permute-done | bytes 786464 | tf_op jit(solution)/shard_map/ppermute | solution.py:60
  516.1 12.4 %collective-permute-done.73 = bf16[256,1536]{1,0:T(8,128)(2,1)S(1)} collective-permute-done((bf16[256,1536]{1,0:T(8,128)(2,1)S(1)}, bf16[256,1536]{1,0:T(8,128)(2,1)S(1)}, u32[]{:S(2)}, u32[]{:S(2)}) %collective-permute-start.73) | collective-permute-done | bytes 786464 | tf_op jit(solution)/shard_map/ppermute | solution.py:60
  534.5 10.0 %collective-permute-done.83 = bf16[128,2048]{1,0:T(8,128)(2,1)} collective-permute-done((bf16[128,2048]{1,0:T(8,128)(2,1)}, bf16[128,2048]{1,0:T(8,128)(2,1)}, u32[]{:S(2)}, u32[]{:S(2)}) %collective-permute-start.83) | collective-permute-done | bytes 524320 | tf_op jit(solution)/shard_map/ppermute | solution.py:64
  547.7 11.6 %collective-permute-done.76 = bf16[256,1536]{1,0:T(8,128)(2,1)} collective-permute-done((bf16[256,1536]{1,0:T(8,128)(2,1)}, bf16[256,1536]{1,0:T(8,128)(2,1)}, u32[]{:S(2)}, u32[]{:S(2)}) %collective-permute-start.76) | collective-permute-done | bytes 786464 | tf_op jit(solution)/shard_map/ppermute | solution.py:64
  574.6 10.0 %collective-permute-done.90 = bf16[256,1536]{1,0:T(8,128)(2,1)} collective-permute-done((bf16[256,1536]{1,0:T(8,128)(2,1)}, bf16[256,1536]{1,0:T(8,128)(2,1)}, u32[]{:S(2)}, u32[]{:S(2)}) %collective-permute-start.90) | collective-permute-done | bytes 786464 | tf_op jit(solution)/shard_map/ppermute | solution.py:64
  588.6 10.0 %collective-permute-done.92 = bf16[64,1536]{1,0:T(8,128)(2,1)S(1)} collective-permute-done((bf16[64,1536]{1,0:T(8,128)(2,1)S(1)}, bf16[64,1536]{1,0:T(8,128)(2,1)S(1)}, u32[]{:S(2)}, u32[]{:S(2)}) %collective-permute-start.92) | collective-permute-done | bytes 196640 | tf_op jit(solution)/shard_map/ppermute | solution.py:105
  598.6 12.6 %collective-permute-done.93 = bf16[64,1536]{1,0:T(8,128)(2,1)S(1)} collective-permute-done((bf16[64,1536]{1,0:T(8,128)(2,1)S(1)}, bf16[64,1536]{1,0:T(8,128)(2,1)S(1)}, u32[]{:S(2)}, u32[]{:S(2)}) %collective-permute-start.93) | collective-permute-done | bytes 196640 | tf_op jit(solution)/shard_map/ppermute | solution.py:105
  615.4 11.0 %all-to-all-done.2 = bf16[8,64,2048]{2,1,0:T(8,128)(2,1)S(1)} async-done(((bf16[8,64,2048]{2,1,0:T(8,128)(2,1)}), bf16[8,64,2048]{2,1,0:T(8,128)(2,1)S(1)}, u32[]{:S(2)}, u32[]{:S(2)}) %all-to-all-start.2) | async-done | bytes 2097184 | tf_op jit(solution)/shard_map/all_to_all | solution.py:171
  (630 shorter events, 362.7 us)
Async XLA Ops:
  3.7 29.8 %collective-permute-start.3 = (bf16[128,2048]{1,0:T(8,128)(2,1)}, bf16[128,2048]{1,0:T(8,128)(2,1)}, u32[]{:S(2)}, u32[]{:S(2)}) collective-permute-start(bf16[128,2048]{1,0:T(8,128)(2,1)} %get-tuple-element.385), channel_id=1, source_target_pairs={{0,8},{8,16},{16,24},{24,0},{1,9},{9,17},{17,25},{25,1},{2,10},{10... | collective-permute-start | bytes 1572872 | tf_op jit(solution)/shard_map/ppermute | solution.py:64
  6.7 48.0 %collective-permute-start.17 = (bf16[128,2048]{1,0:T(8,128)(2,1)}, bf16[128,2048]{1,0:T(8,128)(2,1)}, u32[]{:S(2)}, u32[]{:S(2)}) collective-permute-start(bf16[128,2048]{1,0:T(8,128)(2,1)} %get-tuple-element.385), channel_id=1, source_target_pairs={{0,2},{2,0},{1,3},{3,1},{4,6},{6,4},{5,7},{7,5},{8,10},{10,8},{9,1... | collective-permute-start | bytes 1572872 | tf_op jit(solution)/shard_map/ppermute | solution.py:60
  33.5 29.3 %collective-permute-start.4 = (bf16[264,1536]{1,0:T(8,128)(2,1)}, bf16[264,1536]{1,0:T(8,128)(2,1)}, u32[]{:S(2)}, u32[]{:S(2)}) collective-permute-start(bf16[264,1536]{1,0:T(8,128)(2,1)} %fusion.54), channel_id=1, source_target_pairs={{0,8},{8,16},{16,24},{24,0},{1,9},{9,17},{17,25},{25,1},{2,10},{10... | collective-permute-start | bytes 2433032 | tf_op jit(solution)/shard_map/ppermute | solution.py:64
  35.1 27.8 %collective-permute-start.5 = (bf16[264,1536]{1,0:T(8,128)(2,1)}, bf16[264,1536]{1,0:T(8,128)(2,1)}, u32[]{:S(2)}, u32[]{:S(2)}) collective-permute-start(bf16[264,1536]{1,0:T(8,128)(2,1)} %fusion.54), channel_id=1, source_target_pairs={{0,4},{4,0},{1,5},{5,1},{2,6},{6,2},{3,7},{7,3},{8,12},{12,8},{9,1... | collective-permute-start | bytes 2433032 | tf_op jit(solution)/shard_map/ppermute | solution.py:60
  71.7 32.4 %collective-permute-start.9 = (bf16[128,2048]{1,0:T(8,128)(2,1)}, bf16[128,2048]{1,0:T(8,128)(2,1)S(1)}, u32[]{:S(2)}, u32[]{:S(2)}) collective-permute-start(bf16[128,2048]{1,0:T(8,128)(2,1)} %collective-permute-done.6), channel_id=1, source_target_pairs={{0,8},{8,16},{16,24},{24,0},{1,9},{9,17},{17,25},{25,1},{2,10},{10... | collective-permute-start | bytes 1572872 | tf_op jit(solution)/shard_map/ppermute | solution.py:64
  75.1 31.8 %collective-permute-start.19 = (bf16[128,2048]{1,0:T(8,128)(2,1)}, bf16[128,2048]{1,0:T(8,128)(2,1)}, u32[]{:S(2)}, u32[]{:S(2)}) collective-permute-start(bf16[128,2048]{1,0:T(8,128)(2,1)} %collective-permute-done.6), channel_id=1, source_target_pairs={{0,2},{2,0},{1,3},{3,1},{4,6},{6,4},{5,7},{7,5},{8,10},{10,8},{9,1... | collective-permute-start | bytes 1572872 | tf_op jit(solution)/shard_map/ppermute | solution.py:60
  132.2 52.1 %all-to-all-start = ((bf16[8,64,2048]{2,1,0:T(8,128)(2,1)}), bf16[8,64,2048]{2,1,0:T(8,128)(2,1)}, u32[]{:S(2)}, u32[]{:S(2)}) async-start(bf16[8,64,2048]{2,1,0:T(8,128)(2,1)} %copy.138), calls=%async_computation | async-start | bytes 4194304 | tf_op jit(solution)/shard_map/all_to_all | solution.py:171
  185.8 33.9 %all-to-all-start.1 = ((bf16[8,64,1024]{2,1,0:T(8,128)(2,1)}), bf16[8,64,1024]{2,1,0:T(8,128)(2,1)S(1)}, u32[]{:S(2)}, u32[]{:S(2)}) async-start(bf16[8,64,1024]{2,1,0:T(8,128)(2,1)} %copy.139), calls=%async_computation.1 | async-start | bytes 2097152 | tf_op jit(solution)/shard_map/all_to_all | solution.py:171
  194.0 47.4 %collective-permute-start.38 = (bf16[8,64,2048]{2,1,0:T(8,128)(2,1)}, bf16[8,64,2048]{2,1,0:T(8,128)(2,1)}, u32[]{:S(2)}, u32[]{:S(2)}) collective-permute-start(bf16[8,64,2048]{2,1,0:T(8,128)(2,1)} %all-to-all-done), channel_id=1, source_target_pairs={{0,4},{4,0},{1,5},{5,1},{2,6},{6,2},{3,7},{7,3},{8,12},{12,8},{9,1... | collective-permute-start | bytes 6291464 | tf_op jit(solution)/shard_map/ppermute | solution.py:60
  219.8 29.3 %collective-permute-start.31 = (bf16[128,2048]{1,0:T(8,128)(2,1)S(1)}, bf16[128,2048]{1,0:T(8,128)(2,1)S(1)}, u32[]{:S(2)}, u32[]{:S(2)}) collective-permute-start(bf16[128,2048]{1,0:T(8,128)(2,1)S(1)} %multiply_convert_fusion.8), channel_id=1, source_target_pairs={{0,2},{2,0},{1,3},{3,1},{4,6},{6,4},{5,7},{7,5},{8,10},{10,8},{9,1... | collective-permute-start | bytes 1572872 | tf_op jit(solution)/shard_map/ppermute | solution.py:60
  221.2 29.7 %collective-permute-start.27 = (bf16[128,2048]{1,0:T(8,128)(2,1)S(1)}, bf16[128,2048]{1,0:T(8,128)(2,1)S(1)}, u32[]{:S(2)}, u32[]{:S(2)}) collective-permute-start(bf16[128,2048]{1,0:T(8,128)(2,1)S(1)} %multiply_convert_fusion.8), channel_id=1, source_target_pairs={{0,8},{8,16},{16,24},{24,0},{1,9},{9,17},{17,25},{25,1},{2,10},{10... | collective-permute-start | bytes 1572872 | tf_op jit(solution)/shard_map/ppermute | solution.py:64
  241.5 28.9 %collective-permute-start.47 = (bf16[8,64,1024]{2,1,0:T(8,128)(2,1)S(1)}, bf16[8,64,1024]{2,1,0:T(8,128)(2,1)S(1)}, u32[]{:S(2)}, u32[]{:S(2)}) collective-permute-start(bf16[8,64,1024]{2,1,0:T(8,128)(2,1)S(1)} %all-to-all-done.1), channel_id=1, source_target_pairs={{0,4},{4,0},{1,5},{5,1},{2,6},{6,2},{3,7},{7,3},{8,12},{12,8},{9,1... | collective-permute-start | bytes 3145736 | tf_op jit(solution)/shard_map/ppermute | solution.py:60
  270.3 28.3 %collective-permute-start.29 = (bf16[128,2048]{1,0:T(8,128)(2,1)S(1)}, bf16[128,2048]{1,0:T(8,128)(2,1)S(1)}, u32[]{:S(2)}, u32[]{:S(2)}) collective-permute-start(bf16[128,2048]{1,0:T(8,128)(2,1)S(1)} %collective-permute-done.28), channel_id=1, source_target_pairs={{0,8},{8,16},{16,24},{24,0},{1,9},{9,17},{17,25},{25,1},{2,10},{10... | collective-permute-start | bytes 1572872 | tf_op jit(solution)/shard_map/ppermute | solution.py:64
  351.8 30.7 %collective-permute-start.63 = (bf16[2,2,2,64,1024]{4,3,2,1,0:T(8,128)(2,1)S(1)}, bf16[2,2,2,64,1024]{4,3,2,1,0:T(8,128)(2,1)}, u32[]{:S(2)}, u32[]{:S(2)}) collective-permute-start(bf16[2,2,2,64,1024]{4,3,2,1,0:T(8,128)(2,1)S(1)} %dynamic-slice_bitcast_fusion.5), channel_id=1, source_target_pairs={{0,1},{1,0},{2,3},{3,2},{4,5},{5,4},{6,7},{7,6},{8,9},{9,8},{10,11... | collective-permute-start | bytes 3145736 | tf_op jit(solution)/shard_map/ppermute | solution.py:60
  352.0 32.2 %collective-permute-start.62 = (bf16[2,2,2,64,1024]{4,3,2,1,0:T(8,128)(2,1)S(1)}, bf16[2,2,2,64,1024]{4,3,2,1,0:T(8,128)(2,1)}, u32[]{:S(2)}, u32[]{:S(2)}) collective-permute-start(bf16[2,2,2,64,1024]{4,3,2,1,0:T(8,128)(2,1)S(1)} %dynamic-slice_bitcast_fusion.6), channel_id=1, source_target_pairs={{0,1},{1,0},{2,3},{3,2},{4,5},{5,4},{6,7},{7,6},{8,9},{9,8},{10,11... | collective-permute-start | bytes 3145736 | tf_op jit(solution)/shard_map/ppermute | solution.py:60
  386.2 23.8 %collective-permute-start.64 = (bf16[4,2,64,1024]{3,2,1,0:T(8,128)(2,1)S(1)}, bf16[4,2,64,1024]{3,2,1,0:T(8,128)(2,1)S(1)}, u32[]{:S(2)}, u32[]{:S(2)}) collective-permute-start(bf16[4,2,64,1024]{3,2,1,0:T(8,128)(2,1)S(1)} %fusion.24), channel_id=1, source_target_pairs={{0,4},{4,0},{1,5},{5,1},{2,6},{6,2},{3,7},{7,3},{8,12},{12,8},{9,1... | collective-permute-start | bytes 3145736 | tf_op jit(solution)/shard_map/ppermute | solution.py:60
  393.3 23.4 %collective-permute-start.67 = (bf16[1,2,2,64,2048]{4,3,2,1,0:T(8,128)(2,1)}, bf16[1,2,2,64,2048]{4,3,2,1,0:T(8,128)(2,1)}, u32[]{:S(2)}, u32[]{:S(2)}) collective-permute-start(bf16[1,2,2,64,2048]{4,3,2,1,0:T(8,128)(2,1)} %dynamic-slice_bitcast_fusion.4), channel_id=1, source_target_pairs={{0,1},{1,0},{2,3},{3,2},{4,5},{5,4},{6,7},{7,6},{8,9},{9,8},{10,11... | collective-permute-start | bytes 3145736 | tf_op jit(solution)/shard_map/ppermute | solution.py:60
  394.9 24.1 %collective-permute-start.68 = (bf16[1,2,2,64,2048]{4,3,2,1,0:T(8,128)(2,1)}, bf16[1,2,2,64,2048]{4,3,2,1,0:T(8,128)(2,1)}, u32[]{:S(2)}, u32[]{:S(2)}) collective-permute-start(bf16[1,2,2,64,2048]{4,3,2,1,0:T(8,128)(2,1)} %dynamic-slice_bitcast_fusion.3), channel_id=1, source_target_pairs={{0,1},{1,0},{2,3},{3,2},{4,5},{5,4},{6,7},{7,6},{8,9},{9,8},{10,11... | collective-permute-start | bytes 3145736 | tf_op jit(solution)/shard_map/ppermute | solution.py:60
  411.4 64.4 %all-to-all-start.3 = ((bf16[8,64,1024]{2,1,0:T(8,128)(2,1)}), bf16[8,64,1024]{2,1,0:T(8,128)(2,1)}, u32[]{:S(2)}, u32[]{:S(2)}) async-start(bf16[8,64,1024]{2,1,0:T(8,128)(2,1)} %bitcast.130), calls=%async_computation.3 | async-start | bytes 2097152 | tf_op jit(solution)/shard_map/all_to_all | solution.py:171
  428.0 50.6 %collective-permute-start.71 = (bf16[4,2,64,2048]{3,2,1,0:T(8,128)(2,1)}, bf16[4,2,64,2048]{3,2,1,0:T(8,128)(2,1)}, u32[]{:S(2)}, u32[]{:S(2)}) collective-permute-start(bf16[4,2,64,2048]{3,2,1,0:T(8,128)(2,1)} %dynamic-slice_bitcast_fusion), channel_id=1, source_target_pairs={{0,4},{4,0},{1,5},{5,1},{2,6},{6,2},{3,7},{7,3},{8,12},{12,8},{9,1... | collective-permute-start | bytes 6291464 | tf_op jit(solution)/shard_map/ppermute | solution.py:60
  512.9 31.7 %collective-permute-start.83 = (bf16[128,2048]{1,0:T(8,128)(2,1)}, bf16[128,2048]{1,0:T(8,128)(2,1)}, u32[]{:S(2)}, u32[]{:S(2)}) collective-permute-start(bf16[128,2048]{1,0:T(8,128)(2,1)} %fusion.33), channel_id=1, source_target_pairs={{0,8},{8,16},{16,24},{24,0},{1,9},{9,17},{17,25},{25,1},{2,10},{10... | collective-permute-start | bytes 1572872 | tf_op jit(solution)/shard_map/ppermute | solution.py:64
  513.7 30.9 %collective-permute-start.80 = (bf16[128,2048]{1,0:T(8,128)(2,1)}, bf16[128,2048]{1,0:T(8,128)(2,1)}, u32[]{:S(2)}, u32[]{:S(2)}) collective-permute-start(bf16[128,2048]{1,0:T(8,128)(2,1)} %get-tuple-element.174), channel_id=1, source_target_pairs={{0,2},{2,0},{1,3},{3,1},{4,6},{6,4},{5,7},{7,5},{8,10},{10,8},{9,1... | collective-permute-start | bytes 1572872 | tf_op jit(solution)/shard_map/ppermute | solution.py:60
  534.4 24.9 %collective-permute-start.76 = (bf16[256,1536]{1,0:T(8,128)(2,1)}, bf16[256,1536]{1,0:T(8,128)(2,1)}, u32[]{:S(2)}, u32[]{:S(2)}) collective-permute-start(bf16[256,1536]{1,0:T(8,128)(2,1)} %add_convert_fusion.4), channel_id=1, source_target_pairs={{0,8},{8,16},{16,24},{24,0},{1,9},{9,17},{17,25},{25,1},{2,10},{10... | collective-permute-start | bytes 2359304 | tf_op jit(solution)/shard_map/ppermute | solution.py:64
  568.2 58.1 %all-to-all-start.2 = ((bf16[8,64,2048]{2,1,0:T(8,128)(2,1)}), bf16[8,64,2048]{2,1,0:T(8,128)(2,1)S(1)}, u32[]{:S(2)}, u32[]{:S(2)}) async-start(bf16[8,64,2048]{2,1,0:T(8,128)(2,1)} %bitcast.160), calls=%async_computation.2 | async-start | bytes 4194304 | tf_op jit(solution)/shard_map/all_to_all | solution.py:171
  (173 other events, 2385.2 us)

commit v3 on v2

--- a/solution.py
+++ b/solution.py
@@ -229,8 +229,6 @@
     gate_up_local, around[-1], *dfb_over = tie(gate_up_local, around[-1], *dfb_over)
     gate_up_mine = exchange(gate_up_local)
     over.append(swap(around[-1], "x"))
-    down_local, gate_up_mine = tie(by_chunk(w_down), gate_up_mine)
-    down_mine = exchange(down_local)
     gate_up_over = swap(gate_up_mine, "x")
 
     wqkv = jnp.zeros((size, 2, block_rows, qkv_cols), BF)
@@ -297,15 +295,19 @@
     second_hat = middle * second_scale
     second_normalized = (second_hat * gain_two).astype(BF)
 
-    second_normalized, down_mine = tie(second_normalized, down_mine)
+    second_normalized, gate_up_mine, down_local = tie(
+        second_normalized, gate_up_mine, by_chunk(w_down)
+    )
+    second_normalized, down_mine = tie(second_normalized, exchange(down_local))
     xn2_around = [second_normalized, ring(second_normalized, size)]
-    down_mine, gate_up_over = tie(down_mine, gate_up_over)
+    for s in range(2, size):
+        come = ring(xn2_around[-1], size)
+        if s == 2:
+            come, gate_up_over, down_mine = tie(come, gate_up_over, down_mine)
+        xn2_around.append(come)
     down_over = swap(down_mine, "x")
     wgu = put_rows(put_rows(empty_rows(2 * chunk), gate_up_mine, x), gate_up_over, 1 - x)
     wd = put_rows(put_rows(empty_rows(chunk), down_mine, x), down_over, 1 - x)
-    for s in range(2, size):
-        come = ring(xn2_around[-1], size)
-        xn2_around.append(come)
     wgu = wgu.reshape(width, 2 * chunk)
     wd = wd.reshape(width, chunk)
     xn2_blocks = [b for near in xn2_around for b in (near, swap(near, "y"))]
@@ -375,11 +377,12 @@
     feed_a, feed_b = dot_right(hidden_a, wd).astype(BF), dot_right(hidden_b, wd).astype(BF)
     down_sum = over_x(down_near)
     dxn2, gate_up_grad, feed_a, feed_b = tie(total, gate_up_grad, feed_a, feed_b)
-    gate_up_sum = over_x(over_cores(gate_up_grad, 4))
+    gate_up_near = over_cores(gate_up_grad, 4)
 
     dh1 = dy + norm_backward(second_hat, second_scale, dxn2 * gain_two)
     dab_blocks = gather_yc(dh1.astype(BF).reshape(micro, slots, width))
-    dab_blocks[2], down_sum = tie(dab_blocks[2], down_sum)
+    dab_blocks[2], down_sum, gate_up_near = tie(dab_blocks[2], down_sum, gate_up_near)
+    gate_up_sum = over_x(gate_up_near)
     down_parts = exchange(down_sum)
     dab_blocks[3], feed_a, feed_b = tie(dab_blocks[3], feed_a, feed_b)
     dab = jnp.concatenate(dab_blocks, axis=1).reshape(group_rows, width)
@@ -404,15 +407,21 @@
     dk = rotary_backward(dk[:, :, None, :], cosine, sine).astype(BF).reshape(group_rows, kv_cols)
     dqkv = jnp.concatenate([dq, dk, dv.astype(BF).reshape(group_rows, kv_cols)], axis=1)
 
-    dqkv, gate_up_sum = tie(dqkv, gate_up_sum)
-    gate_up_parts = exchange(gate_up_sum)
     feed = scatter_z(*pieces([feed_a, feed_b]), "y", size)
     outputs = (live * (middle + feed)).astype(BF)
-    head_ties = {size - 2: [outputs]}
-    head_sum = scatter_z(
-        *blocks_of(dot_rows(xn1, dqkv).astype(BF), out_grad_part), "x", size, head_ties
-    )
-    (outputs,) = head_ties[size - 2]
+    head_own, head_away = blocks_of(dot_rows(xn1, dqkv).astype(BF), out_grad_part)
+    order = [(step + 1) % size for step in range(size)]
+    head_away[order[0]], gate_up_sum = tie(head_away[order[0]], gate_up_sum)
+    head_got = swap_in_turn([head_away[s] for s in order], "x")
+    gate_parts = exchange(gate_up_sum[:, :, :chunk])
+    head_got[-1], up_sum = tie(head_got[-1], gate_up_sum[:, :, chunk:])
+    up_parts = exchange(up_sum)
+    head_sum = head_own[order[0]].astype(F32) + head_got[0]
+    for step in range(1, size):
+        head_sum = head_sum.astype(BF)
+        if step == size - 1:
+            head_sum, outputs = tie(head_sum, outputs)
+        head_sum = head_own[order[step]].astype(F32) + head_got[step] + ring(head_sum, size)
     outputs = outputs.reshape(hidden_in.shape)
 
     dxn1_part = dot_right(dqkv, wqkv).astype(BF).reshape(micro, 4, slots, width)
@@ -441,8 +450,8 @@
     grad_key = side_by_side(heads, q_cols, kv_cols)
     grad_value = side_by_side(heads, q_cols + kv_cols, kv_cols)
     grad_out = side_by_side(heads, qkv_cols, q_cols)
-    grad_gate = side_by_side(gate_up_parts, 0, chunk)
-    grad_up = side_by_side(gate_up_parts, chunk, chunk)
+    grad_gate = side_by_side(gate_parts, 0, chunk)
+    grad_up = side_by_side(up_parts, 0, chunk)
     grad_down = side_by_side(down_parts, 0, chunk)
 
     def gain_gradient(gain, *pairs):

time: 641 us -> 613 us (0.956)
  waiting for transfers between devices: 268 us -> 229 us
  starting transfers between devices: 84.1 us -> 96.7 us
    ppermute x18, waiting for transfers between devices: 101 us -> 56.1 us  [ring(): return lax.ppermute(value, 'z', [(i, (i + 1) % size) for i in range(size)])]
    ppermute x70, waiting for transfers between devices: 110 us -> 124 us  [swap(): return lax.ppermute(value, axis, [(0, 1), (1, 0)])]
    ppermute x6, waiting for transfers between devices: 35.1 us -> 23.2 us  [to_peers_yc(): lax.ppermute(piece_for(k), ('y', 'c'), [(i, i ^ k) for i in range(4)])]
    ppermute x18, starting transfers between devices: 10.6 us -> 19 us  [ring(): return lax.ppermute(value, 'z', [(i, (i + 1) % size) for i in range(size)])]
    all_to_all x4 -> x5, waiting for transfers between devices: 21.3 us -> 26 us  [exchange(): return lax.all_to_all(parts, ('z', 'y'), 0, 0, tiled=True)]
    all_to_all x4 -> x5, starting transfers between devices: 24.5 us -> 23.7 us  [exchange(): return lax.all_to_all(parts, ('z', 'y'), 0, 0, tiled=True)]
    unnamed x226 -> x217, local copies, waits for them, and re-layouts: 24.5 us -> 25 us
  transfers between devices with their start and end apart: 98 -> 99, of which waited for: 40 -> 38; matrix products, arithmetic and copies ran while one was open for 37% -> 40% of each run, Pallas kernels for 0% -> 0%
where the time goes in v3:
time: 613 us; the launch traced here: 604 us
  waiting for transfers between devices  229 us (37%)
  local copies, waits for them, and re-layouts  114 us (19%)
  starting transfers between devices  96.7 us (16%)
  matrix products  90.6 us (15%)
  other arithmetic  70.1 us (11%)
    ppermute x70, waiting for transfers between devices, swap(): return lax.ppermute(value, axis, [(0, 1), (1, 0)])  124 us
    ppermute x18, waiting for transfers between devices, ring(): return lax.ppermute(value, 'z', [(i, (i + 1) % size) for i in range(size)])  56.1 us
    ppermute x70, starting transfers between devices, swap(): return lax.ppermute(value, axis, [(0, 1), (1, 0)])  49.7 us
    dot_general x6, matrix products, dot_rows(): lax.dot_general(left, right, (((0,), (0,)), ((), ())), preferred_element_...  34.3 us
    dynamic_update_slice x35, local copies, waits for them, and re-layouts, put(): return lax.dynamic_update_slice(buffer, piece, starts)  30.8 us
    dot_general x6, matrix products, dot_right(): lax.dot_general(left, right, (((1,), (1,)), ((), ())), preferred_element_...  26 us
    all_to_all x5, waiting for transfers between devices, exchange(): return lax.all_to_all(parts, ('z', 'y'), 0, 0, tiled=True)  26 us
    dot_general x6, matrix products, dot(): return jnp.dot(left, right, preferred_element_type=F32)  25.7 us
  transfers between devices with their start and end apart: 99, of which 38 were waited for; matrix products, arithmetic and copies ran while one was open for 40% of the time, Pallas kernels for 0%

profile of v3, /device:TPU:0, one launch (start us, length us, event | category | flops | bytes accessed | tf_op | source)
XLA Modules:
  0.0 603.7 jit_solution(13740555388958269117)
XLA Ops:
  15.1 8.9 %collective-permute-done.2 = bf16[72,1536]{1,0:T(8,128)(2,1)} collective-permute-done((bf16[72,1536]{1,0:T(8,128)(2,1)}, bf16[72,1536]{1,0:T(8,128)(2,1)}, u32[]{:S(2)}, u32[]{:S(2)}) %collective-permute-start.2) | collective-permute-done | bytes 221216 | tf_op jit(solution)/shard_map/ppermute | solution.py:105
  44.3 6.2 %collective-permute-done.12 = bf16[2,64,2048]{2,1,0:T(8,128)(2,1)S(1)} collective-permute-done((bf16[2,64,2048]{2,1,0:T(8,128)(2,1)S(1)}, bf16[2,64,2048]{2,1,0:T(8,128)(2,1)S(1)}, u32[]{:S(2)}, u32[]{:S(2)}) %collective-permute-start.12) | collective-permute-done | bytes 524320 | tf_op jit(solution)/shard_map/ppermute | solution.py:60
  61.5 6.3 %collective-permute-done.6 = bf16[128,2048]{1,0:T(8,128)(2,1)} collective-permute-done((bf16[128,2048]{1,0:T(8,128)(2,1)}, bf16[128,2048]{1,0:T(8,128)(2,1)}, u32[]{:S(2)}, u32[]{:S(2)}) %collective-permute-start.6) | collective-permute-done | bytes 524320 | tf_op jit(solution)/shard_map/ppermute | solution.py:64
  92.2 9.6 %collective-permute-done.9 = bf16[128,2048]{1,0:T(8,128)(2,1)S(1)} collective-permute-done((bf16[128,2048]{1,0:T(8,128)(2,1)}, bf16[128,2048]{1,0:T(8,128)(2,1)S(1)}, u32[]{:S(2)}, u32[]{:S(2)}) %collective-permute-start.9) | collective-permute-done | bytes 524320 | tf_op jit(solution)/shard_map/ppermute | solution.py:64
  113.3 7.1 %collective-permute-done.16 = bf16[264,1536]{1,0:T(8,128)(2,1)S(1)} collective-permute-done((bf16[264,1536]{1,0:T(8,128)(2,1)S(1)}, bf16[264,1536]{1,0:T(8,128)(2,1)S(1)}, u32[]{:S(2)}, u32[]{:S(2)}) %collective-permute-start.16) | collective-permute-done | bytes 811040 | tf_op jit(solution)/shard_map/ppermute | solution.py:60
  167.9 11.3 %collective-permute-done.26 = bf16[2,64,2048]{2,1,0:T(8,128)(2,1)S(1)} collective-permute-done((bf16[2,64,2048]{2,1,0:T(8,128)(2,1)S(1)}, bf16[2,64,2048]{2,1,0:T(8,128)(2,1)S(1)}, u32[]{:S(2)}, u32[]{:S(2)}) %collective-permute-start.26) | collective-permute-done | bytes 524320 | tf_op jit(solution)/shard_map/ppermute | solution.py:60
  203.6 8.7 %all-to-all-done.1 = bf16[8,64,1024]{2,1,0:T(8,128)(2,1)S(1)} async-done(((bf16[8,64,1024]{2,1,0:T(8,128)(2,1)}), bf16[8,64,1024]{2,1,0:T(8,128)(2,1)S(1)}, u32[]{:S(2)}, u32[]{:S(2)}) %all-to-all-start.1) | async-done | bytes 1048608 | tf_op jit(solution)/shard_map/all_to_all | solution.py:171
  219.2 6.7 %collective-permute-done.27 = bf16[128,2048]{1,0:T(8,128)(2,1)S(1)} collective-permute-done((bf16[128,2048]{1,0:T(8,128)(2,1)S(1)}, bf16[128,2048]{1,0:T(8,128)(2,1)S(1)}, u32[]{:S(2)}, u32[]{:S(2)}) %collective-permute-start.27) | collective-permute-done | bytes 524320 | tf_op jit(solution)/shard_map/ppermute | solution.py:64
  228.4 11.6 %collective-permute-done.29 = bf16[8,64,2048]{2,1,0:T(8,128)(2,1)} collective-permute-done((bf16[8,64,2048]{2,1,0:T(8,128)(2,1)}, bf16[8,64,2048]{2,1,0:T(8,128)(2,1)}, u32[]{:S(2)}, u32[]{:S(2)}) %collective-permute-start.29) | collective-permute-done | bytes 2097184 | tf_op jit(solution)/shard_map/ppermute | solution.py:60
  253.4 12.2 %collective-permute-done.30 = bf16[128,2048]{1,0:T(8,128)(2,1)S(1)} collective-permute-done((bf16[128,2048]{1,0:T(8,128)(2,1)S(1)}, bf16[128,2048]{1,0:T(8,128)(2,1)S(1)}, u32[]{:S(2)}, u32[]{:S(2)}) %collective-permute-start.30) | collective-permute-done | bytes 524320 | tf_op jit(solution)/shard_map/ppermute | solution.py:64
  269.5 9.1 %fusion.116 = f32[768,2048]{1,0:T(8,128)S(1)} fusion(bf16[768,2048]{1,0:T(8,128)(2,1)S(1)} %constant_dynamic-update-slice_fusion, bf16[2048,2048]{1,0:T(8,128)(2,1)} %bitcast.95), kind=kOutput, calls=%fused_computation.441 | convolution fusion | flops 6442450944 | bytes 17825792 | tf_op jit(solution)/shard_map/dot_general | solution.py:48
  286.4 9.2 %convolution_convert_fusion.1 = bf16[768,2048]{1,0:T(8,128)(2,1)S(1)} fusion(bf16[2048,2048]{1,0:T(8,128)(2,1)} %bitcast.95, bf16[768,1024]{1,0:T(8,128)(2,1)S(1)} %get-tuple-element.256, bf16[768,1024]{1,0:T(8,128)(2,1)S(1)} %get-tuple-element.255), kind=kOutput, calls=%fused_computation.11 | convolution fusion | flops 6450315264 | bytes 14680064 | tf_op jit(solution)/shard_map/dot_general | solution.py:52
  337.9 10.5 %fusion.119 = f32[2048,2048]{1,0:T(8,128)} fusion(bf16[768,2048]{1,0:T(8,128)(2,1)S(1)} %copy-done.74, bf16[768,2048]{1,0:T(8,128)(2,1)S(1)} %copy-done.28), kind=kOutput, calls=%fused_computation.444 | convolution fusion | flops 6442450944 | bytes 23068672 | tf_op jit(solution)/shard_map/dot_general | solution.py:56
  350.6 11.6 %add_convert_fusion = bf16[2048,2048]{1,0:T(8,128)(2,1)} fusion(f32[2048,2048]{1,0:T(8,128)} %fusion.119, bf16[256,2048]{1,0:T(8,128)(2,1)S(1)} %pad_maximum_fusion.4, bf16[256,2048]{1,0:T(8,128)(2,1)S(1)} %pad_maximum_fusion.5), kind=kOutput, calls=%fused_computation | convolution fusion | flops 2155872256 | bytes 27262976 | tf_op jit(solution)/shard_map/dot_general | solution.py:56
  372.5 11.0 %collective-permute-done.61 = bf16[2,64,2048]{2,1,0:T(8,128)(2,1)S(1)} collective-permute-done((bf16[2,64,2048]{2,1,0:T(8,128)(2,1)S(1)}, bf16[2,64,2048]{2,1,0:T(8,128)(2,1)S(1)}, u32[]{:S(2)}, u32[]{:S(2)}) %collective-permute-start.61) | collective-permute-done | bytes 524320 | tf_op jit(solution)/shard_map/ppermute | solution.py:60
  433.7 10.6 %collective-permute-done.78 = bf16[128,2048]{1,0:T(8,128)(2,1)S(1)} collective-permute-done((bf16[128,2048]{1,0:T(8,128)(2,1)S(1)}, bf16[128,2048]{1,0:T(8,128)(2,1)S(1)}, u32[]{:S(2)}, u32[]{:S(2)}) %collective-permute-start.78) | collective-permute-done | bytes 524320 | tf_op jit(solution)/shard_map/ppermute | solution.py:60
  453.1 6.0 collective-permute-done.88
  460.6 8.5 %collective-permute-done.79 = bf16[128,2048]{1,0:T(8,128)(2,1)} collective-permute-done((bf16[128,2048]{1,0:T(8,128)(2,1)}, bf16[128,2048]{1,0:T(8,128)(2,1)}, u32[]{:S(2)}, u32[]{:S(2)}) %collective-permute-start.79) | collective-permute-done | bytes 524320 | tf_op jit(solution)/shard_map/ppermute | solution.py:60
  474.1 6.8 %collective-permute-done.71 = bf16[4,2,64,2048]{3,2,1,0:T(8,128)(2,1)} collective-permute-done((bf16[4,2,64,2048]{3,2,1,0:T(8,128)(2,1)}, bf16[4,2,64,2048]{3,2,1,0:T(8,128)(2,1)}, u32[]{:S(2)}, u32[]{:S(2)}) %collective-permute-start.71) | collective-permute-done | bytes 2097184 | tf_op jit(solution)/shard_map/ppermute | solution.py:60
  491.0 12.3 %collective-permute-done.72 = bf16[256,1536]{1,0:T(8,128)(2,1)} collective-permute-done((bf16[256,1536]{1,0:T(8,128)(2,1)}, bf16[256,1536]{1,0:T(8,128)(2,1)}, u32[]{:S(2)}, u32[]{:S(2)}) %collective-permute-start.72) | collective-permute-done | bytes 786464 | tf_op jit(solution)/shard_map/ppermute | solution.py:60
  513.7 10.8 %collective-permute-done.73 = bf16[256,1536]{1,0:T(8,128)(2,1)S(1)} collective-permute-done((bf16[256,1536]{1,0:T(8,128)(2,1)}, bf16[256,1536]{1,0:T(8,128)(2,1)S(1)}, u32[]{:S(2)}, u32[]{:S(2)}) %collective-permute-start.73) | collective-permute-done | bytes 786464 | tf_op jit(solution)/shard_map/ppermute | solution.py:60
  533.1 17.2 %all-to-all-done.2 = bf16[8,64,1024]{2,1,0:T(8,128)(2,1)} async-done(((bf16[8,64,1024]{2,1,0:T(8,128)(2,1)}), bf16[8,64,1024]{2,1,0:T(8,128)(2,1)}, u32[]{:S(2)}, u32[]{:S(2)}) %all-to-all-start.2) | async-done | bytes 1048608 | tf_op jit(solution)/shard_map/all_to_all | solution.py:171
  571.8 9.9 %collective-permute-done.90 = bf16[256,1536]{1,0:T(8,128)(2,1)} collective-permute-done((bf16[256,1536]{1,0:T(8,128)(2,1)}, bf16[256,1536]{1,0:T(8,128)(2,1)}, u32[]{:S(2)}, u32[]{:S(2)}) %collective-permute-start.90) | collective-permute-done | bytes 786464 | tf_op jit(solution)/shard_map/ppermute | solution.py:64
  587.0 10.0 %collective-permute-done.92 = bf16[64,1536]{1,0:T(8,128)(2,1)S(1)} collective-permute-done((bf16[64,1536]{1,0:T(8,128)(2,1)S(1)}, bf16[64,1536]{1,0:T(8,128)(2,1)S(1)}, u32[]{:S(2)}, u32[]{:S(2)}) %collective-permute-start.92) | collective-permute-done | bytes 196640 | tf_op jit(solution)/shard_map/ppermute | solution.py:105
  (622 shorter events, 368.3 us)
Async XLA Ops:
  3.7 47.6 %collective-permute-start.17 = (bf16[128,2048]{1,0:T(8,128)(2,1)}, bf16[128,2048]{1,0:T(8,128)(2,1)}, u32[]{:S(2)}, u32[]{:S(2)}) collective-permute-start(bf16[128,2048]{1,0:T(8,128)(2,1)} %get-tuple-element.381), channel_id=1, source_target_pairs={{0,2},{2,0},{1,3},{3,1},{4,6},{6,4},{5,7},{7,5},{8,10},{10,8},{9,1... | collective-permute-start | bytes 1572872 | tf_op jit(solution)/shard_map/ppermute | solution.py:60
  6.7 26.4 %collective-permute-start.3 = (bf16[128,2048]{1,0:T(8,128)(2,1)}, bf16[128,2048]{1,0:T(8,128)(2,1)}, u32[]{:S(2)}, u32[]{:S(2)}) collective-permute-start(bf16[128,2048]{1,0:T(8,128)(2,1)} %get-tuple-element.381), channel_id=1, source_target_pairs={{0,8},{8,16},{16,24},{24,0},{1,9},{9,17},{17,25},{25,1},{2,10},{10... | collective-permute-start | bytes 1572872 | tf_op jit(solution)/shard_map/ppermute | solution.py:64
  33.1 28.5 %collective-permute-start.4 = (bf16[264,1536]{1,0:T(8,128)(2,1)}, bf16[264,1536]{1,0:T(8,128)(2,1)}, u32[]{:S(2)}, u32[]{:S(2)}) collective-permute-start(bf16[264,1536]{1,0:T(8,128)(2,1)} %fusion.54), channel_id=1, source_target_pairs={{0,8},{8,16},{16,24},{24,0},{1,9},{9,17},{17,25},{25,1},{2,10},{10... | collective-permute-start | bytes 2433032 | tf_op jit(solution)/shard_map/ppermute | solution.py:64
  73.7 28.1 %collective-permute-start.9 = (bf16[128,2048]{1,0:T(8,128)(2,1)}, bf16[128,2048]{1,0:T(8,128)(2,1)S(1)}, u32[]{:S(2)}, u32[]{:S(2)}) collective-permute-start(bf16[128,2048]{1,0:T(8,128)(2,1)} %collective-permute-done.6), channel_id=1, source_target_pairs={{0,8},{8,16},{16,24},{24,0},{1,9},{9,17},{17,25},{25,1},{2,10},{10... | collective-permute-start | bytes 1572872 | tf_op jit(solution)/shard_map/ppermute | solution.py:64
  76.4 29.0 %collective-permute-start.19 = (bf16[128,2048]{1,0:T(8,128)(2,1)}, bf16[128,2048]{1,0:T(8,128)(2,1)}, u32[]{:S(2)}, u32[]{:S(2)}) collective-permute-start(bf16[128,2048]{1,0:T(8,128)(2,1)} %collective-permute-done.6), channel_id=1, source_target_pairs={{0,2},{2,0},{1,3},{3,1},{4,6},{6,4},{5,7},{7,5},{8,10},{10,8},{9,1... | collective-permute-start | bytes 1572872 | tf_op jit(solution)/shard_map/ppermute | solution.py:60
  129.1 50.8 %all-to-all-start = ((bf16[8,64,2048]{2,1,0:T(8,128)(2,1)}), bf16[8,64,2048]{2,1,0:T(8,128)(2,1)}, u32[]{:S(2)}, u32[]{:S(2)}) async-start(bf16[8,64,2048]{2,1,0:T(8,128)(2,1)} %copy.138), calls=%async_computation | async-start | bytes 4194304 | tf_op jit(solution)/shard_map/all_to_all | solution.py:171
  181.5 30.9 %all-to-all-start.1 = ((bf16[8,64,1024]{2,1,0:T(8,128)(2,1)}), bf16[8,64,1024]{2,1,0:T(8,128)(2,1)S(1)}, u32[]{:S(2)}, u32[]{:S(2)}) async-start(bf16[8,64,1024]{2,1,0:T(8,128)(2,1)} %copy.139), calls=%async_computation.1 | async-start | bytes 2097152 | tf_op jit(solution)/shard_map/all_to_all | solution.py:171
  192.2 47.9 %collective-permute-start.29 = (bf16[8,64,2048]{2,1,0:T(8,128)(2,1)}, bf16[8,64,2048]{2,1,0:T(8,128)(2,1)}, u32[]{:S(2)}, u32[]{:S(2)}) collective-permute-start(bf16[8,64,2048]{2,1,0:T(8,128)(2,1)} %all-to-all-done), channel_id=1, source_target_pairs={{0,4},{4,0},{1,5},{5,1},{2,6},{6,2},{3,7},{7,3},{8,12},{12,8},{9,1... | collective-permute-start | bytes 6291464 | tf_op jit(solution)/shard_map/ppermute | solution.py:60
  240.1 26.7 %collective-permute-start.34 = (bf16[128,2048]{1,0:T(8,128)(2,1)S(1)}, bf16[128,2048]{1,0:T(8,128)(2,1)S(1)}, u32[]{:S(2)}, u32[]{:S(2)}) collective-permute-start(bf16[128,2048]{1,0:T(8,128)(2,1)S(1)} %collective-permute-done.28), channel_id=1, source_target_pairs={{0,2},{2,0},{1,3},{3,1},{4,6},{6,4},{5,7},{7,5},{8,10},{10,8},{9,1... | collective-permute-start | bytes 1572872 | tf_op jit(solution)/shard_map/ppermute | solution.py:60
  251.1 27.5 %collective-permute-start.47 = (bf16[8,64,1024]{2,1,0:T(8,128)(2,1)S(1)}, bf16[8,64,1024]{2,1,0:T(8,128)(2,1)S(1)}, u32[]{:S(2)}, u32[]{:S(2)}) collective-permute-start(bf16[8,64,1024]{2,1,0:T(8,128)(2,1)S(1)} %all-to-all-done.1), channel_id=1, source_target_pairs={{0,4},{4,0},{1,5},{5,1},{2,6},{6,2},{3,7},{7,3},{8,12},{12,8},{9,1... | collective-permute-start | bytes 3145736 | tf_op jit(solution)/shard_map/ppermute | solution.py:60
  335.6 26.5 %collective-permute-start.63 = (bf16[2,2,2,64,1024]{4,3,2,1,0:T(8,128)(2,1)S(1)}, bf16[2,2,2,64,1024]{4,3,2,1,0:T(8,128)(2,1)}, u32[]{:S(2)}, u32[]{:S(2)}) collective-permute-start(bf16[2,2,2,64,1024]{4,3,2,1,0:T(8,128)(2,1)S(1)} %dynamic-slice_bitcast_fusion.5), channel_id=1, source_target_pairs={{0,1},{1,0},{2,3},{3,2},{4,5},{5,4},{6,7},{7,6},{8,9},{9,8},{10,11... | collective-permute-start | bytes 3145736 | tf_op jit(solution)/shard_map/ppermute | solution.py:60
  335.7 28.0 %collective-permute-start.62 = (bf16[2,2,2,64,1024]{4,3,2,1,0:T(8,128)(2,1)S(1)}, bf16[2,2,2,64,1024]{4,3,2,1,0:T(8,128)(2,1)}, u32[]{:S(2)}, u32[]{:S(2)}) collective-permute-start(bf16[2,2,2,64,1024]{4,3,2,1,0:T(8,128)(2,1)S(1)} %dynamic-slice_bitcast_fusion.6), channel_id=1, source_target_pairs={{0,1},{1,0},{2,3},{3,2},{4,5},{5,4},{6,7},{7,6},{8,9},{9,8},{10,11... | collective-permute-start | bytes 3145736 | tf_op jit(solution)/shard_map/ppermute | solution.py:60
  365.7 28.5 %collective-permute-start.64 = (bf16[4,2,64,1024]{3,2,1,0:T(8,128)(2,1)S(1)}, bf16[4,2,64,1024]{3,2,1,0:T(8,128)(2,1)S(1)}, u32[]{:S(2)}, u32[]{:S(2)}) collective-permute-start(bf16[4,2,64,1024]{3,2,1,0:T(8,128)(2,1)S(1)} %fusion.24), channel_id=1, source_target_pairs={{0,4},{4,0},{1,5},{5,1},{2,6},{6,2},{3,7},{7,3},{8,12},{12,8},{9,1... | collective-permute-start | bytes 3145736 | tf_op jit(solution)/shard_map/ppermute | solution.py:60
  390.0 36.7 %collective-permute-start.77 = (bf16[128,2048]{1,0:T(8,128)(2,1)}, bf16[128,2048]{1,0:T(8,128)(2,1)}, u32[]{:S(2)}, u32[]{:S(2)}) collective-permute-start(bf16[128,2048]{1,0:T(8,128)(2,1)} %get-tuple-element.273), channel_id=1, source_target_pairs={{0,2},{2,0},{1,3},{3,1},{4,6},{6,4},{5,7},{7,5},{8,10},{10,8},{9,1... | collective-permute-start | bytes 1572872 | tf_op jit(solution)/shard_map/ppermute | solution.py:60
  406.9 67.1 %all-to-all-start.4 = ((bf16[8,64,1024]{2,1,0:T(8,128)(2,1)}), bf16[8,64,1024]{2,1,0:T(8,128)(2,1)S(1)}, u32[]{:S(2)}, u32[]{:S(2)}) async-start(bf16[8,64,1024]{2,1,0:T(8,128)(2,1)} %bitcast.686), calls=%async_computation.4 | async-start | bytes 2097152 | tf_op jit(solution)/shard_map/all_to_all | solution.py:171
  422.7 28.3 %collective-permute-start.84 = (bf16[64,2048]{1,0:T(8,128)(2,1)S(1)}, bf16[64,2048]{1,0:T(8,128)(2,1)S(1)}, u32[]{:S(2)}, u32[]{:S(2)}) collective-permute-start(bf16[64,2048]{1,0:T(8,128)(2,1)S(1)} %get-tuple-element.289), channel_id=1, source_target_pairs={{0,1},{1,0},{2,3},{3,2},{4,5},{5,4},{6,7},{7,6},{8,9},{9,8},{10,11... | collective-permute-start | bytes 786440 | tf_op jit(solution)/shard_map/ppermute | solution.py:60
  432.5 48.4 %collective-permute-start.71 = (bf16[4,2,64,2048]{3,2,1,0:T(8,128)(2,1)}, bf16[4,2,64,2048]{3,2,1,0:T(8,128)(2,1)}, u32[]{:S(2)}, u32[]{:S(2)}) collective-permute-start(bf16[4,2,64,2048]{3,2,1,0:T(8,128)(2,1)} %dynamic-slice_bitcast_fusion), channel_id=1, source_target_pairs={{0,4},{4,0},{1,5},{5,1},{2,6},{6,2},{3,7},{7,3},{8,12},{12,8},{9,1... | collective-permute-start | bytes 6291464 | tf_op jit(solution)/shard_map/ppermute | solution.py:60
  469.1 41.7 %collective-permute-start.80 = (bf16[128,2048]{1,0:T(8,128)(2,1)}, bf16[128,2048]{1,0:T(8,128)(2,1)}, u32[]{:S(2)}, u32[]{:S(2)}) collective-permute-start(bf16[128,2048]{1,0:T(8,128)(2,1)} %get-tuple-element.182), channel_id=1, source_target_pairs={{0,2},{2,0},{1,3},{3,1},{4,6},{6,4},{5,7},{7,5},{8,10},{10,8},{9,1... | collective-permute-start | bytes 1572872 | tf_op jit(solution)/shard_map/ppermute | solution.py:60
  473.6 37.2 %collective-permute-start.83 = (bf16[128,2048]{1,0:T(8,128)(2,1)}, bf16[128,2048]{1,0:T(8,128)(2,1)}, u32[]{:S(2)}, u32[]{:S(2)}) collective-permute-start(bf16[128,2048]{1,0:T(8,128)(2,1)} %fusion.33), channel_id=1, source_target_pairs={{0,8},{8,16},{16,24},{24,0},{1,9},{9,17},{17,25},{25,1},{2,10},{10... | collective-permute-start | bytes 1572872 | tf_op jit(solution)/shard_map/ppermute | solution.py:64
  486.7 63.6 %all-to-all-start.2 = ((bf16[8,64,1024]{2,1,0:T(8,128)(2,1)}), bf16[8,64,1024]{2,1,0:T(8,128)(2,1)}, u32[]{:S(2)}, u32[]{:S(2)}) async-start(bf16[8,64,1024]{2,1,0:T(8,128)(2,1)} %get-tuple-element.279), calls=%async_computation.2 | async-start | bytes 2097152 | tf_op jit(solution)/shard_map/all_to_all | solution.py:171
  504.9 23.7 %collective-permute-start.75 = (bf16[256,1536]{1,0:T(8,128)(2,1)S(1)}, bf16[256,1536]{1,0:T(8,128)(2,1)S(1)}, u32[]{:S(2)}, u32[]{:S(2)}) collective-permute-start(bf16[256,1536]{1,0:T(8,128)(2,1)S(1)} %add_convert_fusion.5), channel_id=1, source_target_pairs={{0,8},{8,16},{16,24},{24,0},{1,9},{9,17},{17,25},{25,1},{2,10},{10... | collective-permute-start | bytes 2359304 | tf_op jit(solution)/shard_map/ppermute | solution.py:64
  524.6 31.3 %collective-permute-start.74 = (bf16[256,1536]{1,0:T(8,128)(2,1)}, bf16[256,1536]{1,0:T(8,128)(2,1)}, u32[]{:S(2)}, u32[]{:S(2)}) collective-permute-start(bf16[256,1536]{1,0:T(8,128)(2,1)} %pad_maximum_fusion.8), channel_id=1, source_target_pairs={{0,4},{4,0},{1,5},{5,1},{2,6},{6,2},{3,7},{7,3},{8,12},{12,8},{9,1... | collective-permute-start | bytes 2359304 | tf_op jit(solution)/shard_map/ppermute | solution.py:60
  529.8 27.1 %collective-permute-start.76 = (bf16[256,1536]{1,0:T(8,128)(2,1)}, bf16[256,1536]{1,0:T(8,128)(2,1)}, u32[]{:S(2)}, u32[]{:S(2)}) collective-permute-start(bf16[256,1536]{1,0:T(8,128)(2,1)} %add_convert_fusion.4), channel_id=1, source_target_pairs={{0,8},{8,16},{16,24},{24,0},{1,9},{9,17},{17,25},{25,1},{2,10},{10... | collective-permute-start | bytes 2359304 | tf_op jit(solution)/shard_map/ppermute | solution.py:64
  568.2 32.9 %all-to-all-start.3 = ((bf16[8,64,1024]{2,1,0:T(8,128)(2,1)}), bf16[8,64,1024]{2,1,0:T(8,128)(2,1)S(1)}, u32[]{:S(2)}, u32[]{:S(2)}) async-start(bf16[8,64,1024]{2,1,0:T(8,128)(2,1)} %get-tuple-element.191), calls=%async_computation.3 | async-start | bytes 2097152 | tf_op jit(solution)/shard_map/all_to_all | solution.py:171
  (165 other events, 2262.2 us)

commit v4 on v3

--- a/solution.py
+++ b/solution.py
@@ -208,25 +208,25 @@
         [block.reshape(block_rows, head_cols), beside(gain_block, head_cols)], axis=0
     )
 
-    block, dfb_around[1], hidden_in, w_gate, w_up, w_down = tie(
-        block, dfb_around[1], hidden_in, w_gate, w_up, w_down
+    block, dfb_around[1], dfb_here, hidden_in, w_gate, w_up, w_down = tie(
+        block, dfb_around[1], dfb_around[0], hidden_in, w_gate, w_up, w_down
     )
     tokens = hidden_in.reshape(micro, slots, width)
     around, over = [block], []
-    across = [swap(tokens, "y")]
-    token_blocks = gather_yc(tokens, across[0])
+    across = swap(tokens, "y")
+    dfb_here, across = tie(dfb_here, across)
+    token_blocks = gather_yc(tokens, across)
     for s in range(1, size):
         over.append(swap(around[-1], "x"))
         around.append(ring(around[-1], size))
         around[s], over[s - 1] = tie(around[s], over[s - 1])
-        if s < size - 1:
+        if s > 1:
             dfb_around.append(ring(dfb_around[-1], size))
-            around[s], dfb_around[s + 1] = tie(around[s], dfb_around[s + 1])
         if s == size - 2:
             around[s], *token_blocks = tie(around[s], *token_blocks)
-    dfb_over = swap_in_turn(dfb_around, "y")
+    dfb_over = swap_in_turn([dfb_here, *dfb_around[1:]], "y")
     gate_up_local = jnp.concatenate([by_chunk(w_gate), by_chunk(w_up)], axis=2)
-    gate_up_local, around[-1], *dfb_over = tie(gate_up_local, around[-1], *dfb_over)
+    gate_up_local, around[-1], *dfb_over[:-1] = tie(gate_up_local, around[-1], *dfb_over[:-1])
     gate_up_mine = exchange(gate_up_local)
     over.append(swap(around[-1], "x"))
     gate_up_over = swap(gate_up_mine, "x")

time: 613 us -> 600 us (0.979)
  starting transfers between devices: 96.7 us -> 89.6 us
    ppermute x6, waiting for transfers between devices: 23.2 us -> 16.3 us  [to_peers_yc(): lax.ppermute(piece_for(k), ('y', 'c'), [(i, i ^ k) for i in range(4)])]
    unnamed x217 -> x229, local copies, waits for them, and re-layouts: 25 us -> 23.2 us
  transfers between devices with their start and end apart: 99 -> 99, of which waited for: 38 -> 40; matrix products, arithmetic and copies ran while one was open for 40% -> 40% of each run, Pallas kernels for 0% -> 0%
where the time goes in v4:
time: 600 us; the launch traced here: 591 us
  waiting for transfers between devices  229 us (38%)
  local copies, waits for them, and re-layouts  109 us (18%)
  matrix products  90.6 us (15%)
  starting transfers between devices  89.6 us (15%)
  other arithmetic  68.4 us (11%)
    ppermute x70, waiting for transfers between devices, swap(): return lax.ppermute(value, axis, [(0, 1), (1, 0)])  129 us
    ppermute x18, waiting for transfers between devices, ring(): return lax.ppermute(value, 'z', [(i, (i + 1) % size) for i in range(size)])  56.4 us
    ppermute x70, starting transfers between devices, swap(): return lax.ppermute(value, axis, [(0, 1), (1, 0)])  45.3 us
    dot_general x6, matrix products, dot_rows(): lax.dot_general(left, right, (((0,), (0,)), ((), ())), preferred_element_...  34.3 us
    dynamic_update_slice x35, local copies, waits for them, and re-layouts, put(): return lax.dynamic_update_slice(buffer, piece, starts)  29.2 us
    all_to_all x5, waiting for transfers between devices, exchange(): return lax.all_to_all(parts, ('z', 'y'), 0, 0, tiled=True)  27.9 us
    dot_general x6, matrix products, dot_right(): lax.dot_general(left, right, (((1,), (1,)), ((), ())), preferred_element_...  26 us
    dot_general x6, matrix products, dot(): return jnp.dot(left, right, preferred_element_type=F32)  25.7 us
  transfers between devices with their start and end apart: 99, of which 40 were waited for; matrix products, arithmetic and copies ran while one was open for 40% of the time, Pallas kernels for 0%

profile of v4, /device:TPU:0, one launch (start us, length us, event | category | flops | bytes accessed | tf_op | source)
XLA Modules:
  0.0 590.8 jit_solution(15024348504608840162)
XLA Ops:
  34.5 9.3 %collective-permute-done.10 = bf16[2,64,2048]{2,1,0:T(8,128)(2,1)S(1)} collective-permute-done((bf16[2,64,2048]{2,1,0:T(8,128)(2,1)S(1)}, bf16[2,64,2048]{2,1,0:T(8,128)(2,1)S(1)}, u32[]{:S(2)}, u32[]{:S(2)}) %collective-permute-start.10) | collective-permute-done | bytes 524320 | tf_op jit(solution)/shard_map/ppermute | solution.py:60
  51.9 7.4 %collective-permute-done.16 = bf16[128,2048]{1,0:T(8,128)(2,1)} collective-permute-done((bf16[128,2048]{1,0:T(8,128)(2,1)}, bf16[128,2048]{1,0:T(8,128)(2,1)}, u32[]{:S(2)}, u32[]{:S(2)}) %collective-permute-start.16) | collective-permute-done | bytes 524320 | tf_op jit(solution)/shard_map/ppermute | solution.py:64
  85.3 7.0 %collective-permute-done.6 = bf16[264,1536]{1,0:T(8,128)(2,1)S(1)} collective-permute-done((bf16[264,1536]{1,0:T(8,128)(2,1)}, bf16[264,1536]{1,0:T(8,128)(2,1)S(1)}, u32[]{:S(2)}, u32[]{:S(2)}) %collective-permute-start.6) | collective-permute-done | bytes 811040 | tf_op jit(solution)/shard_map/ppermute | solution.py:64
  102.0 7.8 %collective-permute-done.14 = bf16[264,1536]{1,0:T(8,128)(2,1)S(1)} collective-permute-done((bf16[264,1536]{1,0:T(8,128)(2,1)S(1)}, bf16[264,1536]{1,0:T(8,128)(2,1)S(1)}, u32[]{:S(2)}, u32[]{:S(2)}) %collective-permute-start.14) | collective-permute-done | bytes 811040 | tf_op jit(solution)/shard_map/ppermute | solution.py:60
  152.1 13.5 %collective-permute-done.25 = bf16[2,64,2048]{2,1,0:T(8,128)(2,1)S(1)} collective-permute-done((bf16[2,64,2048]{2,1,0:T(8,128)(2,1)S(1)}, bf16[2,64,2048]{2,1,0:T(8,128)(2,1)S(1)}, u32[]{:S(2)}, u32[]{:S(2)}) %collective-permute-start.25) | collective-permute-done | bytes 524320 | tf_op jit(solution)/shard_map/ppermute | solution.py:60
  190.4 8.9 %all-to-all-done.1 = bf16[8,64,1024]{2,1,0:T(8,128)(2,1)S(1)} async-done(((bf16[8,64,1024]{2,1,0:T(8,128)(2,1)}), bf16[8,64,1024]{2,1,0:T(8,128)(2,1)S(1)}, u32[]{:S(2)}, u32[]{:S(2)}) %all-to-all-start.1) | async-done | bytes 1048608 | tf_op jit(solution)/shard_map/all_to_all | solution.py:171
  206.3 6.8 %collective-permute-done.26 = bf16[128,2048]{1,0:T(8,128)(2,1)S(1)} collective-permute-done((bf16[128,2048]{1,0:T(8,128)(2,1)S(1)}, bf16[128,2048]{1,0:T(8,128)(2,1)S(1)}, u32[]{:S(2)}, u32[]{:S(2)}) %collective-permute-start.26) | collective-permute-done | bytes 524320 | tf_op jit(solution)/shard_map/ppermute | solution.py:64
  215.4 11.5 %collective-permute-done.28 = bf16[8,64,2048]{2,1,0:T(8,128)(2,1)} collective-permute-done((bf16[8,64,2048]{2,1,0:T(8,128)(2,1)}, bf16[8,64,2048]{2,1,0:T(8,128)(2,1)}, u32[]{:S(2)}, u32[]{:S(2)}) %collective-permute-start.28) | collective-permute-done | bytes 2097184 | tf_op jit(solution)/shard_map/ppermute | solution.py:60
  240.2 12.4 %collective-permute-done.29 = bf16[128,2048]{1,0:T(8,128)(2,1)S(1)} collective-permute-done((bf16[128,2048]{1,0:T(8,128)(2,1)S(1)}, bf16[128,2048]{1,0:T(8,128)(2,1)S(1)}, u32[]{:S(2)}, u32[]{:S(2)}) %collective-permute-start.29) | collective-permute-done | bytes 524320 | tf_op jit(solution)/shard_map/ppermute | solution.py:64
  256.4 9.1 %fusion.116 = f32[768,2048]{1,0:T(8,128)S(1)} fusion(bf16[768,2048]{1,0:T(8,128)(2,1)S(1)} %constant_dynamic-update-slice_fusion, bf16[2048,2048]{1,0:T(8,128)(2,1)} %bitcast.95), kind=kOutput, calls=%fused_computation.441 | convolution fusion | flops 6442450944 | bytes 17825792 | tf_op jit(solution)/shard_map/dot_general | solution.py:48
  273.3 9.2 %convolution_convert_fusion.1 = bf16[768,2048]{1,0:T(8,128)(2,1)S(1)} fusion(bf16[2048,2048]{1,0:T(8,128)(2,1)} %bitcast.95, bf16[768,1024]{1,0:T(8,128)(2,1)S(1)} %get-tuple-element.252, bf16[768,1024]{1,0:T(8,128)(2,1)S(1)} %get-tuple-element.251), kind=kOutput, calls=%fused_computation.11 | convolution fusion | flops 6450315264 | bytes 14680064 | tf_op jit(solution)/shard_map/dot_general | solution.py:52
  307.6 5.9 %add_convert_fusion.1 = bf16[2048,1024]{1,0:T(8,128)(2,1)S(1)} fusion(f32[2048,1024]{1,0:T(8,128)S(1)} %fusion.118, bf16[768,2048]{1,0:T(8,128)(2,1)} %copy-done.77, bf16[768,1024]{1,0:T(8,128)(2,1)S(1)} %get-tuple-element.152), kind=kOutput, calls=%fused_computation.1 | convolution fusion | flops 3225419776 | bytes 17301504 | tf_op jit(solution)/shard_map/dot_general | solution.py:56
  325.0 10.5 %fusion.119 = f32[2048,2048]{1,0:T(8,128)} fusion(bf16[768,2048]{1,0:T(8,128)(2,1)S(1)} %copy-done.80, bf16[768,2048]{1,0:T(8,128)(2,1)S(1)} %copy-done.26), kind=kOutput, calls=%fused_computation.444 | convolution fusion | flops 6442450944 | bytes 23068672 | tf_op jit(solution)/shard_map/dot_general | solution.py:56
  337.6 11.6 %add_convert_fusion = bf16[2048,2048]{1,0:T(8,128)(2,1)} fusion(f32[2048,2048]{1,0:T(8,128)} %fusion.119, bf16[256,2048]{1,0:T(8,128)(2,1)S(1)} %pad_maximum_fusion.4, bf16[256,2048]{1,0:T(8,128)(2,1)S(1)} %pad_maximum_fusion.5), kind=kOutput, calls=%fused_computation | convolution fusion | flops 2155872256 | bytes 27262976 | tf_op jit(solution)/shard_map/dot_general | solution.py:56
  359.4 11.0 %collective-permute-done.61 = bf16[2,64,2048]{2,1,0:T(8,128)(2,1)S(1)} collective-permute-done((bf16[2,64,2048]{2,1,0:T(8,128)(2,1)S(1)}, bf16[2,64,2048]{2,1,0:T(8,128)(2,1)S(1)}, u32[]{:S(2)}, u32[]{:S(2)}) %collective-permute-start.61) | collective-permute-done | bytes 524320 | tf_op jit(solution)/shard_map/ppermute | solution.py:60
  420.7 10.5 %collective-permute-done.78 = bf16[128,2048]{1,0:T(8,128)(2,1)S(1)} collective-permute-done((bf16[128,2048]{1,0:T(8,128)(2,1)S(1)}, bf16[128,2048]{1,0:T(8,128)(2,1)S(1)}, u32[]{:S(2)}, u32[]{:S(2)}) %collective-permute-start.78) | collective-permute-done | bytes 524320 | tf_op jit(solution)/shard_map/ppermute | solution.py:60
  440.2 6.0 %collective-permute-done.88 = bf16[2,64,2048]{2,1,0:T(8,128)(2,1)S(1)} collective-permute-done((bf16[2,64,2048]{2,1,0:T(8,128)(2,1)S(1)}, bf16[2,64,2048]{2,1,0:T(8,128)(2,1)S(1)}, u32[]{:S(2)}, u32[]{:S(2)}) %collective-permute-start.88) | collective-permute-done | bytes 524320 | tf_op jit(solution)/shard_map/ppermute | solution.py:60
  447.6 8.5 %collective-permute-done.79 = bf16[128,2048]{1,0:T(8,128)(2,1)} collective-permute-done((bf16[128,2048]{1,0:T(8,128)(2,1)}, bf16[128,2048]{1,0:T(8,128)(2,1)}, u32[]{:S(2)}, u32[]{:S(2)}) %collective-permute-start.79) | collective-permute-done | bytes 524320 | tf_op jit(solution)/shard_map/ppermute | solution.py:60
  461.1 6.8 %collective-permute-done.71 = bf16[4,2,64,2048]{3,2,1,0:T(8,128)(2,1)} collective-permute-done((bf16[4,2,64,2048]{3,2,1,0:T(8,128)(2,1)}, bf16[4,2,64,2048]{3,2,1,0:T(8,128)(2,1)}, u32[]{:S(2)}, u32[]{:S(2)}) %collective-permute-start.71) | collective-permute-done | bytes 2097184 | tf_op jit(solution)/shard_map/ppermute | solution.py:60
  478.0 12.3 %collective-permute-done.72 = bf16[256,1536]{1,0:T(8,128)(2,1)} collective-permute-done((bf16[256,1536]{1,0:T(8,128)(2,1)}, bf16[256,1536]{1,0:T(8,128)(2,1)}, u32[]{:S(2)}, u32[]{:S(2)}) %collective-permute-start.72) | collective-permute-done | bytes 786464 | tf_op jit(solution)/shard_map/ppermute | solution.py:60
  500.8 10.8 %collective-permute-done.73 = bf16[256,1536]{1,0:T(8,128)(2,1)S(1)} collective-permute-done((bf16[256,1536]{1,0:T(8,128)(2,1)}, bf16[256,1536]{1,0:T(8,128)(2,1)S(1)}, u32[]{:S(2)}, u32[]{:S(2)}) %collective-permute-start.73) | collective-permute-done | bytes 786464 | tf_op jit(solution)/shard_map/ppermute | solution.py:60
  520.1 17.2 %all-to-all-done.2 = bf16[8,64,1024]{2,1,0:T(8,128)(2,1)} async-done(((bf16[8,64,1024]{2,1,0:T(8,128)(2,1)}), bf16[8,64,1024]{2,1,0:T(8,128)(2,1)}, u32[]{:S(2)}, u32[]{:S(2)}) %all-to-all-start.2) | async-done | bytes 1048608 | tf_op jit(solution)/shard_map/all_to_all | solution.py:171
  558.8 9.9 %collective-permute-done.90 = bf16[256,1536]{1,0:T(8,128)(2,1)} collective-permute-done((bf16[256,1536]{1,0:T(8,128)(2,1)}, bf16[256,1536]{1,0:T(8,128)(2,1)}, u32[]{:S(2)}, u32[]{:S(2)}) %collective-permute-start.90) | collective-permute-done | bytes 786464 | tf_op jit(solution)/shard_map/ppermute | solution.py:64
  574.0 10.0 %collective-permute-done.92 = bf16[64,1536]{1,0:T(8,128)(2,1)S(1)} collective-permute-done((bf16[64,1536]{1,0:T(8,128)(2,1)S(1)}, bf16[64,1536]{1,0:T(8,128)(2,1)S(1)}, u32[]{:S(2)}, u32[]{:S(2)}) %collective-permute-start.92) | collective-permute-done | bytes 196640 | tf_op jit(solution)/shard_map/ppermute | solution.py:105
  (634 shorter events, 353.5 us)
Async XLA Ops:
  24.7 37.2 %collective-permute-start.5 = (bf16[264,1536]{1,0:T(8,128)(2,1)}, bf16[264,1536]{1,0:T(8,128)(2,1)}, u32[]{:S(2)}, u32[]{:S(2)}) collective-permute-start(bf16[264,1536]{1,0:T(8,128)(2,1)} %fusion.54), channel_id=1, source_target_pairs={{0,4},{4,0},{1,5},{5,1},{2,6},{6,2},{3,7},{7,3},{8,12},{12,8},{9,1... | collective-permute-start | bytes 2433032 | tf_op jit(solution)/shard_map/ppermute | solution.py:60
  26.3 35.6 %collective-permute-start.4 = (bf16[264,1536]{1,0:T(8,128)(2,1)}, bf16[264,1536]{1,0:T(8,128)(2,1)}, u32[]{:S(2)}, u32[]{:S(2)}) collective-permute-start(bf16[264,1536]{1,0:T(8,128)(2,1)} %fusion.54), channel_id=1, source_target_pairs={{0,8},{8,16},{16,24},{24,0},{1,9},{9,17},{17,25},{25,1},{2,10},{10... | collective-permute-start | bytes 2433032 | tf_op jit(solution)/shard_map/ppermute | solution.py:64
  62.5 29.8 %collective-permute-start.6 = (bf16[264,1536]{1,0:T(8,128)(2,1)}, bf16[264,1536]{1,0:T(8,128)(2,1)S(1)}, u32[]{:S(2)}, u32[]{:S(2)}) collective-permute-start(bf16[264,1536]{1,0:T(8,128)(2,1)} %collective-permute-done.4), channel_id=1, source_target_pairs={{0,8},{8,16},{16,24},{24,0},{1,9},{9,17},{17,25},{25,1},{2,10},{10... | collective-permute-start | bytes 2433032 | tf_op jit(solution)/shard_map/ppermute | solution.py:64
  101.5 72.3 %collective-permute-start.52 = (bf16[128,2048]{1,0:T(8,128)(2,1)}, bf16[128,2048]{1,0:T(8,128)(2,1)}, u32[]{:S(2)}, u32[]{:S(2)}) collective-permute-start(bf16[128,2048]{1,0:T(8,128)(2,1)} %collective-permute-done.18), channel_id=1, source_target_pairs={{0,2},{2,0},{1,3},{3,1},{4,6},{6,4},{5,7},{7,5},{8,10},{10,8},{9,1... | collective-permute-start | bytes 1572872 | tf_op jit(solution)/shard_map/ppermute | solution.py:60
  118.5 49.5 %all-to-all-start = ((bf16[8,64,2048]{2,1,0:T(8,128)(2,1)}), bf16[8,64,2048]{2,1,0:T(8,128)(2,1)}, u32[]{:S(2)}, u32[]{:S(2)}) async-start(bf16[8,64,2048]{2,1,0:T(8,128)(2,1)} %copy.138), calls=%async_computation | async-start | bytes 4194304 | tf_op jit(solution)/shard_map/all_to_all | solution.py:171
  169.6 29.7 %all-to-all-start.1 = ((bf16[8,64,1024]{2,1,0:T(8,128)(2,1)}), bf16[8,64,1024]{2,1,0:T(8,128)(2,1)S(1)}, u32[]{:S(2)}, u32[]{:S(2)}) async-start(bf16[8,64,1024]{2,1,0:T(8,128)(2,1)} %copy.139), calls=%async_computation.1 | async-start | bytes 2097152 | tf_op jit(solution)/shard_map/all_to_all | solution.py:171
  179.1 47.9 %collective-permute-start.28 = (bf16[8,64,2048]{2,1,0:T(8,128)(2,1)}, bf16[8,64,2048]{2,1,0:T(8,128)(2,1)}, u32[]{:S(2)}, u32[]{:S(2)}) collective-permute-start(bf16[8,64,2048]{2,1,0:T(8,128)(2,1)} %all-to-all-done), channel_id=1, source_target_pairs={{0,4},{4,0},{1,5},{5,1},{2,6},{6,2},{3,7},{7,3},{8,12},{12,8},{9,1... | collective-permute-start | bytes 6291464 | tf_op jit(solution)/shard_map/ppermute | solution.py:60
  226.9 26.9 %collective-permute-start.33 = (bf16[128,2048]{1,0:T(8,128)(2,1)S(1)}, bf16[128,2048]{1,0:T(8,128)(2,1)S(1)}, u32[]{:S(2)}, u32[]{:S(2)}) collective-permute-start(bf16[128,2048]{1,0:T(8,128)(2,1)S(1)} %collective-permute-done.27), channel_id=1, source_target_pairs={{0,2},{2,0},{1,3},{3,1},{4,6},{6,4},{5,7},{7,5},{8,10},{10,8},{9,1... | collective-permute-start | bytes 1572872 | tf_op jit(solution)/shard_map/ppermute | solution.py:60
  238.0 27.6 %collective-permute-start.46 = (bf16[8,64,1024]{2,1,0:T(8,128)(2,1)S(1)}, bf16[8,64,1024]{2,1,0:T(8,128)(2,1)S(1)}, u32[]{:S(2)}, u32[]{:S(2)}) collective-permute-start(bf16[8,64,1024]{2,1,0:T(8,128)(2,1)S(1)} %all-to-all-done.1), channel_id=1, source_target_pairs={{0,4},{4,0},{1,5},{5,1},{2,6},{6,2},{3,7},{7,3},{8,12},{12,8},{9,1... | collective-permute-start | bytes 3145736 | tf_op jit(solution)/shard_map/ppermute | solution.py:60
  322.7 26.5 %collective-permute-start.63 = (bf16[2,2,2,64,1024]{4,3,2,1,0:T(8,128)(2,1)S(1)}, bf16[2,2,2,64,1024]{4,3,2,1,0:T(8,128)(2,1)}, u32[]{:S(2)}, u32[]{:S(2)}) collective-permute-start(bf16[2,2,2,64,1024]{4,3,2,1,0:T(8,128)(2,1)S(1)} %dynamic-slice_bitcast_fusion.5), channel_id=1, source_target_pairs={{0,1},{1,0},{2,3},{3,2},{4,5},{5,4},{6,7},{7,6},{8,9},{9,8},{10,11... | collective-permute-start | bytes 3145736 | tf_op jit(solution)/shard_map/ppermute | solution.py:60
  322.7 28.0 %collective-permute-start.62 = (bf16[2,2,2,64,1024]{4,3,2,1,0:T(8,128)(2,1)S(1)}, bf16[2,2,2,64,1024]{4,3,2,1,0:T(8,128)(2,1)}, u32[]{:S(2)}, u32[]{:S(2)}) collective-permute-start(bf16[2,2,2,64,1024]{4,3,2,1,0:T(8,128)(2,1)S(1)} %dynamic-slice_bitcast_fusion.6), channel_id=1, source_target_pairs={{0,1},{1,0},{2,3},{3,2},{4,5},{5,4},{6,7},{7,6},{8,9},{9,8},{10,11... | collective-permute-start | bytes 3145736 | tf_op jit(solution)/shard_map/ppermute | solution.py:60
  352.7 28.5 %collective-permute-start.64 = (bf16[4,2,64,1024]{3,2,1,0:T(8,128)(2,1)S(1)}, bf16[4,2,64,1024]{3,2,1,0:T(8,128)(2,1)S(1)}, u32[]{:S(2)}, u32[]{:S(2)}) collective-permute-start(bf16[4,2,64,1024]{3,2,1,0:T(8,128)(2,1)S(1)} %fusion.24), channel_id=1, source_target_pairs={{0,4},{4,0},{1,5},{5,1},{2,6},{6,2},{3,7},{7,3},{8,12},{12,8},{9,1... | collective-permute-start | bytes 3145736 | tf_op jit(solution)/shard_map/ppermute | solution.py:60
  377.0 36.7 %collective-permute-start.77 = (bf16[128,2048]{1,0:T(8,128)(2,1)}, bf16[128,2048]{1,0:T(8,128)(2,1)}, u32[]{:S(2)}, u32[]{:S(2)}) collective-permute-start(bf16[128,2048]{1,0:T(8,128)(2,1)} %get-tuple-element.269), channel_id=1, source_target_pairs={{0,2},{2,0},{1,3},{3,1},{4,6},{6,4},{5,7},{7,5},{8,10},{10,8},{9,1... | collective-permute-start | bytes 1572872 | tf_op jit(solution)/shard_map/ppermute | solution.py:60
  394.0 67.1 %all-to-all-start.4 = ((bf16[8,64,1024]{2,1,0:T(8,128)(2,1)}), bf16[8,64,1024]{2,1,0:T(8,128)(2,1)S(1)}, u32[]{:S(2)}, u32[]{:S(2)}) async-start(bf16[8,64,1024]{2,1,0:T(8,128)(2,1)} %bitcast.686), calls=%async_computation.4 | async-start | bytes 2097152 | tf_op jit(solution)/shard_map/all_to_all | solution.py:171
  409.7 28.3 %collective-permute-start.84 = (bf16[64,2048]{1,0:T(8,128)(2,1)S(1)}, bf16[64,2048]{1,0:T(8,128)(2,1)S(1)}, u32[]{:S(2)}, u32[]{:S(2)}) collective-permute-start(bf16[64,2048]{1,0:T(8,128)(2,1)S(1)} %get-tuple-element.285), channel_id=1, source_target_pairs={{0,1},{1,0},{2,3},{3,2},{4,5},{5,4},{6,7},{7,6},{8,9},{9,8},{10,11... | collective-permute-start | bytes 786440 | tf_op jit(solution)/shard_map/ppermute | solution.py:60
  419.5 48.4 %collective-permute-start.71 = (bf16[4,2,64,2048]{3,2,1,0:T(8,128)(2,1)}, bf16[4,2,64,2048]{3,2,1,0:T(8,128)(2,1)}, u32[]{:S(2)}, u32[]{:S(2)}) collective-permute-start(bf16[4,2,64,2048]{3,2,1,0:T(8,128)(2,1)} %dynamic-slice_bitcast_fusion), channel_id=1, source_target_pairs={{0,4},{4,0},{1,5},{5,1},{2,6},{6,2},{3,7},{7,3},{8,12},{12,8},{9,1... | collective-permute-start | bytes 6291464 | tf_op jit(solution)/shard_map/ppermute | solution.py:60
  434.6 23.6 %collective-permute-start.82 = (bf16[128,2048]{1,0:T(8,128)(2,1)}, bf16[128,2048]{1,0:T(8,128)(2,1)}, u32[]{:S(2)}, u32[]{:S(2)}) collective-permute-start(bf16[128,2048]{1,0:T(8,128)(2,1)} %fusion.31), channel_id=1, source_target_pairs={{0,8},{8,16},{16,24},{24,0},{1,9},{9,17},{17,25},{25,1},{2,10},{10... | collective-permute-start | bytes 1572872 | tf_op jit(solution)/shard_map/ppermute | solution.py:64
  456.1 41.7 %collective-permute-start.80 = (bf16[128,2048]{1,0:T(8,128)(2,1)}, bf16[128,2048]{1,0:T(8,128)(2,1)}, u32[]{:S(2)}, u32[]{:S(2)}) collective-permute-start(bf16[128,2048]{1,0:T(8,128)(2,1)} %get-tuple-element.178), channel_id=1, source_target_pairs={{0,2},{2,0},{1,3},{3,1},{4,6},{6,4},{5,7},{7,5},{8,10},{10,8},{9,1... | collective-permute-start | bytes 1572872 | tf_op jit(solution)/shard_map/ppermute | solution.py:60
  460.6 37.2 %collective-permute-start.83 = (bf16[128,2048]{1,0:T(8,128)(2,1)}, bf16[128,2048]{1,0:T(8,128)(2,1)}, u32[]{:S(2)}, u32[]{:S(2)}) collective-permute-start(bf16[128,2048]{1,0:T(8,128)(2,1)} %fusion.33), channel_id=1, source_target_pairs={{0,8},{8,16},{16,24},{24,0},{1,9},{9,17},{17,25},{25,1},{2,10},{10... | collective-permute-start | bytes 1572872 | tf_op jit(solution)/shard_map/ppermute | solution.py:64
  473.7 63.6 %all-to-all-start.2 = ((bf16[8,64,1024]{2,1,0:T(8,128)(2,1)}), bf16[8,64,1024]{2,1,0:T(8,128)(2,1)}, u32[]{:S(2)}, u32[]{:S(2)}) async-start(bf16[8,64,1024]{2,1,0:T(8,128)(2,1)} %get-tuple-element.275), calls=%async_computation.2 | async-start | bytes 2097152 | tf_op jit(solution)/shard_map/all_to_all | solution.py:171
  491.9 23.7 %collective-permute-start.75 = (bf16[256,1536]{1,0:T(8,128)(2,1)S(1)}, bf16[256,1536]{1,0:T(8,128)(2,1)S(1)}, u32[]{:S(2)}, u32[]{:S(2)}) collective-permute-start(bf16[256,1536]{1,0:T(8,128)(2,1)S(1)} %add_convert_fusion.5), channel_id=1, source_target_pairs={{0,8},{8,16},{16,24},{24,0},{1,9},{9,17},{17,25},{25,1},{2,10},{10... | collective-permute-start | bytes 2359304 | tf_op jit(solution)/shard_map/ppermute | solution.py:64
  511.6 31.3 %collective-permute-start.74 = (bf16[256,1536]{1,0:T(8,128)(2,1)}, bf16[256,1536]{1,0:T(8,128)(2,1)}, u32[]{:S(2)}, u32[]{:S(2)}) collective-permute-start(bf16[256,1536]{1,0:T(8,128)(2,1)} %pad_maximum_fusion.8), channel_id=1, source_target_pairs={{0,4},{4,0},{1,5},{5,1},{2,6},{6,2},{3,7},{7,3},{8,12},{12,8},{9,1... | collective-permute-start | bytes 2359304 | tf_op jit(solution)/shard_map/ppermute | solution.py:60
  516.8 27.1 %collective-permute-start.76 = (bf16[256,1536]{1,0:T(8,128)(2,1)}, bf16[256,1536]{1,0:T(8,128)(2,1)}, u32[]{:S(2)}, u32[]{:S(2)}) collective-permute-start(bf16[256,1536]{1,0:T(8,128)(2,1)} %add_convert_fusion.4), channel_id=1, source_target_pairs={{0,8},{8,16},{16,24},{24,0},{1,9},{9,17},{17,25},{25,1},{2,10},{10... | collective-permute-start | bytes 2359304 | tf_op jit(solution)/shard_map/ppermute | solution.py:64
  555.2 32.9 %all-to-all-start.3 = ((bf16[8,64,1024]{2,1,0:T(8,128)(2,1)}), bf16[8,64,1024]{2,1,0:T(8,128)(2,1)S(1)}, u32[]{:S(2)}, u32[]{:S(2)}) async-start(bf16[8,64,1024]{2,1,0:T(8,128)(2,1)} %get-tuple-element.187), calls=%async_computation.3 | async-start | bytes 2097152 | tf_op jit(solution)/shard_map/all_to_all | solution.py:171
  (171 other events, 2217.5 us)

commit v5 on v4

--- a/solution.py
+++ b/solution.py
@@ -419,7 +419,7 @@
     head_sum = head_own[order[0]].astype(F32) + head_got[0]
     for step in range(1, size):
         head_sum = head_sum.astype(BF)
-        if step == size - 1:
+        if step == size - 2:
             head_sum, outputs = tie(head_sum, outputs)
         head_sum = head_own[order[step]].astype(F32) + head_got[step] + ring(head_sum, size)
     outputs = outputs.reshape(hidden_in.shape)

time: 600 us -> 600 us (level)
    ppermute x18, waiting for transfers between devices: 56.4 us -> 47.5 us  [ring(): return lax.ppermute(value, 'z', [(i, (i + 1) % size) for i in range(size)])]
  transfers between devices with their start and end apart: 99 -> 99, of which waited for: 40 -> 39; matrix products, arithmetic and copies ran while one was open for 40% -> 40% of each run, Pallas kernels for 0% -> 0%
where the time goes in v5:
time: 600 us; the launch traced here: 591 us
  waiting for transfers between devices  228 us (38%)
  local copies, waits for them, and re-layouts  109 us (18%)
  starting transfers between devices  91.4 us (15%)
  matrix products  90.6 us (15%)
  other arithmetic  68.4 us (11%)
    ppermute x70, waiting for transfers between devices, swap(): return lax.ppermute(value, axis, [(0, 1), (1, 0)])  132 us
    ppermute x18, waiting for transfers between devices, ring(): return lax.ppermute(value, 'z', [(i, (i + 1) % size) for i in range(size)])  47.5 us
    ppermute x70, starting transfers between devices, swap(): return lax.ppermute(value, axis, [(0, 1), (1, 0)])  45.3 us
    dot_general x6, matrix products, dot_rows(): lax.dot_general(left, right, (((0,), (0,)), ((), ())), preferred_element_...  34.3 us
    dynamic_update_slice x35, local copies, waits for them, and re-layouts, put(): return lax.dynamic_update_slice(buffer, piece, starts)  29.2 us
    all_to_all x5, waiting for transfers between devices, exchange(): return lax.all_to_all(parts, ('z', 'y'), 0, 0, tiled=True)  26.9 us
    dot_general x6, matrix products, dot_right(): lax.dot_general(left, right, (((1,), (1,)), ((), ())), preferred_element_...  26 us
    dot_general x6, matrix products, dot(): return jnp.dot(left, right, preferred_element_type=F32)  25.7 us
  transfers between devices with their start and end apart: 99, of which 39 were waited for; matrix products, arithmetic and copies ran while one was open for 40% of the time, Pallas kernels for 0%

profile of v5, /device:TPU:0, one launch (start us, length us, event | category | flops | bytes accessed | tf_op | source)
XLA Modules:
  0.0 591.1 jit_solution(8611839548332549007)
XLA Ops:
  34.5 9.3 %collective-permute-done.10 = bf16[2,64,2048]{2,1,0:T(8,128)(2,1)S(1)} collective-permute-done((bf16[2,64,2048]{2,1,0:T(8,128)(2,1)S(1)}, bf16[2,64,2048]{2,1,0:T(8,128)(2,1)S(1)}, u32[]{:S(2)}, u32[]{:S(2)}) %collective-permute-start.10) | collective-permute-done | bytes 524320 | tf_op jit(solution)/shard_map/ppermute | solution.py:60
  51.9 7.4 %collective-permute-done.16 = bf16[128,2048]{1,0:T(8,128)(2,1)} collective-permute-done((bf16[128,2048]{1,0:T(8,128)(2,1)}, bf16[128,2048]{1,0:T(8,128)(2,1)}, u32[]{:S(2)}, u32[]{:S(2)}) %collective-permute-start.16) | collective-permute-done | bytes 524320 | tf_op jit(solution)/shard_map/ppermute | solution.py:64
  85.3 7.0 %collective-permute-done.6 = bf16[264,1536]{1,0:T(8,128)(2,1)S(1)} collective-permute-done((bf16[264,1536]{1,0:T(8,128)(2,1)}, bf16[264,1536]{1,0:T(8,128)(2,1)S(1)}, u32[]{:S(2)}, u32[]{:S(2)}) %collective-permute-start.6) | collective-permute-done | bytes 811040 | tf_op jit(solution)/shard_map/ppermute | solution.py:64
  102.0 7.8 %collective-permute-done.14 = bf16[264,1536]{1,0:T(8,128)(2,1)S(1)} collective-permute-done((bf16[264,1536]{1,0:T(8,128)(2,1)S(1)}, bf16[264,1536]{1,0:T(8,128)(2,1)S(1)}, u32[]{:S(2)}, u32[]{:S(2)}) %collective-permute-start.14) | collective-permute-done | bytes 811040 | tf_op jit(solution)/shard_map/ppermute | solution.py:60
  152.1 13.5 %collective-permute-done.25 = bf16[2,64,2048]{2,1,0:T(8,128)(2,1)S(1)} collective-permute-done((bf16[2,64,2048]{2,1,0:T(8,128)(2,1)S(1)}, bf16[2,64,2048]{2,1,0:T(8,128)(2,1)S(1)}, u32[]{:S(2)}, u32[]{:S(2)}) %collective-permute-start.25) | collective-permute-done | bytes 524320 | tf_op jit(solution)/shard_map/ppermute | solution.py:60
  190.4 8.9 %all-to-all-done.1 = bf16[8,64,1024]{2,1,0:T(8,128)(2,1)S(1)} async-done(((bf16[8,64,1024]{2,1,0:T(8,128)(2,1)}), bf16[8,64,1024]{2,1,0:T(8,128)(2,1)S(1)}, u32[]{:S(2)}, u32[]{:S(2)}) %all-to-all-start.1) | async-done | bytes 1048608 | tf_op jit(solution)/shard_map/all_to_all | solution.py:171
  206.3 6.8 %collective-permute-done.26 = bf16[128,2048]{1,0:T(8,128)(2,1)S(1)} collective-permute-done((bf16[128,2048]{1,0:T(8,128)(2,1)S(1)}, bf16[128,2048]{1,0:T(8,128)(2,1)S(1)}, u32[]{:S(2)}, u32[]{:S(2)}) %collective-permute-start.26) | collective-permute-done | bytes 524320 | tf_op jit(solution)/shard_map/ppermute | solution.py:64
  215.4 11.5 %collective-permute-done.28 = bf16[8,64,2048]{2,1,0:T(8,128)(2,1)} collective-permute-done((bf16[8,64,2048]{2,1,0:T(8,128)(2,1)}, bf16[8,64,2048]{2,1,0:T(8,128)(2,1)}, u32[]{:S(2)}, u32[]{:S(2)}) %collective-permute-start.28) | collective-permute-done | bytes 2097184 | tf_op jit(solution)/shard_map/ppermute | solution.py:60
  240.2 12.4 %collective-permute-done.29 = bf16[128,2048]{1,0:T(8,128)(2,1)S(1)} collective-permute-done((bf16[128,2048]{1,0:T(8,128)(2,1)S(1)}, bf16[128,2048]{1,0:T(8,128)(2,1)S(1)}, u32[]{:S(2)}, u32[]{:S(2)}) %collective-permute-start.29) | collective-permute-done | bytes 524320 | tf_op jit(solution)/shard_map/ppermute | solution.py:64
  256.4 9.1 %fusion.116 = f32[768,2048]{1,0:T(8,128)S(1)} fusion(bf16[768,2048]{1,0:T(8,128)(2,1)S(1)} %constant_dynamic-update-slice_fusion, bf16[2048,2048]{1,0:T(8,128)(2,1)} %bitcast.95), kind=kOutput, calls=%fused_computation.441 | convolution fusion | flops 6442450944 | bytes 17825792 | tf_op jit(solution)/shard_map/dot_general | solution.py:48
  273.3 9.2 %convolution_convert_fusion.1 = bf16[768,2048]{1,0:T(8,128)(2,1)S(1)} fusion(bf16[2048,2048]{1,0:T(8,128)(2,1)} %bitcast.95, bf16[768,1024]{1,0:T(8,128)(2,1)S(1)} %get-tuple-element.252, bf16[768,1024]{1,0:T(8,128)(2,1)S(1)} %get-tuple-element.251), kind=kOutput, calls=%fused_computation.11 | convolution fusion | flops 6450315264 | bytes 14680064 | tf_op jit(solution)/shard_map/dot_general | solution.py:52
  307.6 5.9 %add_convert_fusion.1 = bf16[2048,1024]{1,0:T(8,128)(2,1)S(1)} fusion(f32[2048,1024]{1,0:T(8,128)S(1)} %fusion.118, bf16[768,2048]{1,0:T(8,128)(2,1)} %copy-done.77, bf16[768,1024]{1,0:T(8,128)(2,1)S(1)} %get-tuple-element.152), kind=kOutput, calls=%fused_computation.1 | convolution fusion | flops 3225419776 | bytes 17301504 | tf_op jit(solution)/shard_map/dot_general | solution.py:56
  325.0 10.5 %fusion.119 = f32[2048,2048]{1,0:T(8,128)} fusion(bf16[768,2048]{1,0:T(8,128)(2,1)S(1)} %copy-done.80, bf16[768,2048]{1,0:T(8,128)(2,1)S(1)} %copy-done.26), kind=kOutput, calls=%fused_computation.444 | convolution fusion | flops 6442450944 | bytes 23068672 | tf_op jit(solution)/shard_map/dot_general | solution.py:56
  337.6 11.6 %add_convert_fusion = bf16[2048,2048]{1,0:T(8,128)(2,1)} fusion(f32[2048,2048]{1,0:T(8,128)} %fusion.119, bf16[256,2048]{1,0:T(8,128)(2,1)S(1)} %pad_maximum_fusion.4, bf16[256,2048]{1,0:T(8,128)(2,1)S(1)} %pad_maximum_fusion.5), kind=kOutput, calls=%fused_computation | convolution fusion | flops 2155872256 | bytes 27262976 | tf_op jit(solution)/shard_map/dot_general | solution.py:56
  359.4 11.0 %collective-permute-done.61 = bf16[2,64,2048]{2,1,0:T(8,128)(2,1)S(1)} collective-permute-done((bf16[2,64,2048]{2,1,0:T(8,128)(2,1)S(1)}, bf16[2,64,2048]{2,1,0:T(8,128)(2,1)S(1)}, u32[]{:S(2)}, u32[]{:S(2)}) %collective-permute-start.61) | collective-permute-done | bytes 524320 | tf_op jit(solution)/shard_map/ppermute | solution.py:60
  420.8 10.5 %collective-permute-done.76 = bf16[128,2048]{1,0:T(8,128)(2,1)S(1)} collective-permute-done((bf16[128,2048]{1,0:T(8,128)(2,1)S(1)}, bf16[128,2048]{1,0:T(8,128)(2,1)S(1)}, u32[]{:S(2)}, u32[]{:S(2)}) %collective-permute-start.76) | collective-permute-done | bytes 524320 | tf_op jit(solution)/shard_map/ppermute | solution.py:60
  440.2 6.0 %collective-permute-done.86 = bf16[2,64,2048]{2,1,0:T(8,128)(2,1)S(1)} collective-permute-done((bf16[2,64,2048]{2,1,0:T(8,128)(2,1)S(1)}, bf16[2,64,2048]{2,1,0:T(8,128)(2,1)S(1)}, u32[]{:S(2)}, u32[]{:S(2)}) %collective-permute-start.86) | collective-permute-done | bytes 524320 | tf_op jit(solution)/shard_map/ppermute | solution.py:60
  447.6 8.5 %collective-permute-done.77 = bf16[128,2048]{1,0:T(8,128)(2,1)} collective-permute-done((bf16[128,2048]{1,0:T(8,128)(2,1)}, bf16[128,2048]{1,0:T(8,128)(2,1)}, u32[]{:S(2)}, u32[]{:S(2)}) %collective-permute-start.77) | collective-permute-done | bytes 524320 | tf_op jit(solution)/shard_map/ppermute | solution.py:60
  461.1 6.8 %collective-permute-done.71 = bf16[4,2,64,2048]{3,2,1,0:T(8,128)(2,1)} collective-permute-done((bf16[4,2,64,2048]{3,2,1,0:T(8,128)(2,1)}, bf16[4,2,64,2048]{3,2,1,0:T(8,128)(2,1)}, u32[]{:S(2)}, u32[]{:S(2)}) %collective-permute-start.71) | collective-permute-done | bytes 2097184 | tf_op jit(solution)/shard_map/ppermute | solution.py:60
  478.1 12.3 %collective-permute-done.72 = bf16[256,1536]{1,0:T(8,128)(2,1)} collective-permute-done((bf16[256,1536]{1,0:T(8,128)(2,1)}, bf16[256,1536]{1,0:T(8,128)(2,1)}, u32[]{:S(2)}, u32[]{:S(2)}) %collective-permute-start.72) | collective-permute-done | bytes 786464 | tf_op jit(solution)/shard_map/ppermute | solution.py:60
  500.8 10.8 %collective-permute-done.73 = bf16[256,1536]{1,0:T(8,128)(2,1)S(1)} collective-permute-done((bf16[256,1536]{1,0:T(8,128)(2,1)}, bf16[256,1536]{1,0:T(8,128)(2,1)S(1)}, u32[]{:S(2)}, u32[]{:S(2)}) %collective-permute-start.73) | collective-permute-done | bytes 786464 | tf_op jit(solution)/shard_map/ppermute | solution.py:60
  521.1 16.3 %all-to-all-done.2 = bf16[8,64,1024]{2,1,0:T(8,128)(2,1)} async-done(((bf16[8,64,1024]{2,1,0:T(8,128)(2,1)}), bf16[8,64,1024]{2,1,0:T(8,128)(2,1)}, u32[]{:S(2)}, u32[]{:S(2)}) %all-to-all-start.2) | async-done | bytes 1048608 | tf_op jit(solution)/shard_map/all_to_all | solution.py:171
  550.1 7.9 %collective-permute-done.88 = bf16[256,1536]{1,0:T(8,128)(2,1)} collective-permute-done((bf16[256,1536]{1,0:T(8,128)(2,1)}, bf16[256,1536]{1,0:T(8,128)(2,1)}, u32[]{:S(2)}, u32[]{:S(2)}) %collective-permute-start.88) | collective-permute-done | bytes 786464 | tf_op jit(solution)/shard_map/ppermute | solution.py:60
  568.7 15.6 %collective-permute-done.92 = bf16[64,1536]{1,0:T(8,128)(2,1)S(1)} collective-permute-done((bf16[64,1536]{1,0:T(8,128)(2,1)S(1)}, bf16[64,1536]{1,0:T(8,128)(2,1)S(1)}, u32[]{:S(2)}, u32[]{:S(2)}) %collective-permute-start.92) | collective-permute-done | bytes 196640 | tf_op jit(solution)/shard_map/ppermute | solution.py:105
  (634 shorter events, 351.3 us)
Async XLA Ops:
  24.7 37.2 %collective-permute-start.5 = (bf16[264,1536]{1,0:T(8,128)(2,1)}, bf16[264,1536]{1,0:T(8,128)(2,1)}, u32[]{:S(2)}, u32[]{:S(2)}) collective-permute-start(bf16[264,1536]{1,0:T(8,128)(2,1)} %fusion.54), channel_id=1, source_target_pairs={{0,4},{4,0},{1,5},{5,1},{2,6},{6,2},{3,7},{7,3},{8,12},{12,8},{9,1... | collective-permute-start | bytes 2433032 | tf_op jit(solution)/shard_map/ppermute | solution.py:60
  26.3 35.6 %collective-permute-start.4 = (bf16[264,1536]{1,0:T(8,128)(2,1)}, bf16[264,1536]{1,0:T(8,128)(2,1)}, u32[]{:S(2)}, u32[]{:S(2)}) collective-permute-start(bf16[264,1536]{1,0:T(8,128)(2,1)} %fusion.54), channel_id=1, source_target_pairs={{0,8},{8,16},{16,24},{24,0},{1,9},{9,17},{17,25},{25,1},{2,10},{10... | collective-permute-start | bytes 2433032 | tf_op jit(solution)/shard_map/ppermute | solution.py:64
  62.5 29.8 %collective-permute-start.6 = (bf16[264,1536]{1,0:T(8,128)(2,1)}, bf16[264,1536]{1,0:T(8,128)(2,1)S(1)}, u32[]{:S(2)}, u32[]{:S(2)}) collective-permute-start(bf16[264,1536]{1,0:T(8,128)(2,1)} %collective-permute-done.4), channel_id=1, source_target_pairs={{0,8},{8,16},{16,24},{24,0},{1,9},{9,17},{17,25},{25,1},{2,10},{10... | collective-permute-start | bytes 2433032 | tf_op jit(solution)/shard_map/ppermute | solution.py:64
  101.5 72.3 %collective-permute-start.52 = (bf16[128,2048]{1,0:T(8,128)(2,1)}, bf16[128,2048]{1,0:T(8,128)(2,1)}, u32[]{:S(2)}, u32[]{:S(2)}) collective-permute-start(bf16[128,2048]{1,0:T(8,128)(2,1)} %collective-permute-done.18), channel_id=1, source_target_pairs={{0,2},{2,0},{1,3},{3,1},{4,6},{6,4},{5,7},{7,5},{8,10},{10,8},{9,1... | collective-permute-start | bytes 1572872 | tf_op jit(solution)/shard_map/ppermute | solution.py:60
  118.5 49.5 %all-to-all-start = ((bf16[8,64,2048]{2,1,0:T(8,128)(2,1)}), bf16[8,64,2048]{2,1,0:T(8,128)(2,1)}, u32[]{:S(2)}, u32[]{:S(2)}) async-start(bf16[8,64,2048]{2,1,0:T(8,128)(2,1)} %copy.138), calls=%async_computation | async-start | bytes 4194304 | tf_op jit(solution)/shard_map/all_to_all | solution.py:171
  169.6 29.7 %all-to-all-start.1 = ((bf16[8,64,1024]{2,1,0:T(8,128)(2,1)}), bf16[8,64,1024]{2,1,0:T(8,128)(2,1)S(1)}, u32[]{:S(2)}, u32[]{:S(2)}) async-start(bf16[8,64,1024]{2,1,0:T(8,128)(2,1)} %copy.139), calls=%async_computation.1 | async-start | bytes 2097152 | tf_op jit(solution)/shard_map/all_to_all | solution.py:171
  179.1 47.9 %collective-permute-start.28 = (bf16[8,64,2048]{2,1,0:T(8,128)(2,1)}, bf16[8,64,2048]{2,1,0:T(8,128)(2,1)}, u32[]{:S(2)}, u32[]{:S(2)}) collective-permute-start(bf16[8,64,2048]{2,1,0:T(8,128)(2,1)} %all-to-all-done), channel_id=1, source_target_pairs={{0,4},{4,0},{1,5},{5,1},{2,6},{6,2},{3,7},{7,3},{8,12},{12,8},{9,1... | collective-permute-start | bytes 6291464 | tf_op jit(solution)/shard_map/ppermute | solution.py:60
  226.9 26.9 %collective-permute-start.33 = (bf16[128,2048]{1,0:T(8,128)(2,1)S(1)}, bf16[128,2048]{1,0:T(8,128)(2,1)S(1)}, u32[]{:S(2)}, u32[]{:S(2)}) collective-permute-start(bf16[128,2048]{1,0:T(8,128)(2,1)S(1)} %collective-permute-done.27), channel_id=1, source_target_pairs={{0,2},{2,0},{1,3},{3,1},{4,6},{6,4},{5,7},{7,5},{8,10},{10,8},{9,1... | collective-permute-start | bytes 1572872 | tf_op jit(solution)/shard_map/ppermute | solution.py:60
  238.0 27.6 %collective-permute-start.46 = (bf16[8,64,1024]{2,1,0:T(8,128)(2,1)S(1)}, bf16[8,64,1024]{2,1,0:T(8,128)(2,1)S(1)}, u32[]{:S(2)}, u32[]{:S(2)}) collective-permute-start(bf16[8,64,1024]{2,1,0:T(8,128)(2,1)S(1)} %all-to-all-done.1), channel_id=1, source_target_pairs={{0,4},{4,0},{1,5},{5,1},{2,6},{6,2},{3,7},{7,3},{8,12},{12,8},{9,1... | collective-permute-start | bytes 3145736 | tf_op jit(solution)/shard_map/ppermute | solution.py:60
  322.7 26.5 %collective-permute-start.63 = (bf16[2,2,2,64,1024]{4,3,2,1,0:T(8,128)(2,1)S(1)}, bf16[2,2,2,64,1024]{4,3,2,1,0:T(8,128)(2,1)}, u32[]{:S(2)}, u32[]{:S(2)}) collective-permute-start(bf16[2,2,2,64,1024]{4,3,2,1,0:T(8,128)(2,1)S(1)} %dynamic-slice_bitcast_fusion.5), channel_id=1, source_target_pairs={{0,1},{1,0},{2,3},{3,2},{4,5},{5,4},{6,7},{7,6},{8,9},{9,8},{10,11... | collective-permute-start | bytes 3145736 | tf_op jit(solution)/shard_map/ppermute | solution.py:60
  322.7 28.0 %collective-permute-start.62 = (bf16[2,2,2,64,1024]{4,3,2,1,0:T(8,128)(2,1)S(1)}, bf16[2,2,2,64,1024]{4,3,2,1,0:T(8,128)(2,1)}, u32[]{:S(2)}, u32[]{:S(2)}) collective-permute-start(bf16[2,2,2,64,1024]{4,3,2,1,0:T(8,128)(2,1)S(1)} %dynamic-slice_bitcast_fusion.6), channel_id=1, source_target_pairs={{0,1},{1,0},{2,3},{3,2},{4,5},{5,4},{6,7},{7,6},{8,9},{9,8},{10,11... | collective-permute-start | bytes 3145736 | tf_op jit(solution)/shard_map/ppermute | solution.py:60
  352.7 28.5 %collective-permute-start.64 = (bf16[4,2,64,1024]{3,2,1,0:T(8,128)(2,1)S(1)}, bf16[4,2,64,1024]{3,2,1,0:T(8,128)(2,1)S(1)}, u32[]{:S(2)}, u32[]{:S(2)}) collective-permute-start(bf16[4,2,64,1024]{3,2,1,0:T(8,128)(2,1)S(1)} %fusion.24), channel_id=1, source_target_pairs={{0,4},{4,0},{1,5},{5,1},{2,6},{6,2},{3,7},{7,3},{8,12},{12,8},{9,1... | collective-permute-start | bytes 3145736 | tf_op jit(solution)/shard_map/ppermute | solution.py:60
  359.2 23.5 %collective-permute-start.59 = (bf16[64,2048]{1,0:T(8,128)(2,1)S(1)}, bf16[64,2048]{1,0:T(8,128)(2,1)S(1)}, u32[]{:S(2)}, u32[]{:S(2)}) collective-permute-start(bf16[64,2048]{1,0:T(8,128)(2,1)S(1)} %get-tuple-element.341), channel_id=1, source_target_pairs={{0,1},{1,0},{2,3},{3,2},{4,5},{5,4},{6,7},{7,6},{8,9},{9,8},{10,11... | collective-permute-start | bytes 786440 | tf_op jit(solution)/shard_map/ppermute | solution.py:60
  377.0 36.7 %collective-permute-start.75 = (bf16[128,2048]{1,0:T(8,128)(2,1)}, bf16[128,2048]{1,0:T(8,128)(2,1)}, u32[]{:S(2)}, u32[]{:S(2)}) collective-permute-start(bf16[128,2048]{1,0:T(8,128)(2,1)} %get-tuple-element.269), channel_id=1, source_target_pairs={{0,2},{2,0},{1,3},{3,1},{4,6},{6,4},{5,7},{7,5},{8,10},{10,8},{9,1... | collective-permute-start | bytes 1572872 | tf_op jit(solution)/shard_map/ppermute | solution.py:60
  394.0 67.1 %all-to-all-start.4 = ((bf16[8,64,1024]{2,1,0:T(8,128)(2,1)}), bf16[8,64,1024]{2,1,0:T(8,128)(2,1)S(1)}, u32[]{:S(2)}, u32[]{:S(2)}) async-start(bf16[8,64,1024]{2,1,0:T(8,128)(2,1)} %bitcast.686), calls=%async_computation.4 | async-start | bytes 2097152 | tf_op jit(solution)/shard_map/all_to_all | solution.py:171
  409.7 28.2 %collective-permute-start.82 = (bf16[64,2048]{1,0:T(8,128)(2,1)S(1)}, bf16[64,2048]{1,0:T(8,128)(2,1)S(1)}, u32[]{:S(2)}, u32[]{:S(2)}) collective-permute-start(bf16[64,2048]{1,0:T(8,128)(2,1)S(1)} %get-tuple-element.285), channel_id=1, source_target_pairs={{0,1},{1,0},{2,3},{3,2},{4,5},{5,4},{6,7},{7,6},{8,9},{9,8},{10,11... | collective-permute-start | bytes 786440 | tf_op jit(solution)/shard_map/ppermute | solution.py:60
  419.6 48.4 %collective-permute-start.71 = (bf16[4,2,64,2048]{3,2,1,0:T(8,128)(2,1)}, bf16[4,2,64,2048]{3,2,1,0:T(8,128)(2,1)}, u32[]{:S(2)}, u32[]{:S(2)}) collective-permute-start(bf16[4,2,64,2048]{3,2,1,0:T(8,128)(2,1)} %dynamic-slice_bitcast_fusion), channel_id=1, source_target_pairs={{0,4},{4,0},{1,5},{5,1},{2,6},{6,2},{3,7},{7,3},{8,12},{12,8},{9,1... | collective-permute-start | bytes 6291464 | tf_op jit(solution)/shard_map/ppermute | solution.py:60
  434.7 23.6 %collective-permute-start.80 = (bf16[128,2048]{1,0:T(8,128)(2,1)}, bf16[128,2048]{1,0:T(8,128)(2,1)}, u32[]{:S(2)}, u32[]{:S(2)}) collective-permute-start(bf16[128,2048]{1,0:T(8,128)(2,1)} %fusion.31), channel_id=1, source_target_pairs={{0,8},{8,16},{16,24},{24,0},{1,9},{9,17},{17,25},{25,1},{2,10},{10... | collective-permute-start | bytes 1572872 | tf_op jit(solution)/shard_map/ppermute | solution.py:64
  456.1 41.8 %collective-permute-start.78 = (bf16[128,2048]{1,0:T(8,128)(2,1)}, bf16[128,2048]{1,0:T(8,128)(2,1)}, u32[]{:S(2)}, u32[]{:S(2)}) collective-permute-start(bf16[128,2048]{1,0:T(8,128)(2,1)} %get-tuple-element.176), channel_id=1, source_target_pairs={{0,2},{2,0},{1,3},{3,1},{4,6},{6,4},{5,7},{7,5},{8,10},{10,8},{9,1... | collective-permute-start | bytes 1572872 | tf_op jit(solution)/shard_map/ppermute | solution.py:60
  460.6 37.3 %collective-permute-start.81 = (bf16[128,2048]{1,0:T(8,128)(2,1)}, bf16[128,2048]{1,0:T(8,128)(2,1)}, u32[]{:S(2)}, u32[]{:S(2)}) collective-permute-start(bf16[128,2048]{1,0:T(8,128)(2,1)} %fusion.33), channel_id=1, source_target_pairs={{0,8},{8,16},{16,24},{24,0},{1,9},{9,17},{17,25},{25,1},{2,10},{10... | collective-permute-start | bytes 1572872 | tf_op jit(solution)/shard_map/ppermute | solution.py:64
  473.8 63.6 %all-to-all-start.2 = ((bf16[8,64,1024]{2,1,0:T(8,128)(2,1)}), bf16[8,64,1024]{2,1,0:T(8,128)(2,1)}, u32[]{:S(2)}, u32[]{:S(2)}) async-start(bf16[8,64,1024]{2,1,0:T(8,128)(2,1)} %get-tuple-element.275), calls=%async_computation.2 | async-start | bytes 2097152 | tf_op jit(solution)/shard_map/all_to_all | solution.py:171
  492.0 23.7 %collective-permute-start.74 = (bf16[256,1536]{1,0:T(8,128)(2,1)S(1)}, bf16[256,1536]{1,0:T(8,128)(2,1)S(1)}, u32[]{:S(2)}, u32[]{:S(2)}) collective-permute-start(bf16[256,1536]{1,0:T(8,128)(2,1)S(1)} %add_convert_fusion.5), channel_id=1, source_target_pairs={{0,8},{8,16},{16,24},{24,0},{1,9},{9,17},{17,25},{25,1},{2,10},{10... | collective-permute-start | bytes 2359304 | tf_op jit(solution)/shard_map/ppermute | solution.py:64
  516.9 27.1 %collective-permute-start.89 = (bf16[256,1536]{1,0:T(8,128)(2,1)}, bf16[256,1536]{1,0:T(8,128)(2,1)}, u32[]{:S(2)}, u32[]{:S(2)}) collective-permute-start(bf16[256,1536]{1,0:T(8,128)(2,1)} %add_convert_fusion.4), channel_id=1, source_target_pairs={{0,8},{8,16},{16,24},{24,0},{1,9},{9,17},{17,25},{25,1},{2,10},{10... | collective-permute-start | bytes 2359304 | tf_op jit(solution)/shard_map/ppermute | solution.py:64
  558.0 30.4 %all-to-all-start.3 = ((bf16[8,64,1024]{2,1,0:T(8,128)(2,1)}), bf16[8,64,1024]{2,1,0:T(8,128)(2,1)S(1)}, u32[]{:S(2)}, u32[]{:S(2)}) async-start(bf16[8,64,1024]{2,1,0:T(8,128)(2,1)} %get-tuple-element.187), calls=%async_computation.3 | async-start | bytes 2097152 | tf_op jit(solution)/shard_map/all_to_all | solution.py:171
  (171 other events, 2248.7 us)
